TPU v7x, 32 devices: a whole 2x2x4 slice. The times are simulated.
32 devices in a mesh: section: 2 (over core), expert: 8 (over z, y), dp: 2 (over x).
Axes of the slice: x: 2, y: 2, z: 4, core: 2. Of those that a mesh axis runs over, the one named last changes fastest.
Arguments:
- hidden_held: bfloat16 [2, 1024, 4096], P('section', 'expert'), may hold values from -6 to 6
- fresh_rows: bfloat16 [1, 1024, 4096], P(None, 'expert'), may hold values from -6 to 6
- doc_held: int32 [2, 1024], P('section', 'expert'), may hold values from 0 to 15, never falling along the last dimension, each value on 1 to 128 neighbouring positions
- doc_fresh: int32 [1, 1024], P(None, 'expert'), may hold values from 0 to 15, never falling along the last dimension, each value on 1 to 128 neighbouring positions
- routes: int32 [2, 2, 1024, 2], P(None, 'section', 'expert'), may hold values from 0 to 7, all different within a row; in each aligned block of 128 rows (0 to 127, 128 to 255, ..., all dimensions but the last counted through in order) at most 48 rows name the same one
- attn_gain: bfloat16 [2, 4096], P('section'), may hold values from 0.25 to 1.75
- query_gain: bfloat16 [2, 4096], P('section'), may hold values from -4 to 4
- key_gain: bfloat16 [2, 4096], P('section'), may hold values from -4 to 4
- ffn_gain: bfloat16 [2, 4096], P('section'), may hold values from 0.25 to 1.75
- router: bfloat16 [2, 4096, 8], P('section'), may hold values from -0.09375 to 0.09375
- weight_in: bfloat16 [2, 8, 4096, 2, 1536], P('section', 'expert', None, None, 'dp'), may hold values from -0.09375 to 0.09375
- weight_out: bfloat16 [2, 8, 1536, 4096], P('section', 'expert', 'dp'), may hold values from -0.15625 to 0.15625
Outputs:
- layer_out: bfloat16 [2, 2, 1024, 4096], P(None, 'section', 'expert')
Inputs may be any that keep to these rules, and one draw needn't show every extreme that they name: `doc_held`: ids never fall along a row; every document has at most 128 tokens, and one has exactly 128. `doc_fresh`: ids never fall along a row; every document has at most 128 tokens, and one has exactly 128. `routes`: the 2 experts of a token differ; among the 128 tokens of one device for one step and layer, no expert is chosen more than 48 times, a bound that some block reaches.
All inputs are finite; a program needn't handle non-finite values.
Results may differ from a plain program's by a relative error of at most 0.017.
Values may be sent and summed in bfloat16 or wider, within the bound.
No kernel may reach another device: no remote copies, remote signals or barrier semaphores. Data moves between devices by JAX's collectives and lax.ppermute only.
A program may use at most 128 MiB of HBM per device.

v0:
```python
import jax
import jax.numpy as jnp
from jax import lax
from jax.sharding import PartitionSpec as P

HEAD_DIM = 128


def shifted(array, axis, by):
    devices = lax.axis_size(axis)
    pairs = [(i, i + by) for i in range(devices) if 0 <= i + by < devices]
    return lax.ppermute(array, axis, pairs)


def rms_norm(rows, gain):
    wide = rows.astype(jnp.float32)
    return (
        wide
        * lax.rsqrt(jnp.mean(wide * wide, axis=-1, keepdims=True) + 1e-06)
        * gain.astype(jnp.float32)
    )


def attend(own_rows, prior_rows, own_ids, prior_ids, query_gain, key_gain):
    tok_rows = own_rows.shape[0]
    head_count = own_rows.shape[1] // HEAD_DIM
    source_rows = jnp.concatenate([prior_rows, own_rows], axis=0)
    queries = (own_rows.astype(jnp.float32) * query_gain.astype(jnp.float32)).astype(jnp.bfloat16)
    key_rows = (source_rows.astype(jnp.float32) * key_gain.astype(jnp.float32)).astype(jnp.bfloat16)
    queries = queries.reshape(tok_rows, head_count, HEAD_DIM)
    key_rows = key_rows.reshape(2 * tok_rows, head_count, HEAD_DIM)
    value_rows = source_rows.reshape(2 * tok_rows, head_count, HEAD_DIM)
    scores = jnp.einsum(
        "qhd,khd->hqk", queries, key_rows, preferred_element_type=jnp.float32
    ) * HEAD_DIM ** (-0.5)
    key_ids = jnp.concatenate([prior_ids, own_ids], axis=0)
    query_places = jnp.arange(tok_rows, dtype=jnp.int32)
    key_places = jnp.arange(2 * tok_rows, dtype=jnp.int32) - tok_rows
    allowed = (own_ids[:, None] == key_ids[None, :]) & (
        key_places[None, :] <= query_places[:, None]
    )
    scores = jnp.where(allowed[None], scores, -1e30)
    scores = scores - jnp.max(scores, axis=2, keepdims=True)
    raised = jnp.exp(scores)
    weights = (raised / jnp.sum(raised, axis=2, keepdims=True)).astype(jnp.bfloat16)
    mixed = jnp.einsum("hqk,khd->qhd", weights, value_rows, preferred_element_type=jnp.float32)
    return mixed.astype(jnp.bfloat16).reshape(tok_rows, head_count * HEAD_DIM)


def layer(
    current,
    documents,
    chosen,
    attn_gain,
    query_gain,
    key_gain,
    ffn_gain,
    router,
    weight_in,
    weight_out,
):
    tok_rows, model_width = current.shape
    top_count = chosen.shape[1]
    experts = router.shape[1]
    capacity = min(tok_rows, 3 * tok_rows * top_count // (2 * experts))
    normed = rms_norm(current, attn_gain).astype(jnp.bfloat16)
    own_ids = documents + 1
    dp_count = lax.axis_size("dp")
    share_width = model_width // dp_count
    col_start = lax.axis_index("dp") * share_width
    own_rows = lax.dynamic_slice_in_dim(normed, col_start, share_width, 1)
    query_part = lax.dynamic_slice_in_dim(query_gain, col_start, share_width, 0)
    key_part = lax.dynamic_slice_in_dim(key_gain, col_start, share_width, 0)
    prior_rows, prior_ids = shifted((own_rows, own_ids), "expert", 1)
    mixed_part = attend(own_rows, prior_rows, own_ids, prior_ids, query_part, key_part)
    mixed = lax.all_gather(mixed_part, "dp", axis=1, tiled=True)
    residual = current.astype(jnp.float32) + mixed.astype(jnp.float32)
    moe_in = rms_norm(residual, ffn_gain).astype(jnp.bfloat16)
    logits = jnp.dot(moe_in, router, preferred_element_type=jnp.float32)
    chances = jax.nn.softmax(logits, axis=-1)
    picked = jnp.take_along_axis(chances, chosen, axis=1)
    gate_weights = picked / jnp.sum(picked, axis=1, keepdims=True)
    labels = jnp.arange(experts, dtype=jnp.int32)
    member = jnp.sum((chosen[:, :, None] == labels).astype(jnp.int32), axis=1, dtype=jnp.int32)
    ranking = jnp.cumsum(member, axis=0, dtype=jnp.int32) - member
    slot_index = jnp.take_along_axis(ranking, chosen, axis=1)
    positions = chosen * capacity + slot_index
    buffer = jnp.zeros((experts * capacity, model_width), jnp.bfloat16)
    buffer = buffer.at[positions.reshape(-1)].set(jnp.repeat(moe_in, top_count, axis=0))
    grouped = buffer.reshape(experts, capacity, model_width)
    arrived = lax.all_to_all(grouped, "expert", split_axis=0, concat_axis=0, tiled=True)
    rows_in = arrived.reshape(experts * capacity, model_width)
    projected = jnp.dot(
        rows_in, weight_in.reshape(model_width, -1), preferred_element_type=jnp.float32
    )
    half_width = projected.shape[1] // 2
    inner_act = (jax.nn.silu(projected[:, :half_width]) * projected[:, half_width:]).astype(
        jnp.bfloat16
    )
    summed = lax.psum_scatter(
        jnp.dot(inner_act, weight_out, preferred_element_type=jnp.float32),
        "dp",
        scatter_dimension=0,
        tiled=True,
    )
    expert_rows = lax.all_gather(summed.astype(jnp.bfloat16), "dp", axis=0, tiled=True)
    returned = lax.all_to_all(
        expert_rows.reshape(experts, capacity, model_width),
        "expert",
        split_axis=0,
        concat_axis=0,
        tiled=True,
    )
    returned = returned.reshape(experts * capacity, model_width)
    picked_rows = returned[positions]
    combined = jnp.sum(gate_weights[:, :, None] * picked_rows.astype(jnp.float32), axis=1)
    return (residual + combined).astype(jnp.bfloat16)


def body(
    hidden_held,
    fresh_rows,
    doc_held,
    doc_fresh,
    routes,
    attn_gain,
    query_gain,
    key_gain,
    ffn_gain,
    router,
    weight_in,
    weight_out,
):
    tick_count = routes.shape[0]
    phase_first = lax.axis_index("section") == 0
    current = hidden_held[0]
    documents = doc_held[0]
    results = []
    for step_index in range(tick_count):
        made = layer(
            current,
            documents,
            routes[step_index, 0],
            attn_gain[0],
            query_gain[0],
            key_gain[0],
            ffn_gain[0],
            router[0],
            weight_in[0, 0],
            weight_out[0, 0],
        )
        results.append(made)
        if step_index + 1 < tick_count:
            passed, passed_ids = shifted((made, documents), "section", 1)
            current = jnp.where(phase_first, fresh_rows[step_index], passed)
            documents = jnp.where(phase_first, doc_fresh[step_index], passed_ids)
    return jnp.stack(results)[:, None]


def solution(mesh):
    in_specs = (
        P("section", "expert", None),
        P(None, "expert", None),
        P("section", "expert"),
        P(None, "expert"),
        P(None, "section", "expert", None),
        P("section", None),
        P("section", None),
        P("section", None),
        P("section", None),
        P("section", None, None),
        P("section", "expert", None, None, "dp"),
        P("section", "expert", "dp", None),
    )
    out_specs = P(None, "section", "expert", None)
    return jax.shard_map(body, mesh=mesh, in_specs=in_specs, out_specs=out_specs, check_vma=False)
```

profile of v0, /device:TPU:0, one launch (start us, length us, event | category | flops | bytes accessed | tf_op | source)
XLA Modules:
  0.0 768.5 jit_solution(3443020249734330939)
XLA Ops:
  9.8 4.9 collective-permute-start
  16.1 3.4 collective-permute-start.1
  20.9 3.4 collective-permute-start.5
  29.7 3.5 fusion.89
  33.3 2.2 convolution_convert_fusion.1
  37.2 1.9 gather_fusion.3
  39.5 20.6 %all-gather.5.cloned.1.call-done = bf16[128,4096]{1,0:T(8,128)(2,1)} async-done(((bf16[128,2048]{1,0:T(8,128)(2,1)}), bf16[128,4096]{1,0:T(8,128)(2,1)}) %all-gather.5.cloned.1.call-update) | async-done | bytes 1048592 | tf_op jit(solution)/shard_map/all_gather | solution.py:76
  60.1 1.7 multiply_reduce_fusion.4
  63.3 2.1 broadcast_in_dim.36
  65.4 2.2 reshape.366
  67.6 6.5 scatter_custom_fusion
  74.1 5.5 all-to-all-start
  79.6 11.0 %reduce-scatter.3.cloned.1.call-start = ((), (), s32[]{:S(2)}) async-start(), calls=%async_computation.7 | async-start | bytes 9437184 | tf_op jit(solution)/shard_map/reduce_scatter | solution.py:100
  90.7 13.1 %copy.80 = bf16[512,8,2,768]{3,1,2,0:T(8,128)(2,1)} copy(bf16[512,8,2,768]{3,2,1,0:T(2,128)(2,1)} %bitcast.134) | data formatting | bytes 25165824
  103.8 46.6 %all-to-all-done = bf16[8,48,4096]{2,1,0:T(8,128)(2,1)S(1)} async-done(((bf16[8,48,4096]{2,1,0:T(8,128)(2,1)}), bf16[8,48,4096]{2,1,0:T(8,128)(2,1)S(1)}, u32[]{:S(2)}, u32[]{:S(2)}) %all-to-all-start) | async-done | bytes 3145760 | tf_op jit(solution)/shard_map/all_to_all | solution.py:91
  150.3 8.0 %fusion.97 = f32[384,1536]{1,0:T(8,128)S(1)} fusion(bf16[384,4096]{1,0:T(8,128)(2,1)S(1)} %bitcast.141, bf16[4096,1536]{1,0:T(8,128)(2,1)} %bitcast.135), kind=kOutput, calls=%fused_computation.150 | convolution fusion | flops 4831838208 | bytes 18087936 | tf_op jit(solution)/shard_map/dot_general | solution.py:93
  158.4 7.4 fusion.4
  165.8 75.3 %reduce-scatter.3.cloned.1.call-done = f32[192,4096]{1,0:T(8,128)} async-done(((f32[384,4096]{1,0:T(8,128)}), f32[192,4096]{1,0:T(8,128)}) %reduce-scatter.3.cloned.1.call-update) | async-done | bytes 3145744 | tf_op jit(solution)/shard_map/reduce_scatter | solution.py:100
  241.1 3.2 convert_element_type.131
  244.4 45.1 %all-gather.7.cloned.1.call-done = bf16[384,4096]{1,0:T(8,128)(2,1)} async-done(((bf16[192,4096]{1,0:T(8,128)(2,1)}), bf16[384,4096]{1,0:T(8,128)(2,1)}) %all-gather.7.cloned.1.call-update) | async-done | bytes 3145744 | tf_op jit(solution)/shard_map/all_gather | solution.py:106
  289.4 5.5 all-to-all-start.1
  298.6 67.1 %all-to-all-done.1 = bf16[8,48,4096]{2,1,0:T(8,128)(2,1)S(1)} async-done(((bf16[8,48,4096]{2,1,0:T(8,128)(2,1)}), bf16[8,48,4096]{2,1,0:T(8,128)(2,1)S(1)}, u32[]{:S(2)}, u32[]{:S(2)}) %all-to-all-start.1) | async-done | bytes 3145760 | tf_op jit(solution)/shard_map/all_to_all | solution.py:107
  365.7 3.2 gather_fusion
  368.8 5.5 reshape.394
  374.3 8.9 %multiply_reduce_fusion.1 = f32[128,4096]{1,0:T(8,128)S(1)} fusion(f32[128,2,4096]{2,1,0:T(2,128)} %reshape.394, f32[128,2]{1,0:T(8,128)S(1)} %fusion.60), kind=kLoop, calls=%fused_computation.15 | loop fusion | flops 1572864 | bytes 6292480 | tf_op jit(solution)/shard_map/reduce_sum | solution.py:116
  384.9 2.2 collective-permute-done.2
  389.0 3.8 collective-permute-start.3
  393.8 10.2 %collective-permute-done.3 = bf16[128,2048]{1,0:T(8,128)(2,1)S(1)} collective-permute-done((bf16[128,2048]{1,0:T(8,128)(2,1)S(1)}, bf16[128,2048]{1,0:T(8,128)(2,1)S(1)}, u32[]{:S(2)}, u32[]{:S(2)}) %collective-permute-start.3) | collective-permute-done | bytes 524320 | tf_op jit(solution)/shard_map/ppermute | solution.py:12
  405.1 2.3 copy.61
  408.4 3.7 fusion.93
  412.0 2.9 convolution_convert_fusion
  414.9 2.0 copy.66
  417.7 1.9 gather_fusion.5
  420.0 19.1 %all-gather.9.cloned.1.call-done = bf16[128,4096]{1,0:T(8,128)(2,1)} async-done(((bf16[128,2048]{1,0:T(8,128)(2,1)}), bf16[128,4096]{1,0:T(8,128)(2,1)}) %all-gather.9.cloned.1.call-update) | async-done | bytes 1048592 | tf_op jit(solution)/shard_map/all_gather | solution.py:76
  442.2 2.1 broadcast_in_dim.39
  444.2 2.2 reshape.374
  446.4 5.5 scatter_custom_fusion.1
  452.0 76.4 %all_to_all.20 = bf16[8,48,4096]{2,1,0:T(8,128)(2,1)S(1)} all-to-all(bf16[8,48,4096]{2,1,0:T(8,128)(2,1)S(1)} %bitcast.137), channel_id=1, replica_groups=mesh['section'=2,'expert'=8,'dp'=2] {'expert'}, dimensions={0} | all-to-all | bytes 6291456 | tf_op jit(solution)/shard_map/all_to_all | solution.py:91
  528.4 8.2 %fusion.98 = f32[384,1536]{1,0:T(8,128)S(1)} fusion(bf16[384,4096]{1,0:T(8,128)(2,1)S(1)} %bitcast.142, bf16[4096,1536]{1,0:T(8,128)(2,1)} %bitcast.136), kind=kOutput, calls=%fused_computation.151 | convolution fusion | flops 4831838208 | bytes 18087936 | tf_op jit(solution)/shard_map/dot_general | solution.py:93
  536.6 4.6 fusion.2
  541.4 75.3 %reduce-scatter.5.cloned.1.call-done = f32[192,4096]{1,0:T(8,128)} async-done(((f32[384,4096]{1,0:T(8,128)}), f32[192,4096]{1,0:T(8,128)}) %reduce-scatter.5.cloned.1.call-update) | async-done | bytes 3145744 | tf_op jit(solution)/shard_map/reduce_scatter | solution.py:100
  616.6 3.2 convert_element_type.147
  619.9 45.1 %all-gather.11.cloned.1.call-done = bf16[384,4096]{1,0:T(8,128)(2,1)} async-done(((bf16[192,4096]{1,0:T(8,128)(2,1)}), bf16[384,4096]{1,0:T(8,128)(2,1)}) %all-gather.11.cloned.1.call-update) | async-done | bytes 3145744 | tf_op jit(solution)/shard_map/all_gather | solution.py:106
  664.9 5.5 all-to-all-start.3
  674.0 67.2 %all-to-all-done.3 = bf16[8,48,4096]{2,1,0:T(8,128)(2,1)S(1)} async-done(((bf16[8,48,4096]{2,1,0:T(8,128)(2,1)}), bf16[8,48,4096]{2,1,0:T(8,128)(2,1)S(1)}, u32[]{:S(2)}, u32[]{:S(2)}) %all-to-all-start.3) | async-done | bytes 3145760 | tf_op jit(solution)/shard_map/all_to_all | solution.py:107
  741.2 3.2 gather_fusion.1
  744.3 5.4 reshape.395
  749.8 8.9 %multiply_reduce_fusion = f32[128,4096]{1,0:T(8,128)S(1)} fusion(f32[128,2,4096]{2,1,0:T(2,128)} %reshape.395, f32[128,2]{1,0:T(8,128)S(1)} %fusion.62), kind=kLoop, calls=%fused_computation.14 | loop fusion | flops 1572864 | bytes 6292480 | tf_op jit(solution)/shard_map/reduce_sum | solution.py:116
  (145 shorter events, 35.3 us)
Async XLA Ops:
  6.5 288.6 %copy-start = (bf16[1,4096,8]{1,2,0:T(8,128)(2,1)S(1)}, bf16[1,4096,8]{1,2,0:T(8,128)(2,1)}, u32[]{:S(2)}) copy-start(bf16[1,4096,8]{1,2,0:T(8,128)(2,1)} %param.25) | copy-start | bytes 196612
  6.5 1.6 copy-start.3
  6.5 53.6 %all-gather.5.cloned.1.call-start = ((), (), s32[]{:S(2)}) async-start(), calls=%async_computation.6 | async-start | bytes 1572864 | tf_op jit(solution)/shard_map/all_gather | solution.py:76
  6.5 1.9 copy-start.16
  6.5 1.9 copy-start.18
  8.1 6.5 copy-start.22
  8.1 11.4 %copy-start.19 = (bf16[1,4096]{1,0:T(2,128)(2,1)S(1)}, bf16[1,4096]{1,0:T(2,128)(2,1)}, u32[]{:S(2)}) copy-start(bf16[1,4096]{1,0:T(2,128)(2,1)} %param.23) | copy-start | bytes 24580
  8.1 12.8 %copy-start.21 = (s32[1,128]{1,0:T(1,128)S(1)}, s32[1,128]{1,0:T(1,128)}, u32[]{:S(2)}) copy-start(s32[1,128]{1,0:T(1,128)} %param.19) | copy-start | bytes 1540
  9.8 16.5 %collective-permute-start = (bf16[128,2048]{1,0:T(8,128)(2,1)}, bf16[128,2048]{1,0:T(8,128)(2,1)S(1)}, u32[]{:S(2)}, u32[]{:S(2)}) collective-permute-start(bf16[128,2048]{1,0:T(8,128)(2,1)} %get-tuple-element.16), channel_id=1, source_target_pairs={{0,2},{2,4},{4,6},{6,8},{8,10},{10,12},{12,14},{1,3},{3,5},{5,7},{... | collective-permute-start | bytes 1572872 | tf_op jit(solution)/shard_map/ppermute | solution.py:12
  14.7 6.3 collective-permute-start.4
  16.1 10.0 %collective-permute-start.1 = (s32[128]{0:T(128)S(1)}, s32[128]{0:T(128)S(1)}, u32[]{:S(2)}, u32[]{:S(2)}) collective-permute-start(s32[128]{0:T(128)S(1)} %broadcast_add_fusion), channel_id=1, source_target_pairs={{0,2},{2,4},{4,6},{6,8},{8,10},{10,12},{12,14},{1,3},{3,5},{5,7},{... | collective-permute-start | bytes 1544 | tf_op jit(solution)/shard_map/ppermute | solution.py:12
  20.9 5.2 collective-permute-start.5
  29.7 3.5 copy-start.15
  33.3 3.2 copy-start.17
  33.3 3.2 copy-start.20
  60.1 1.7 copy-start.6
  62.3 1.0 copy-start.8
  74.1 76.2 %all-to-all-start = ((bf16[8,48,4096]{2,1,0:T(8,128)(2,1)}), bf16[8,48,4096]{2,1,0:T(8,128)(2,1)S(1)}, u32[]{:S(2)}, u32[]{:S(2)}) async-start(bf16[8,48,4096]{2,1,0:T(8,128)(2,1)} %bitcast.17), calls=%async_computation | async-start | bytes 6291456 | tf_op jit(solution)/shard_map/all_to_all | solution.py:91
  79.6 161.5 %reduce-scatter.3.cloned.1.call-start = ((), (), s32[]{:S(2)}) async-start(), calls=%async_computation.7 | async-start | bytes 9437184 | tf_op jit(solution)/shard_map/reduce_scatter | solution.py:100
  165.8 123.7 %all-gather.7.cloned.1.call-start = ((), (), s32[]{:S(2)}) async-start(), calls=%async_computation.8 | async-start | bytes 4718592 | tf_op jit(solution)/shard_map/all_gather | solution.py:106
  289.4 76.2 %all-to-all-start.1 = ((bf16[8,48,4096]{2,1,0:T(8,128)(2,1)}), bf16[8,48,4096]{2,1,0:T(8,128)(2,1)S(1)}, u32[]{:S(2)}, u32[]{:S(2)}) async-start(bf16[8,48,4096]{2,1,0:T(8,128)(2,1)} %bitcast.139), calls=%async_computation.2 | async-start | bytes 6291456 | tf_op jit(solution)/shard_map/all_to_all | solution.py:107
  294.9 144.1 %all-gather.9.cloned.1.call-start = ((), (), s32[]{:S(2)}) async-start(), calls=%async_computation.9 | async-start | bytes 1572864 | tf_op jit(solution)/shard_map/all_gather | solution.py:76
  374.3 8.9 %copy-start.4 = (bf16[1,128,4096]{2,1,0:T(8,128)(2,1)S(1)}, bf16[1,128,4096]{2,1,0:T(8,128)(2,1)}, u32[]{:S(2)}) copy-start(bf16[1,128,4096]{2,1,0:T(8,128)(2,1)} %param.16) | copy-start | bytes 3145732
  374.3 8.9 %copy-start.7 = (bf16[128,4096]{1,0:T(8,128)(2,1)S(1)}, bf16[128,4096]{1,0:T(8,128)(2,1)}, u32[]{:S(2)}) copy-start(bf16[128,4096]{1,0:T(8,128)(2,1)} %all-gather.5.cloned.1.call-done) | copy-start | bytes 3145732
  383.2 4.0 copy-start.13
  383.6 4.0 copy-start.11
  383.6 3.6 collective-permute-start.2
  387.6 53.1 %copy-start.1 = (f32[128,4096]{1,0:T(8,128)}, f32[128,4096]{1,0:T(8,128)S(1)}, u32[]{:S(2)}) copy-start(f32[128,4096]{1,0:T(8,128)S(1)} %get-tuple-element.12) | copy-start | bytes 6291460
  389.0 15.1 %collective-permute-start.3 = (bf16[128,2048]{1,0:T(8,128)(2,1)S(1)}, bf16[128,2048]{1,0:T(8,128)(2,1)S(1)}, u32[]{:S(2)}, u32[]{:S(2)}) collective-permute-start(bf16[128,2048]{1,0:T(8,128)(2,1)S(1)} %get-tuple-element.10), channel_id=1, source_target_pairs={{0,2},{2,4},{4,6},{6,8},{8,10},{10,12},{12,14},{1,3},{3,5},{5,7},{... | collective-permute-start | bytes 1572872 | tf_op jit(solution)/shard_map/ppermute | solution.py:12
  408.4 3.7 copy-start.14
  417.0 199.6 %reduce-scatter.5.cloned.1.call-start = ((), (), s32[]{:S(2)}) async-start(), calls=%async_computation.10 | async-start | bytes 9437184 | tf_op jit(solution)/shard_map/reduce_scatter | solution.py:100
  439.1 1.7 copy-start.9
  441.2 1.0 copy-start.5
  451.9 84.7 %slice-start = ((s8[6291456]{0:T(1024)(128)(4,1)}), s8[4194304]{0:T(1024)(128)(4,1)S(1)}, s32[]{:S(2)}) async-start(s8[6291456]{0:T(1024)(128)(4,1)} %bitcast.162), calls=%async_computation.12 | async-start | bytes 8388608
  528.4 8.2 %slice-start.1 = ((s8[6291456]{0:T(1024)(128)(4,1)}), s8[2097152]{0:T(1024)(128)(4,1)S(1)}, s32[]{:S(2)}) async-start(s8[6291456]{0:T(1024)(128)(4,1)} %bitcast.162), calls=%async_computation.13 | async-start | bytes 4194304
  541.3 123.6 %all-gather.11.cloned.1.call-start = ((), (), s32[]{:S(2)}) async-start(), calls=%async_computation.11 | async-start | bytes 4718592 | tf_op jit(solution)/shard_map/all_gather | solution.py:106
  664.9 76.2 %all-to-all-start.3 = ((bf16[8,48,4096]{2,1,0:T(8,128)(2,1)}), bf16[8,48,4096]{2,1,0:T(8,128)(2,1)S(1)}, u32[]{:S(2)}, u32[]{:S(2)}) async-start(bf16[8,48,4096]{2,1,0:T(8,128)(2,1)} %bitcast.140), calls=%async_computation.5 | async-start | bytes 6291456 | tf_op jit(solution)/shard_map/all_to_all | solution.py:107
  749.8 8.9 %copy-start.2 = (f32[128,4096]{1,0:T(8,128)S(1)}, f32[128,4096]{1,0:T(8,128)}, u32[]{:S(2)}) copy-start(f32[128,4096]{1,0:T(8,128)} %copy-done.1) | copy-start | bytes 6291460
  749.8 8.9 %copy-start.10 = (bf16[128,4096]{1,0:T(8,128)(2,1)S(1)}, bf16[128,4096]{1,0:T(8,128)(2,1)}, u32[]{:S(2)}) copy-start(bf16[128,4096]{1,0:T(8,128)(2,1)} %all-gather.9.cloned.1.call-done) | copy-start | bytes 3145732
  758.7 1.2 copy-start.12
Sparse Core Ops, SparseCore 0:
  36.6 23.4 all-gather.4
  165.9 75.1 reduce-scatter.2
  244.5 44.9 all-gather.6
  417.1 21.8 all-gather.8
  541.4 75.1 reduce-scatter.4
  620.0 44.9 all-gather.10
where the time goes:
time: 778 us; the launch traced here: 768 us
  waiting for transfers between devices  475 us (61%)
  blocking collectives  76.4 us (10%)
  local copies, waits for them, and re-layouts  73.5 us (9%)
  starting transfers between devices  46.1 us (6%)
  matrix products  43.7 us (6%)
  other arithmetic  38.8 us (5%)
  between operations  14.4 us (2%)
    reduce_scatter x2, waiting for transfers between devices, layer(): lax.psum_scatter(jnp.dot(inner_act, weight_out, preferred_element_type=jn...  151 us
    all_to_all x2, waiting for transfers between devices, layer(): lax.all_to_all(expert_rows.reshape(experts, capacity, model_width), 'expe...  134 us
    all_gather x2, waiting for transfers between devices, layer(): lax.all_gather(summed.astype(jnp.bfloat16), 'dp', axis=0, tiled=True)  90.2 us
    all_to_all x1, blocking collectives, layer(): lax.all_to_all(grouped, 'expert', split_axis=0, concat_axis=0, tiled=True)  76.4 us
    all_to_all x1, waiting for transfers between devices, layer(): lax.all_to_all(grouped, 'expert', split_axis=0, concat_axis=0, tiled=True)  46.6 us
    all_gather x2, waiting for transfers between devices, layer(): mixed = lax.all_gather(mixed_part, 'dp', axis=1, tiled=True)  39.7 us
    ppermute x6, starting transfers between devices, shifted(): return lax.ppermute(array, axis, pairs)  18.3 us
    reduce_sum x2, other arithmetic, layer(): jnp.sum(gate_weights[:, :, None] * picked_rows.astype(jnp.float32), axis=1)  17.8 us
  transfers between devices with their start and end apart: 15, of which 12 were waited for; matrix products, arithmetic and copies ran while one was open for 4% of the time, Pallas kernels for 0%

commit v1 on v0

v1 whole, which is shorter than its diff:
```python
import functools

import jax
import jax.numpy as jnp
from jax import lax
from jax.experimental import pallas as pl
from jax.experimental.pallas import tpu as pltpu
from jax.sharding import PartitionSpec as P

HEAD_DIM = 128
LANES = 128
EPS = 1e-06
F32 = jnp.float32
BF16 = jnp.bfloat16
MIB = 1024 * 1024


def params(mib):
    return pltpu.CompilerParams(vmem_limit_bytes=mib * MIB)


def cost():
    return pl.CostEstimate(flops=1, bytes_accessed=1, transcendentals=0)


def vmem():
    return pl.BlockSpec(memory_space=pltpu.VMEM)


def smem():
    return pl.BlockSpec(memory_space=pltpu.SMEM)


def to_next_block(array, sections):
    count = lax.axis_size("expert")
    pairs = [(s * count + i, s * count + i + 1) for s in sections for i in range(count - 1)]
    return lax.ppermute(array, ("section", "expert"), pairs)


def to_next_phase(array, step, swap):
    count, planes = lax.axis_size("expert"), lax.axis_size("dp")
    pairs = []
    for e in range(count - step):
        for d in range(planes):
            target = (count + e + step) * planes + (planes - 1 - d if swap else d)
            pairs.append((e * planes + d, target))
    return lax.ppermute(array, ("section", "expert", "dp"), pairs)


def to_other_plane(array, sections):
    pairs = [(2 * s + d, 2 * s + 1 - d) for s in sections for d in (0, 1)]
    return lax.ppermute(array, ("section", "dp"), pairs)


def across(array, distance, sections):
    if distance == 0:
        return array
    count = lax.axis_size("expert")
    pairs = [(s * count + e, s * count + (e ^ distance)) for s in sections for e in range(count)]
    return lax.ppermute(array, ("section", "expert"), pairs)


def eye(size):
    return lax.broadcasted_iota(jnp.int32, (size, size), 0) == lax.broadcasted_iota(
        jnp.int32, (size, size), 1
    )


def as_column(row, diagonal):
    return jnp.sum(jnp.where(diagonal, row, 0.0), axis=1, keepdims=True)


def as_row(column, diagonal):
    return jnp.sum(jnp.where(diagonal, column, 0.0), axis=0, keepdims=True)


def dot(a, b, contract=((1,), (0,))):
    return lax.dot_general(a, b, (contract, ((), ())), preferred_element_type=F32)


def attend_kernel(merged, width, expert_count, scalar_ref, own_ref, prior_ref, *refs):
    meta_ref, prior_meta_ref, *refs = refs
    ids, scale = meta_ref[0:1, :], meta_ref[1:2, :]
    prior_ids, prior_scale = prior_meta_ref[0:1, :], prior_meta_ref[1:2, :]
    if merged:
        sent_ref, sent_prior_ref, ids_ref, prior_ids_ref, *refs = refs
        squares_ref, squares_other_ref, *refs = refs
        prior_squares_ref, prior_squares_other_ref, *refs = refs
        first = scalar_ref[1] == 0
        ids = jnp.where(first, ids, ids_ref[...])
        prior_ids = jnp.where(first, prior_ids, prior_ids_ref[...])
        passed = lax.rsqrt((squares_ref[...] + squares_other_ref[...]) / width + EPS)
        prior_passed = lax.rsqrt(
            (prior_squares_ref[...] + prior_squares_other_ref[...]) / width + EPS
        )
        scale = jnp.where(first, scale, passed)
        prior_scale = jnp.where(first, prior_scale, prior_passed)
    gain_ref, query_ref, key_ref, ffn_ref, router_ref, place_ref = refs[:6]
    residual_ref, stats_ref, *block_refs = refs[6:]
    rows, features = own_ref.shape
    diagonal = eye(rows)
    own_scale, prior_scale = as_column(scale, diagonal), as_column(prior_scale, diagonal)
    own_ids = as_column(ids, diagonal)
    causal = lax.broadcasted_iota(jnp.int32, (rows, rows), 1) <= lax.broadcasted_iota(
        jnp.int32, (rows, rows), 0
    )
    bias_own = jnp.where((own_ids == ids) & causal, 0.0, -1e30)
    bias_prior = jnp.where(own_ids == prior_ids, 0.0, -1e30)
    factor = HEAD_DIM ** (-0.5)
    squares = jnp.zeros((rows, HEAD_DIM), F32)
    scaled, sent_rows = [], []
    all_heads = features // HEAD_DIM
    batch = min(8, all_heads)
    for base in range(0, all_heads, batch):
        heads = [slice(h * HEAD_DIM, (h + 1) * HEAD_DIM) for h in range(base, base + batch)]
        owns, normeds, prior_normeds, scores = [], [], [], []
        for at in heads:
            gain = gain_ref[:, at].astype(F32)
            query_gain, key_gain = query_ref[:, at].astype(F32), key_ref[:, at].astype(F32)
            own, prior = own_ref[:, at], prior_ref[:, at]
            if merged:
                own = jnp.where(first, own, sent_ref[:, at])
                prior = jnp.where(first, prior, sent_prior_ref[:, at])
            own = own.astype(F32)
            normed = (own * own_scale * gain).astype(BF16)
            prior_normed = (prior.astype(F32) * prior_scale * gain).astype(BF16)
            queries = (normed.astype(F32) * query_gain).astype(BF16)
            keys = (normed.astype(F32) * key_gain).astype(BF16)
            prior_keys = (prior_normed.astype(F32) * key_gain).astype(BF16)
            owns.append(own)
            normeds.append(normed)
            prior_normeds.append(prior_normed)
            scores.append(
                (dot(queries, keys, ((1,), (1,))), dot(queries, prior_keys, ((1,), (1,))))
            )
        weights = []
        for score, prior_score in scores:
            score = score * factor + bias_own
            prior_score = prior_score * factor + bias_prior
            top = jnp.max(jnp.maximum(score, prior_score), axis=1, keepdims=True)
            raised, prior_raised = jnp.exp(score - top), jnp.exp(prior_score - top)
            inverse = 1.0 / jnp.sum(raised + prior_raised, axis=1, keepdims=True)
            weights.append(
                ((raised * inverse).astype(BF16), (prior_raised * inverse).astype(BF16))
            )
        for index, at in enumerate(heads):
            weight, prior_weight = weights[index]
            mixed = dot(weight, normeds[index]) + dot(prior_weight, prior_normeds[index])
            residual = owns[index] + mixed.astype(BF16).astype(F32)
            residual_ref[:, at] = residual
            squares = squares + residual * residual
            scaled.append((residual * ffn_ref[:, at].astype(F32)).astype(BF16))
            sent_rows.append(residual.astype(BF16))
    sent = dot(place_ref[...], jnp.concatenate(sent_rows, axis=1)).astype(BF16)
    start = 0
    for block_ref in block_refs:
        block_ref[...] = sent[start : start + block_ref.shape[0]]
        start += block_ref.shape[0]
    squares = jnp.sum(squares, axis=1, keepdims=True)
    logits = dot(jnp.concatenate(scaled, axis=1), router_ref[...], ((1,), (1,)))
    lane = lax.broadcasted_iota(jnp.int32, (rows, LANES), 1)
    stats_ref[...] = jnp.where(lane == expert_count, squares, logits)


def attend(merged, width, expert_count, plane, operands, gains, router, place):
    rows, features = operands[0].shape
    capacity = place.shape[0] // expert_count
    whole = lambda shape: pl.BlockSpec(shape, lambda step, plane_ref: (0, 0))
    side = lambda step, plane_ref: (0, plane_ref[0])
    in_specs = [whole(array.shape) for array in operands]
    in_specs += [pl.BlockSpec((1, features), side)] * len(gains)
    in_specs += [pl.BlockSpec((LANES, features), side), whole(place.shape)]
    shapes = [((rows, features), F32), ((rows, LANES), F32)]
    shapes += [((capacity, features), BF16)] * expert_count
    residual, stats, *blocks = pl.pallas_call(
        functools.partial(attend_kernel, merged, width, expert_count),
        out_shape=[jax.ShapeDtypeStruct(*shape) for shape in shapes],
        grid_spec=pltpu.PrefetchScalarGridSpec(
            num_scalar_prefetch=1,
            grid=(1,),
            in_specs=in_specs,
            out_specs=[whole(shape) for shape, _ in shapes],
        ),
        compiler_params=params(16),
        cost_estimate=cost(),
        name="attend",
    )(plane, *operands, *gains, router, place)
    return residual, stats, blocks


def expert_kernel(blocks, width, scalar_ref, *refs):
    own_refs, far_refs, refs = refs[:blocks], refs[blocks : 2 * blocks], refs[2 * blocks :]
    up_ref, down_ref, gain_ref, *refs = refs
    away_refs, kept_refs = refs[:blocks], refs[blocks : 2 * blocks]
    rows_ref, sum_ref, inner_ref, up_held, down_held, up_sems, down_sems = refs[2 * blocks :]
    slots, half = rows_ref.shape[1:]
    hidden = down_ref.shape[0]
    plane = scalar_ref[0]
    sides = (plane * half, (1 - plane) * half)
    depth = up_held.shape[1]
    parts = half // depth
    down_depth = down_held.shape[1]

    copies = []
    for index in range(2 * parts):
        first = pl.multiple_of(sides[index // parts] + index % parts * depth, depth)
        copies.append(
            pltpu.make_async_copy(
                up_ref.at[pl.ds(first, depth)], up_held.at[index], up_sems.at[index]
            )
        )
    down_copies = [
        pltpu.make_async_copy(
            down_ref.at[pl.ds(index * down_depth, down_depth)],
            down_held.at[index],
            down_sems.at[index],
        )
        for index in range(hidden // down_depth)
    ]
    for copy in copies + down_copies:
        copy.start()

    scales = []
    start = 0
    for own_ref, far_ref in zip(own_refs, far_refs):
        at = slice(start, start + own_ref.shape[0])
        start += own_ref.shape[0]
        squares = 0.0
        for which, source_ref in enumerate((own_ref, far_ref)):
            lanes = pl.ds(pl.multiple_of(sides[which], half), half)
            rows = source_ref[...].astype(F32)
            squares = squares + jnp.sum(rows * rows, axis=1, keepdims=True)
            rows_ref[which, at, :] = (rows * gain_ref[:, lanes].astype(F32)).astype(BF16)
        scales.append(lax.rsqrt(squares / width + EPS))
    scale = jnp.concatenate(scales, axis=0)

    columns = min(512, hidden)
    for index, copy in enumerate(copies):
        copy.wait()
        lanes = slice(index % parts * depth, (index % parts + 1) * depth)

        @pl.loop(0, 2 * hidden // columns)
        def _(step, index=index, lanes=lanes):
            at = pl.ds(pl.multiple_of(step * columns, columns), columns)
            made = dot(rows_ref[index // parts, :, lanes], up_held[index, :, at])
            sum_ref[:, at] = made if index == 0 else sum_ref[:, at] + made

    gate = sum_ref[:, :hidden] * scale
    value = sum_ref[:, hidden:] * scale
    inner_ref[...] = (gate / (1.0 + jnp.exp(-gate)) * value).astype(BF16)
    for copy in down_copies:
        copy.wait()
    columns = min(512, half)
    for target_refs, side in ((away_refs, sides[1]), (kept_refs, sides[0])):

        @pl.loop(0, half // columns)
        def _(step, target_refs=target_refs, side=side):
            first = pl.multiple_of(step * columns, columns)
            at = pl.ds(pl.multiple_of(side + first, columns), columns)
            made = 0.0
            for index in range(hidden // down_depth):
                inner = inner_ref[:, index * down_depth : (index + 1) * down_depth]
                made = made + dot(inner, down_held[index, :, at])
            start = 0
            for ref in target_refs:
                piece = made[start : start + ref.shape[0]]
                ref[:, pl.ds(first, columns)] = piece.astype(ref.dtype)
                start += ref.shape[0]


def expert_rows(scalars, own, far, up, down, gain):
    blocks = len(own)
    slots = sum(array.shape[0] for array in own)
    half = own[0].shape[1]
    hidden, width = down.shape
    depth, down_depth = min(1024, half), min(256, hidden)
    anywhere = pl.BlockSpec(memory_space=pl.ANY)
    outs = pl.pallas_call(
        functools.partial(expert_kernel, blocks, width),
        out_shape=[jax.ShapeDtypeStruct(array.shape, BF16) for array in (*own, *own)],
        in_specs=[smem()] + [vmem()] * (2 * blocks) + [anywhere, anywhere, vmem()],
        out_specs=[vmem()] * (2 * blocks),
        scratch_shapes=[
            pltpu.VMEM((2, slots, half), BF16),
            pltpu.VMEM((slots, 2 * hidden), F32),
            pltpu.VMEM((slots, hidden), BF16),
            pltpu.VMEM((width // depth, depth, 2 * hidden), BF16),
            pltpu.VMEM((hidden // down_depth, down_depth, width), BF16),
            pltpu.SemaphoreType.DMA((width // depth,)),
            pltpu.SemaphoreType.DMA((hidden // down_depth,)),
        ],
        compiler_params=params(32),
        cost_estimate=cost(),
        name="expert_rows",
    )(scalars, *own, *far, up, down, gain)
    return list(outs[:blocks]), list(outs[blocks:])


def combine_kernel(expert_count, width, *refs):
    *rows_refs, residual_ref, stats_ref, stats_other_ref, place_ref, made_ref, squares_ref = refs
    tokens, slots = place_ref.shape
    capacity = slots // expert_count
    stats = stats_ref[...] + stats_other_ref[...]
    lane = lax.broadcasted_iota(jnp.int32, (tokens, LANES), 1)
    total = jnp.sum(jnp.where(lane == expert_count, stats, 0.0), axis=1, keepdims=True)
    logits = stats * lax.rsqrt(total / width + EPS)
    expert = lax.broadcasted_iota(jnp.int32, (LANES, slots), 0)
    slot = lax.broadcasted_iota(jnp.int32, (LANES, slots), 1)
    spread = jnp.where(
        (slot >= expert * capacity) & (slot < (expert + 1) * capacity), 1.0, 0.0
    ).astype(BF16)
    place = place_ref[...]
    member = dot(place, spread, ((1,), (1,))) > 0.5
    logits = jnp.where(member, logits, -1e30)
    raised = jnp.exp(logits - jnp.max(logits, axis=1, keepdims=True))
    gates = raised / jnp.sum(raised, axis=1, keepdims=True)
    high = gates.astype(BF16)
    low = (gates - high.astype(F32)).astype(BF16)
    place = place.astype(F32)
    rows = jnp.concatenate([ref[...] for ref in rows_refs], axis=0)
    made = dot((dot(high, spread) * place).astype(BF16), rows)
    made = made + dot((dot(low, spread) * place).astype(BF16), rows)
    made = (residual_ref[...] + made).astype(BF16)
    made_ref[...] = made
    wide = made.astype(F32)
    squares_ref[...] = as_row(jnp.sum(wide * wide, axis=1, keepdims=True), eye(tokens))


def combine(expert_count, width, returned, residual, stats, stats_other, place):
    tokens, features = residual.shape
    return pl.pallas_call(
        functools.partial(combine_kernel, expert_count, width),
        out_shape=(
            jax.ShapeDtypeStruct((tokens, features), BF16),
            jax.ShapeDtypeStruct((1, tokens), F32),
        ),
        in_specs=[vmem()] * (len(returned) + 4),
        out_specs=(vmem(), vmem()),
        compiler_params=params(16),
        cost_estimate=cost(),
        name="combine",
    )(*returned, residual, stats, stats_other, place)


def body(
    hidden_held,
    fresh_rows,
    doc_held,
    doc_fresh,
    routes,
    attn_gain,
    query_gain,
    key_gain,
    ffn_gain,
    router,
    weight_in,
    weight_out,
):
    ticks = routes.shape[0]
    assert ticks == 2 and lax.axis_size("section") == 2 and lax.axis_size("dp") == 2
    tokens, width = hidden_held.shape[1:]
    top_count = routes.shape[3]
    count = router.shape[2]
    assert count == lax.axis_size("expert")
    capacity = min(tokens, 3 * tokens * top_count // (2 * count))
    capacity = -(-capacity // 16) * 16
    section = lax.axis_index("section").astype(jnp.int32)
    plane = lax.axis_index("dp").astype(jnp.int32)
    here = lax.axis_index("expert").astype(jnp.int32)
    half = width // 2
    scalars = jnp.stack([plane, section])
    both = (0, 1)

    def half_of(rows):
        return lax.dynamic_slice_in_dim(rows, plane * half, half, 1)

    def meta_of(rows, ids):
        wide = rows.astype(F32)
        scale = lax.rsqrt(jnp.mean(wide * wide, axis=1) + EPS)
        return jnp.stack([(ids + 1).astype(F32), scale])

    held = half_of(hidden_held[0])
    held_prior = to_next_block(held, both)
    held_meta = meta_of(hidden_held[0], doc_held[0])
    held_prior_meta = to_next_block(held_meta, both)

    labels = jnp.arange(count, dtype=jnp.int32)
    gains = [attn_gain, query_gain, key_gain, ffn_gain]
    wanted = (jnp.arange(LANES, dtype=jnp.int32)[:, None] == (labels ^ here)[None, :]).astype(BF16)
    router_rows = jnp.dot(wanted, router[0].T, preferred_element_type=F32).astype(BF16)
    up_weight = weight_in[0, 0].reshape(width, -1)
    down_weight = weight_out[0, 0]

    chosen = routes[:, 0] ^ here
    member = jnp.sum((chosen[..., None] == labels).astype(F32), axis=2)
    before = jnp.tril(jnp.ones((tokens, tokens), F32), -1)
    ranking = jnp.einsum("ij,tje->tie", before, member).astype(jnp.int32)
    ranking = jnp.where(member > 0, ranking, -1)
    slot = jnp.arange(capacity, dtype=jnp.int32)
    combine_place = (ranking[:, :, :, None] == slot).astype(BF16)
    combine_place = combine_place.reshape(ticks, tokens, count * capacity)
    send_place = (ranking.transpose(0, 2, 1)[:, :, None, :] == slot[:, None]).astype(BF16)
    send_place = send_place.reshape(ticks, count * capacity, tokens)

    near = range(count // 2)
    far, farther = range(count // 2, 3 * count // 4), range(3 * count // 4, count)

    def exchange(blocks):
        got = list(blocks)
        for k in [*far, *near]:
            got[k] = across(blocks[k], k, both)
        for k, sooner in zip(farther, far):
            block, got[sooner] = lax.optimization_barrier((blocks[k], got[sooner]))
            got[k] = across(block, k, both)
        return got

    def experts(own):
        other = [to_other_plane(block, both) for block in own]
        away, kept = [], []
        for group in ([*near, *far], farther):
            mine, theirs = [own[k] for k in group], [other[k] for k in group]
            if kept:
                theirs[0], kept[0] = lax.optimization_barrier((theirs[0], kept[0]))
            made = expert_rows(scalars, mine, theirs, up_weight, down_weight, ffn_gain)
            away += made[0]
            kept += made[1]
        received = [None] * count
        for k in [*far, *farther]:
            received[k] = to_other_plane(away[k], both)
        for k in near:
            later = far[k % len(far)]
            block, received[later] = lax.optimization_barrier((away[k], received[later]))
            received[k] = to_other_plane(block, both)
        return [k + r for k, r in zip(kept, received)]

    def whole_rows(made):
        other = to_other_plane(made, both)
        low, high = jnp.where(plane == 0, made, other), jnp.where(plane == 0, other, made)
        return jnp.concatenate([low, high], axis=1)

    ids = held_meta[0:1]
    sent_ids = [to_next_phase(ids, step, False) for step in (0, 1)]
    held_meta, up_weight, *sent_ids = lax.optimization_barrier((held_meta, up_weight, *sent_ids))
    residual, stats, rows = attend(
        False, width, count, scalars, [held, held_prior, held_meta, held_prior_meta],
        gains, router_rows, send_place[0],
    )
    stats_other = to_other_plane(stats, both)
    returned = exchange(experts(exchange(rows)))
    made, squares = combine(
        count, width, returned, residual, stats, stats_other, combine_place[0]
    )

    fresh = half_of(fresh_rows[0])
    fresh_prior = to_next_block(fresh, (0,))
    fresh_meta = meta_of(fresh_rows[0], doc_fresh[0])
    fresh_prior_meta = to_next_block(fresh_meta, (0,))
    sent_prior, sent = to_next_phase(made, 1, False), to_next_phase(made, 0, False)
    scales = [to_next_phase(squares, step, swap) for step in (0, 1) for swap in (False, True)]
    results = [whole_rows(made)]
    residual, stats, rows = attend(
        True, width, count, scalars,
        [fresh, fresh_prior, fresh_meta, fresh_prior_meta, sent, sent_prior, *sent_ids, *scales],
        gains, router_rows, send_place[1],
    )
    stats_other = to_other_plane(stats, both)
    returned = exchange(experts(exchange(rows)))
    made, squares = combine(
        count, width, returned, residual, stats, stats_other, combine_place[1]
    )
    results.append(whole_rows(made))
    return jnp.stack(results)[:, None]


def solution(mesh):
    in_specs = (
        P("section", "expert", None),
        P(None, "expert", None),
        P("section", "expert"),
        P(None, "expert"),
        P(None, "section", "expert", None),
        P("section", None),
        P("section", None),
        P("section", None),
        P("section", None),
        P("section", None, None),
        P("section", "expert", None, None, "dp"),
        P("section", "expert", "dp", None),
    )
    out_specs = P(None, "section", "expert", None)
    return jax.shard_map(body, mesh=mesh, in_specs=in_specs, out_specs=out_specs, check_vma=False)
```

time: 778 us -> 319 us (0.41); the launches traced: 768 us -> 318 us
  waiting for transfers between devices: 475 us -> 116 us
  blocking collectives: 76.4 us -> 0 us
  starting transfers between devices: 46.1 us -> 113 us
  local copies, waits for them, and re-layouts: 73.5 us -> 21.7 us
  Pallas kernels: 0 us -> 49.9 us
  matrix products: 43.7 us -> 1.22 us
  other arithmetic: 38.8 us -> 15.6 us
  between operations: 14.4 us -> 0.72 us
    all_to_all x3 -> x0, waiting for transfers between devices: 181 us -> none  [the longest x2 134 us: layer(): lax.all_to_all(expert_rows.reshape(experts, capacity, model_width), 'expe...]
    reduce_scatter x2 -> x0, waiting for transfers between devices: 151 us -> none  [layer(): lax.psum_scatter(jnp.dot(inner_act, weight_out, preferred_element_type=jn...]
    all_gather x4 -> x0, waiting for transfers between devices: 130 us -> none  [the longest x2 90.2 us: layer(): lax.all_gather(summed.astype(jnp.bfloat16), 'dp', axis=0, tiled=True)]
    ppermute x6 -> x76, waiting for transfers between devices: 14.2 us -> 116 us  [the longest x36 81.9 us: to_other_plane(): return lax.ppermute(array, ('section', 'dp'), pairs)]
    ppermute x6 -> x76, starting transfers between devices: 18.3 us -> 113 us  [the longest x28 46.1 us: across(): return lax.ppermute(array, ('section', 'expert'), pairs)]
    all_to_all x1 -> x0, blocking collectives: 76.4 us -> none  [layer(): lax.all_to_all(grouped, 'expert', split_axis=0, concat_axis=0, tiled=True)]
    pallas_call x0 -> x8, Pallas kernels: none -> 49.9 us  [the longest x4 40.3 us: expert_rows(): pl.pallas_call(functools.partial(expert_kernel, blocks, width), out_shape...]
    dot_general x8 -> x2, matrix products: 36.5 us -> 1.22 us  [the longest x1 0.82 us: body(): ranking = jnp.einsum('ij,tje->tie', before, member).astype(jnp.int32)]
  transfers between devices with their start and end apart: 15 -> 76, of which waited for: 12 -> 36; matrix products, arithmetic and copies ran while one was open for 4% -> 10% of each run, Pallas kernels for 0% -> 14%
where the time goes in v1:
time: 319 us; the launch traced here: 318 us
  waiting for transfers between devices  116 us (36%)
  starting transfers between devices  113 us (35%)
  Pallas kernels  49.9 us (16%)
  local copies, waits for them, and re-layouts  21.7 us (7%)
  other arithmetic  15.6 us (5%)
    ppermute x36, waiting for transfers between devices, to_other_plane(): return lax.ppermute(array, ('section', 'dp'), pairs)  81.9 us
    ppermute x28, starting transfers between devices, across(): return lax.ppermute(array, ('section', 'expert'), pairs)  46.1 us
    ppermute x36, starting transfers between devices, to_other_plane(): return lax.ppermute(array, ('section', 'dp'), pairs)  41.3 us
    pallas_call x4, Pallas kernels, expert_rows(): pl.pallas_call(functools.partial(expert_kernel, blocks, width), out_shape...  40.3 us
    ppermute x28, waiting for transfers between devices, across(): return lax.ppermute(array, ('section', 'expert'), pairs)  28.6 us
    unnamed x63, local copies, waits for them, and re-layouts  18.7 us
    ppermute x8, starting transfers between devices, to_next_phase(): return lax.ppermute(array, ('section', 'expert', 'dp'), pairs)  13.4 us
    ppermute x4, starting transfers between devices, to_next_block(): return lax.ppermute(array, ('section', 'expert'), pairs)  12.7 us
  transfers between devices with their start and end apart: 76, of which 36 were waited for; matrix products, arithmetic and copies ran while one was open for 10% of the time, Pallas kernels for 14%

profile of v1, /device:TPU:0, one launch (start us, length us, event | category | flops | bytes accessed | tf_op | source)
XLA Modules:
  0.0 318.1 jit_solution(11834412421057567967)
XLA Ops:
  0.7 2.3 collective-permute-start.1
  3.1 3.2 %collective-permute-start.2 = (f32[1,128]{1,0:T(1,128)S(1)}, f32[1,128]{1,0:T(1,128)S(1)}, u32[]{:S(2)}, u32[]{:S(2)}) collective-permute-start(f32[1,128]{1,0:T(1,128)S(1)} %add_convert_fusion.1), channel_id=1, source_target_pairs={{0,18},{1,19},{2,20},{3,21},{4,22},{5,23},{6,24},{7,25},{8,26},{9,... | collective-permute-start | bytes 1544 | tf_op jit(solution)/shard_map/ppermute | solution.py:47
  7.4 3.5 %collective-permute-start = (bf16[128,2048]{1,0:T(8,128)(2,1)S(1)}, bf16[128,2048]{1,0:T(8,128)(2,1)S(1)}, u32[]{:S(2)}, u32[]{:S(2)}) collective-permute-start(bf16[128,2048]{1,0:T(8,128)(2,1)S(1)} %dynamic-slice_bitcast_fusion.1.own_ref), channel_id=1, source_target_pairs={{0,2},{2,4},{4,6},{6,8},{8,10},{10,12},{12,14},{16,18},{18,20},{20... | collective-permute-start | bytes 1572872 | tf_op jit(solution)/shard_map/ppermute | solution.py:37
  12.4 3.4 %collective-permute-start.3 = (f32[2,128]{1,0:T(2,128)S(1)}, f32[2,128]{1,0:T(2,128)S(1)}, u32[]{:S(2)}, u32[]{:S(2)}) collective-permute-start(f32[2,128]{1,0:T(2,128)S(1)} %pad_maximum_fusion.refs_0_), channel_id=1, source_target_pairs={{0,2},{2,4},{4,6},{6,8},{8,10},{10,12},{12,14},{16,18},{18,20},{20... | collective-permute-start | bytes 3080 | tf_op jit(solution)/shard_map/ppermute | solution.py:37
  17.3 13.9 %copy.23 = bf16[512,8,2,768]{3,1,2,0:T(8,128)(2,1)} copy(bf16[512,8,2,768]{3,2,1,0:T(2,128)(2,1)} %bitcast.57) | data formatting | bytes 25165824
  31.3 2.9 attend.2
  35.1 2.0 collective-permute-start.10
  42.5 8.5 %collective-permute-done.10.refs_5_ = bf16[48,2048]{1,0:T(8,128)(2,1)S(1)} collective-permute-done((bf16[48,2048]{1,0:T(8,128)(2,1)S(1)}, bf16[48,2048]{1,0:T(8,128)(2,1)S(1)}, u32[]{:S(2)}, u32[]{:S(2)}) %collective-permute-start.10) | collective-permute-done | bytes 196640 | tf_op jit(solution)/shard_map/ppermute | solution.py:60
  59.8 2.3 collective-permute-done.16.refs_11_
  62.1 3.5 %collective-permute-start.5 = (bf16[48,2048]{1,0:T(8,128)(2,1)S(1)}, bf16[48,2048]{1,0:T(8,128)(2,1)S(1)}, u32[]{:S(2)}, u32[]{:S(2)}) collective-permute-start(bf16[48,2048]{1,0:T(8,128)(2,1)S(1)} %get-tuple-element.103), channel_id=1, source_target_pairs={{0,12},{2,14},{4,8},{6,10},{8,4},{10,6},{12,0},{14,2},{16,28},{18,... | collective-permute-start | bytes 589832 | tf_op jit(solution)/shard_map/ppermute | solution.py:60
  66.3 3.6 %collective-permute-start.26 = (bf16[48,2048]{1,0:T(8,128)(2,1)S(1)}, bf16[48,2048]{1,0:T(8,128)(2,1)S(1)}, u32[]{:S(2)}, u32[]{:S(2)}) collective-permute-start(bf16[48,2048]{1,0:T(8,128)(2,1)S(1)} %get-tuple-element.130), channel_id=1, source_target_pairs={{0,14},{2,12},{4,10},{6,8},{8,6},{10,4},{12,2},{14,0},{16,30},{18,... | collective-permute-start | bytes 589832 | tf_op jit(solution)/shard_map/ppermute | solution.py:60
  70.5 4.2 %collective-permute-done.13.refs_8_ = bf16[48,2048]{1,0:T(8,128)(2,1)S(1)} collective-permute-done((bf16[48,2048]{1,0:T(8,128)(2,1)S(1)}, bf16[48,2048]{1,0:T(8,128)(2,1)S(1)}, u32[]{:S(2)}, u32[]{:S(2)}) %collective-permute-start.13) | collective-permute-done | bytes 196640 | tf_op jit(solution)/shard_map/ppermute | solution.py:52
  74.7 3.1 collective-permute-done.14.refs_9_
  77.8 12.0 %expert_rows.4 = (bf16[48,2048]{1,0:T(8,128)(2,1)S(1)}, bf16[48,2048]{1,0:T(8,128)(2,1)S(1)}, bf16[48,2048]{1,0:T(8,128)(2,1)S(1)}, bf16[48,2048]{1,0:T(8,128)(2...) custom-call(s32[2]{0:T(128)S(1)} %pad_add_fusion.scalar_ref, ...), custom_call_target="tpu_custom_call" | custom-call | flops 1 | bytes 1 | tf_op jit(solution)/shard_map/expert_rows/pallas_call | solution.py:278
  94.0 3.8 %collective-permute-done.19 = bf16[48,2048]{1,0:T(8,128)(2,1)S(1)} collective-permute-done((bf16[48,2048]{1,0:T(8,128)(2,1)S(1)}, bf16[48,2048]{1,0:T(8,128)(2,1)S(1)}, u32[]{:S(2)}, u32[]{:S(2)}) %collective-permute-start.19) | collective-permute-done | bytes 196640 | tf_op jit(solution)/shard_map/ppermute | solution.py:52
  97.9 4.1 %collective-permute-done.6.refs_2_ = bf16[48,2048]{1,0:T(8,128)(2,1)S(1)} collective-permute-done((bf16[48,2048]{1,0:T(8,128)(2,1)S(1)}, bf16[48,2048]{1,0:T(8,128)(2,1)S(1)}, u32[]{:S(2)}, u32[]{:S(2)}) %collective-permute-start.6) | collective-permute-done | bytes 196640 | tf_op jit(solution)/shard_map/ppermute | solution.py:52
  102.0 4.2 %collective-permute-done.27.refs_3_ = bf16[48,2048]{1,0:T(8,128)(2,1)S(1)} collective-permute-done((bf16[48,2048]{1,0:T(8,128)(2,1)S(1)}, bf16[48,2048]{1,0:T(8,128)(2,1)S(1)}, u32[]{:S(2)}, u32[]{:S(2)}) %collective-permute-start.27) | collective-permute-done | bytes 196640 | tf_op jit(solution)/shard_map/ppermute | solution.py:52
  106.2 8.3 %expert_rows.5 = (bf16[48,2048]{1,0:T(8,128)(2,1)S(1)}, bf16[48,2048]{1,0:T(8,128)(2,1)S(1)}, bf16[48,2048]{1,0:T(8,128)(2,1)S(1)}, bf16[48,2048]{1,0:T(8,128)(2,1)S(1)}) custom-call(s32[2]{0:T(128)S(1)} %pad_add_fusion.scalar_ref, bf16[48,2048]{1,0:T(8,128)(2,1)S(1)} %collective-permute-done.5.refs_0_, ...), custom_call_target="tpu_custom_call" | custom-call | flops 1 | bytes 1 | tf_op jit(solution)/shard_map/expert_rows/pallas_call | solution.py:278
  118.9 3.5 %collective-permute-done.30 = bf16[48,2048]{1,0:T(8,128)(2,1)S(1)} collective-permute-done((bf16[48,2048]{1,0:T(8,128)(2,1)S(1)}, bf16[48,2048]{1,0:T(8,128)(2,1)S(1)}, u32[]{:S(2)}, u32[]{:S(2)}) %collective-permute-start.30) | collective-permute-done | bytes 196640 | tf_op jit(solution)/shard_map/ppermute | solution.py:52
  124.4 2.2 collective-permute-done.28
  129.6 2.6 collective-permute-done.24
  132.2 2.3 collective-permute-start.33
  146.3 3.4 %collective-permute-start.36 = (bf16[128,2048]{1,0:T(8,128)(2,1)S(1)}, bf16[128,2048]{1,0:T(8,128)(2,1)S(1)}, u32[]{:S(2)}, u32[]{:S(2)}) collective-permute-start(bf16[128,2048]{1,0:T(8,128)(2,1)S(1)} %dynamic-slice_bitcast_fusion.own_ref), channel_id=1, source_target_pairs={{0,2},{2,4},{4,6},{6,8},{8,10},{10,12},{12,14},{1,3},{3,5},{5,7},{... | collective-permute-start | bytes 1572872 | tf_op jit(solution)/shard_map/ppermute | solution.py:37
  154.4 2.4 collective-permute-start.37
  158.1 3.7 %collective-permute-done.37.refs_1_ = f32[2,128]{1,0:T(2,128)S(1)} collective-permute-done((f32[2,128]{1,0:T(2,128)S(1)}, f32[2,128]{1,0:T(2,128)S(1)}, u32[]{:S(2)}, u32[]{:S(2)}) %collective-permute-start.37) | collective-permute-done | bytes 1056 | tf_op jit(solution)/shard_map/ppermute | solution.py:37
  167.1 3.0 attend.3
  171.0 2.7 collective-permute-start.50
  173.7 2.1 collective-permute-start.44
  179.2 8.7 %collective-permute-done.50.refs_5_ = bf16[48,2048]{1,0:T(8,128)(2,1)S(1)} collective-permute-done((bf16[48,2048]{1,0:T(8,128)(2,1)S(1)}, bf16[48,2048]{1,0:T(8,128)(2,1)S(1)}, u32[]{:S(2)}, u32[]{:S(2)}) %collective-permute-start.50) | collective-permute-done | bytes 196640 | tf_op jit(solution)/shard_map/ppermute | solution.py:60
  189.8 4.1 %collective-permute-done.44.refs_4_ = bf16[48,2048]{1,0:T(8,128)(2,1)S(1)} collective-permute-done((bf16[48,2048]{1,0:T(8,128)(2,1)S(1)}, bf16[48,2048]{1,0:T(8,128)(2,1)S(1)}, u32[]{:S(2)}, u32[]{:S(2)}) %collective-permute-start.44) | collective-permute-done | bytes 196640 | tf_op jit(solution)/shard_map/ppermute | solution.py:60
  198.5 3.2 %collective-permute-done.56.refs_11_ = bf16[48,2048]{1,0:T(8,128)(2,1)S(1)} collective-permute-done((bf16[48,2048]{1,0:T(8,128)(2,1)S(1)}, bf16[48,2048]{1,0:T(8,128)(2,1)S(1)}, u32[]{:S(2)}, u32[]{:S(2)}) %collective-permute-start.56) | collective-permute-done | bytes 196640 | tf_op jit(solution)/shard_map/ppermute | solution.py:52
  201.7 3.8 %collective-permute-start.45 = (bf16[48,2048]{1,0:T(8,128)(2,1)S(1)}, bf16[48,2048]{1,0:T(8,128)(2,1)S(1)}, u32[]{:S(2)}, u32[]{:S(2)}) collective-permute-start(bf16[48,2048]{1,0:T(8,128)(2,1)S(1)} %get-tuple-element.152), channel_id=1, source_target_pairs={{0,12},{2,14},{4,8},{6,10},{8,4},{10,6},{12,0},{14,2},{16,28},{18,... | collective-permute-start | bytes 589832 | tf_op jit(solution)/shard_map/ppermute | solution.py:60
  205.9 3.5 %collective-permute-start.66 = (bf16[48,2048]{1,0:T(8,128)(2,1)S(1)}, bf16[48,2048]{1,0:T(8,128)(2,1)S(1)}, u32[]{:S(2)}, u32[]{:S(2)}) collective-permute-start(bf16[48,2048]{1,0:T(8,128)(2,1)S(1)} %get-tuple-element.178), channel_id=1, source_target_pairs={{0,14},{2,12},{4,10},{6,8},{8,6},{10,4},{12,2},{14,0},{16,30},{18,... | collective-permute-start | bytes 589832 | tf_op jit(solution)/shard_map/ppermute | solution.py:60
  210.1 4.2 %collective-permute-done.53.refs_8_ = bf16[48,2048]{1,0:T(8,128)(2,1)S(1)} collective-permute-done((bf16[48,2048]{1,0:T(8,128)(2,1)S(1)}, bf16[48,2048]{1,0:T(8,128)(2,1)S(1)}, u32[]{:S(2)}, u32[]{:S(2)}) %collective-permute-start.53) | collective-permute-done | bytes 196640 | tf_op jit(solution)/shard_map/ppermute | solution.py:52
  214.3 3.0 collective-permute-done.54.refs_9_
  217.3 2.8 copy-done.2
  220.1 11.7 %expert_rows.6 = (bf16[48,2048]{1,0:T(8,128)(2,1)S(1)}, bf16[48,2048]{1,0:T(8,128)(2,1)S(1)}, bf16[48,2048]{1,0:T(8,128)(2,1)S(1)}, bf16[48,2048]{1,0:T(8,128)(2...) custom-call(s32[2]{0:T(128)S(1)} %pad_add_fusion.scalar_ref, ...), custom_call_target="tpu_custom_call" | custom-call | flops 1 | bytes 1 | tf_op jit(solution)/shard_map/expert_rows/pallas_call | solution.py:278
  236.0 3.8 %collective-permute-done.59 = bf16[48,2048]{1,0:T(8,128)(2,1)S(1)} collective-permute-done((bf16[48,2048]{1,0:T(8,128)(2,1)S(1)}, bf16[48,2048]{1,0:T(8,128)(2,1)S(1)}, u32[]{:S(2)}, u32[]{:S(2)}) %collective-permute-start.59) | collective-permute-done | bytes 196640 | tf_op jit(solution)/shard_map/ppermute | solution.py:52
  239.9 4.1 %collective-permute-done.46.refs_2_ = bf16[48,2048]{1,0:T(8,128)(2,1)S(1)} collective-permute-done((bf16[48,2048]{1,0:T(8,128)(2,1)S(1)}, bf16[48,2048]{1,0:T(8,128)(2,1)S(1)}, u32[]{:S(2)}, u32[]{:S(2)}) %collective-permute-start.46) | collective-permute-done | bytes 196640 | tf_op jit(solution)/shard_map/ppermute | solution.py:52
  244.0 4.2 %collective-permute-done.67.refs_3_ = bf16[48,2048]{1,0:T(8,128)(2,1)S(1)} collective-permute-done((bf16[48,2048]{1,0:T(8,128)(2,1)S(1)}, bf16[48,2048]{1,0:T(8,128)(2,1)S(1)}, u32[]{:S(2)}, u32[]{:S(2)}) %collective-permute-start.67) | collective-permute-done | bytes 196640 | tf_op jit(solution)/shard_map/ppermute | solution.py:52
  248.2 8.3 %expert_rows.7 = (bf16[48,2048]{1,0:T(8,128)(2,1)S(1)}, bf16[48,2048]{1,0:T(8,128)(2,1)S(1)}, bf16[48,2048]{1,0:T(8,128)(2,1)S(1)}, bf16[48,2048]{1,0:T(8,128)(2,1)S(1)}) custom-call(s32[2]{0:T(128)S(1)} %pad_add_fusion.scalar_ref, bf16[48,2048]{1,0:T(8,128)(2,1)S(1)} %collective-permute-done.45.refs_0_, ...), custom_call_target="tpu_custom_call" | custom-call | flops 1 | bytes 1 | tf_op jit(solution)/shard_map/expert_rows/pallas_call | solution.py:278
  260.8 3.6 %collective-permute-done.70 = bf16[48,2048]{1,0:T(8,128)(2,1)S(1)} collective-permute-done((bf16[48,2048]{1,0:T(8,128)(2,1)S(1)}, bf16[48,2048]{1,0:T(8,128)(2,1)S(1)}, u32[]{:S(2)}, u32[]{:S(2)}) %collective-permute-start.70) | collective-permute-done | bytes 196640 | tf_op jit(solution)/shard_map/ppermute | solution.py:52
  269.9 2.9 collective-permute-done.64
  272.8 3.5 %collective-permute-start.73 = (bf16[48,2048]{1,0:T(8,128)(2,1)S(1)}, bf16[48,2048]{1,0:T(8,128)(2,1)S(1)}, u32[]{:S(2)}, u32[]{:S(2)}) collective-permute-start(bf16[48,2048]{1,0:T(8,128)(2,1)S(1)} %add.112), channel_id=1, source_target_pairs={{0,14},{2,12},{4,10},{6,8},{8,6},{10,4},{12,2},{14,0},{16,30},{18,... | collective-permute-start | bytes 589832 | tf_op jit(solution)/shard_map/ppermute | solution.py:60
  276.3 11.9 %collective-permute-done.62 = bf16[48,2048]{1,0:T(8,128)(2,1)S(1)} collective-permute-done((bf16[48,2048]{1,0:T(8,128)(2,1)S(1)}, bf16[48,2048]{1,0:T(8,128)(2,1)S(1)}, u32[]{:S(2)}, u32[]{:S(2)}) %collective-permute-start.62) | collective-permute-done | bytes 196640 | tf_op jit(solution)/shard_map/ppermute | solution.py:52
  299.9 2.6 collective-permute-done.65.refs_3_
  305.9 2.2 collective-permute-start.75
  309.2 7.1 %collective-permute-done.75 = bf16[128,2048]{1,0:T(8,128)(2,1)S(1)} collective-permute-done((bf16[128,2048]{1,0:T(8,128)(2,1)S(1)}, bf16[128,2048]{1,0:T(8,128)(2,1)S(1)}, u32[]{:S(2)}, u32[]{:S(2)}) %collective-permute-start.75) | collective-permute-done | bytes 524320 | tf_op jit(solution)/shard_map/ppermute | solution.py:52
  (223 shorter events, 101.5 us)
Async XLA Ops:
  0.7 30.5 %collective-permute-start.1 = (f32[1,128]{1,0:T(1,128)S(1)}, f32[1,128]{1,0:T(1,128)S(1)}, u32[]{:S(2)}, u32[]{:S(2)}) collective-permute-start(f32[1,128]{1,0:T(1,128)S(1)} %add_convert_fusion.1), channel_id=1, source_target_pairs={{0,16},{1,17},{2,18},{3,19},{4,20},{5,21},{6,22},{7,23},{8,24},{9,... | collective-permute-start | bytes 1544 | tf_op jit(solution)/shard_map/ppermute | solution.py:47
  3.1 28.2 %collective-permute-start.2 = (f32[1,128]{1,0:T(1,128)S(1)}, f32[1,128]{1,0:T(1,128)S(1)}, u32[]{:S(2)}, u32[]{:S(2)}) collective-permute-start(f32[1,128]{1,0:T(1,128)S(1)} %add_convert_fusion.1), channel_id=1, source_target_pairs={{0,18},{1,19},{2,20},{3,21},{4,22},{5,23},{6,24},{7,25},{8,26},{9,... | collective-permute-start | bytes 1544 | tf_op jit(solution)/shard_map/ppermute | solution.py:47
  7.4 23.8 %collective-permute-start = (bf16[128,2048]{1,0:T(8,128)(2,1)S(1)}, bf16[128,2048]{1,0:T(8,128)(2,1)S(1)}, u32[]{:S(2)}, u32[]{:S(2)}) collective-permute-start(bf16[128,2048]{1,0:T(8,128)(2,1)S(1)} %dynamic-slice_bitcast_fusion.1.own_ref), channel_id=1, source_target_pairs={{0,2},{2,4},{4,6},{6,8},{8,10},{10,12},{12,14},{16,18},{18,20},{20... | collective-permute-start | bytes 1572872 | tf_op jit(solution)/shard_map/ppermute | solution.py:37
  12.4 18.8 %collective-permute-start.3 = (f32[2,128]{1,0:T(2,128)S(1)}, f32[2,128]{1,0:T(2,128)S(1)}, u32[]{:S(2)}, u32[]{:S(2)}) collective-permute-start(f32[2,128]{1,0:T(2,128)S(1)} %pad_maximum_fusion.refs_0_), channel_id=1, source_target_pairs={{0,2},{2,4},{4,6},{6,8},{8,10},{10,12},{12,14},{16,18},{18,20},{20... | collective-permute-start | bytes 3080 | tf_op jit(solution)/shard_map/ppermute | solution.py:37
  35.1 15.9 %collective-permute-start.10 = (bf16[48,2048]{1,0:T(8,128)(2,1)S(1)}, bf16[48,2048]{1,0:T(8,128)(2,1)S(1)}, u32[]{:S(2)}, u32[]{:S(2)}) collective-permute-start(bf16[48,2048]{1,0:T(8,128)(2,1)S(1)} %get-tuple-element.110), channel_id=1, source_target_pairs={{0,10},{2,8},{4,14},{6,12},{8,2},{10,0},{12,6},{14,4},{16,26},{18,... | collective-permute-start | bytes 589832 | tf_op jit(solution)/shard_map/ppermute | solution.py:60
  37.2 17.1 %collective-permute-start.4 = (bf16[48,2048]{1,0:T(8,128)(2,1)S(1)}, bf16[48,2048]{1,0:T(8,128)(2,1)S(1)}, u32[]{:S(2)}, u32[]{:S(2)}) collective-permute-start(bf16[48,2048]{1,0:T(8,128)(2,1)S(1)} %get-tuple-element.102), channel_id=1, source_target_pairs={{0,8},{2,10},{4,12},{6,14},{8,0},{10,2},{12,4},{14,6},{16,24},{18,... | collective-permute-start | bytes 589832 | tf_op jit(solution)/shard_map/ppermute | solution.py:60
  39.0 16.7 %collective-permute-start.7 = (bf16[48,2048]{1,0:T(8,128)(2,1)S(1)}, bf16[48,2048]{1,0:T(8,128)(2,1)S(1)}, u32[]{:S(2)}, u32[]{:S(2)}) collective-permute-start(bf16[48,2048]{1,0:T(8,128)(2,1)S(1)} %get-tuple-element.105), channel_id=1, source_target_pairs={{0,2},{2,0},{4,6},{6,4},{8,10},{10,8},{12,14},{14,12},{16,18},{18,... | collective-permute-start | bytes 589832 | tf_op jit(solution)/shard_map/ppermute | solution.py:60
  39.5 16.8 %collective-permute-start.8 = (bf16[48,2048]{1,0:T(8,128)(2,1)S(1)}, bf16[48,2048]{1,0:T(8,128)(2,1)S(1)}, u32[]{:S(2)}, u32[]{:S(2)}) collective-permute-start(bf16[48,2048]{1,0:T(8,128)(2,1)S(1)} %get-tuple-element.106), channel_id=1, source_target_pairs={{0,4},{2,6},{4,0},{6,2},{8,12},{10,14},{12,8},{14,10},{16,20},{18,... | collective-permute-start | bytes 589832 | tf_op jit(solution)/shard_map/ppermute | solution.py:60
  41.1 16.7 %collective-permute-start.9 = (bf16[48,2048]{1,0:T(8,128)(2,1)S(1)}, bf16[48,2048]{1,0:T(8,128)(2,1)S(1)}, u32[]{:S(2)}, u32[]{:S(2)}) collective-permute-start(bf16[48,2048]{1,0:T(8,128)(2,1)S(1)} %get-tuple-element.107), channel_id=1, source_target_pairs={{0,6},{2,4},{4,2},{6,0},{8,14},{10,12},{12,10},{14,8},{16,22},{18,... | collective-permute-start | bytes 589832 | tf_op jit(solution)/shard_map/ppermute | solution.py:60
  56.3 14.2 %collective-permute-start.12 = (bf16[48,2048]{1,0:T(8,128)(2,1)S(1)}, bf16[48,2048]{1,0:T(8,128)(2,1)S(1)}, u32[]{:S(2)}, u32[]{:S(2)}) collective-permute-start(bf16[48,2048]{1,0:T(8,128)(2,1)S(1)} %collective-permute-done.7.refs_1_), channel_id=1, source_target_pairs={{0,1},{1,0},{16,17},{17,16},{2,3},{3,2},{18,19},{19,18},{4,5},{5,4... | collective-permute-start | bytes 589832 | tf_op jit(solution)/shard_map/ppermute | solution.py:52
  57.8 16.9 %collective-permute-start.13 = (bf16[48,2048]{1,0:T(8,128)(2,1)S(1)}, bf16[48,2048]{1,0:T(8,128)(2,1)S(1)}, u32[]{:S(2)}, u32[]{:S(2)}) collective-permute-start(bf16[48,2048]{1,0:T(8,128)(2,1)S(1)} %collective-permute-done.8.refs_2_), channel_id=1, source_target_pairs={{0,1},{1,0},{16,17},{17,16},{2,3},{3,2},{18,19},{19,18},{4,5},{5,4... | collective-permute-start | bytes 589832 | tf_op jit(solution)/shard_map/ppermute | solution.py:52
  58.3 19.5 %collective-permute-start.14 = (bf16[48,2048]{1,0:T(8,128)(2,1)S(1)}, bf16[48,2048]{1,0:T(8,128)(2,1)S(1)}, u32[]{:S(2)}, u32[]{:S(2)}) collective-permute-start(bf16[48,2048]{1,0:T(8,128)(2,1)S(1)} %collective-permute-done.9.refs_3_), channel_id=1, source_target_pairs={{0,1},{1,0},{16,17},{17,16},{2,3},{3,2},{18,19},{19,18},{4,5},{5,4... | collective-permute-start | bytes 589832 | tf_op jit(solution)/shard_map/ppermute | solution.py:52
  62.1 29.3 %collective-permute-start.5 = (bf16[48,2048]{1,0:T(8,128)(2,1)S(1)}, bf16[48,2048]{1,0:T(8,128)(2,1)S(1)}, u32[]{:S(2)}, u32[]{:S(2)}) collective-permute-start(bf16[48,2048]{1,0:T(8,128)(2,1)S(1)} %get-tuple-element.103), channel_id=1, source_target_pairs={{0,12},{2,14},{4,8},{6,10},{8,4},{10,6},{12,0},{14,2},{16,28},{18,... | collective-permute-start | bytes 589832 | tf_op jit(solution)/shard_map/ppermute | solution.py:60
  66.3 25.7 %collective-permute-start.26 = (bf16[48,2048]{1,0:T(8,128)(2,1)S(1)}, bf16[48,2048]{1,0:T(8,128)(2,1)S(1)}, u32[]{:S(2)}, u32[]{:S(2)}) collective-permute-start(bf16[48,2048]{1,0:T(8,128)(2,1)S(1)} %get-tuple-element.130), channel_id=1, source_target_pairs={{0,14},{2,12},{4,10},{6,8},{8,6},{10,4},{12,2},{14,0},{16,30},{18,... | collective-permute-start | bytes 589832 | tf_op jit(solution)/shard_map/ppermute | solution.py:60
  92.0 14.2 %collective-permute-start.27 = (bf16[48,2048]{1,0:T(8,128)(2,1)S(1)}, bf16[48,2048]{1,0:T(8,128)(2,1)S(1)}, u32[]{:S(2)}, u32[]{:S(2)}) collective-permute-start(bf16[48,2048]{1,0:T(8,128)(2,1)S(1)} %collective-permute-done.26.refs_1_), channel_id=1, source_target_pairs={{0,1},{1,0},{16,17},{17,16},{2,3},{3,2},{18,19},{19,18},{4,5},{5,4... | collective-permute-start | bytes 589832 | tf_op jit(solution)/shard_map/ppermute | solution.py:52
  93.4 22.6 %collective-permute-start.17 = (bf16[48,2048]{1,0:T(8,128)(2,1)S(1)}, bf16[48,2048]{1,0:T(8,128)(2,1)S(1)}, u32[]{:S(2)}, u32[]{:S(2)}) collective-permute-start(bf16[48,2048]{1,0:T(8,128)(2,1)S(1)} %get-tuple-element.116), channel_id=1, source_target_pairs={{0,1},{1,0},{16,17},{17,16},{2,3},{3,2},{18,19},{19,18},{4,5},{5,4... | collective-permute-start | bytes 589832 | tf_op jit(solution)/shard_map/ppermute | solution.py:52
  97.8 20.6 %collective-permute-start.31 = (bf16[48,2048]{1,0:T(8,128)(2,1)S(1)}, bf16[48,2048]{1,0:T(8,128)(2,1)S(1)}, u32[]{:S(2)}, u32[]{:S(2)}) collective-permute-start(bf16[48,2048]{1,0:T(8,128)(2,1)S(1)} %add.103), channel_id=1, source_target_pairs={{0,10},{2,8},{4,14},{6,12},{8,2},{10,0},{12,6},{14,4},{16,26},{18,... | collective-permute-start | bytes 589832 | tf_op jit(solution)/shard_map/ppermute | solution.py:60
  116.8 22.7 %collective-permute-start.34 = (f32[128,128]{1,0:T(8,128)S(1)}, f32[128,128]{1,0:T(8,128)S(1)}, u32[]{:S(2)}, u32[]{:S(2)}) collective-permute-start(f32[128,128]{1,0:T(8,128)S(1)} %get-tuple-element.145.refs_9_), channel_id=1, source_target_pairs={{0,1},{1,0},{16,17},{17,16},{2,3},{3,2},{18,19},{19,18},{4,5},{5,4... | collective-permute-start | bytes 196616 | tf_op jit(solution)/shard_map/ppermute | solution.py:52
  118.4 13.8 %collective-permute-start.24 = (bf16[48,2048]{1,0:T(8,128)(2,1)S(1)}, bf16[48,2048]{1,0:T(8,128)(2,1)S(1)}, u32[]{:S(2)}, u32[]{:S(2)}) collective-permute-start(bf16[48,2048]{1,0:T(8,128)(2,1)S(1)} %get-tuple-element.129), channel_id=1, source_target_pairs={{0,1},{1,0},{16,17},{17,16},{2,3},{3,2},{18,19},{19,18},{4,5},{5,4... | collective-permute-start | bytes 589832 | tf_op jit(solution)/shard_map/ppermute | solution.py:52
  122.4 13.2 %collective-permute-start.22 = (bf16[48,2048]{1,0:T(8,128)(2,1)S(1)}, bf16[48,2048]{1,0:T(8,128)(2,1)S(1)}, u32[]{:S(2)}, u32[]{:S(2)}) collective-permute-start(bf16[48,2048]{1,0:T(8,128)(2,1)S(1)} %get-tuple-element.125), channel_id=1, source_target_pairs={{0,1},{1,0},{16,17},{17,16},{2,3},{3,2},{18,19},{19,18},{4,5},{5,4... | collective-permute-start | bytes 589832 | tf_op jit(solution)/shard_map/ppermute | solution.py:52
  123.9 13.8 %collective-permute-start.20 = (bf16[48,2048]{1,0:T(8,128)(2,1)S(1)}, bf16[48,2048]{1,0:T(8,128)(2,1)S(1)}, u32[]{:S(2)}, u32[]{:S(2)}) collective-permute-start(bf16[48,2048]{1,0:T(8,128)(2,1)S(1)} %get-tuple-element.121), channel_id=1, source_target_pairs={{0,1},{1,0},{16,17},{17,16},{2,3},{3,2},{18,19},{19,18},{4,5},{5,4... | collective-permute-start | bytes 589832 | tf_op jit(solution)/shard_map/ppermute | solution.py:52
  126.6 14.6 %collective-permute-start.18 = (bf16[48,2048]{1,0:T(8,128)(2,1)S(1)}, bf16[48,2048]{1,0:T(8,128)(2,1)S(1)}, u32[]{:S(2)}, u32[]{:S(2)}) collective-permute-start(bf16[48,2048]{1,0:T(8,128)(2,1)S(1)} %get-tuple-element.117), channel_id=1, source_target_pairs={{0,1},{1,0},{16,17},{17,16},{2,3},{3,2},{18,19},{19,18},{4,5},{5,4... | collective-permute-start | bytes 589832 | tf_op jit(solution)/shard_map/ppermute | solution.py:52
  132.2 14.0 %collective-permute-start.33 = (bf16[48,2048]{1,0:T(8,128)(2,1)}, bf16[48,2048]{1,0:T(8,128)(2,1)S(1)}, u32[]{:S(2)}, u32[]{:S(2)}) collective-permute-start(bf16[48,2048]{1,0:T(8,128)(2,1)} %add.102), channel_id=1, source_target_pairs={{0,14},{2,12},{4,10},{6,8},{8,6},{10,4},{12,2},{14,0},{16,30},{18,... | collective-permute-start | bytes 589832 | tf_op jit(solution)/shard_map/ppermute | solution.py:60
  135.6 14.1 %collective-permute-start.32 = (bf16[48,2048]{1,0:T(8,128)(2,1)}, bf16[48,2048]{1,0:T(8,128)(2,1)S(1)}, u32[]{:S(2)}, u32[]{:S(2)}) collective-permute-start(bf16[48,2048]{1,0:T(8,128)(2,1)} %add.100), channel_id=1, source_target_pairs={{0,12},{2,14},{4,8},{6,10},{8,4},{10,6},{12,0},{14,2},{16,28},{18,... | collective-permute-start | bytes 589832 | tf_op jit(solution)/shard_map/ppermute | solution.py:60
  137.7 12.0 %collective-permute-start.25 = (bf16[48,2048]{1,0:T(8,128)(2,1)}, bf16[48,2048]{1,0:T(8,128)(2,1)S(1)}, u32[]{:S(2)}, u32[]{:S(2)}) collective-permute-start(bf16[48,2048]{1,0:T(8,128)(2,1)} %add.99), channel_id=1, source_target_pairs={{0,6},{2,4},{4,2},{6,0},{8,14},{10,12},{12,10},{14,8},{16,22},{18,... | collective-permute-start | bytes 589832 | tf_op jit(solution)/shard_map/ppermute | solution.py:60
  146.3 16.9 %collective-permute-start.36 = (bf16[128,2048]{1,0:T(8,128)(2,1)S(1)}, bf16[128,2048]{1,0:T(8,128)(2,1)S(1)}, u32[]{:S(2)}, u32[]{:S(2)}) collective-permute-start(bf16[128,2048]{1,0:T(8,128)(2,1)S(1)} %dynamic-slice_bitcast_fusion.own_ref), channel_id=1, source_target_pairs={{0,2},{2,4},{4,6},{6,8},{8,10},{10,12},{12,14},{1,3},{3,5},{5,7},{... | collective-permute-start | bytes 1572872 | tf_op jit(solution)/shard_map/ppermute | solution.py:37
  151.7 15.3 %collective-permute-start.38 = (bf16[128,2048]{1,0:T(8,128)(2,1)}, bf16[128,2048]{1,0:T(8,128)(2,1)S(1)}, u32[]{:S(2)}, u32[]{:S(2)}) collective-permute-start(bf16[128,2048]{1,0:T(8,128)(2,1)} %get-tuple-element.146), channel_id=1, source_target_pairs={{0,16},{1,17},{2,18},{3,19},{4,20},{5,21},{6,22},{7,23},{8,24},{9,... | collective-permute-start | bytes 1572872 | tf_op jit(solution)/shard_map/ppermute | solution.py:47
  153.0 14.0 %collective-permute-start.39 = (bf16[128,2048]{1,0:T(8,128)(2,1)}, bf16[128,2048]{1,0:T(8,128)(2,1)S(1)}, u32[]{:S(2)}, u32[]{:S(2)}) collective-permute-start(bf16[128,2048]{1,0:T(8,128)(2,1)} %get-tuple-element.146), channel_id=1, source_target_pairs={{0,18},{1,19},{2,20},{3,21},{4,22},{5,23},{6,24},{7,25},{8,26},{9,... | collective-permute-start | bytes 1572872 | tf_op jit(solution)/shard_map/ppermute | solution.py:47
  171.0 16.9 %collective-permute-start.50 = (bf16[48,2048]{1,0:T(8,128)(2,1)S(1)}, bf16[48,2048]{1,0:T(8,128)(2,1)S(1)}, u32[]{:S(2)}, u32[]{:S(2)}) collective-permute-start(bf16[48,2048]{1,0:T(8,128)(2,1)S(1)} %get-tuple-element.159), channel_id=1, source_target_pairs={{0,10},{2,8},{4,14},{6,12},{8,2},{10,0},{12,6},{14,4},{16,26},{18,... | collective-permute-start | bytes 589832 | tf_op jit(solution)/shard_map/ppermute | solution.py:60
  173.7 20.2 %collective-permute-start.44 = (bf16[48,2048]{1,0:T(8,128)(2,1)S(1)}, bf16[48,2048]{1,0:T(8,128)(2,1)S(1)}, u32[]{:S(2)}, u32[]{:S(2)}) collective-permute-start(bf16[48,2048]{1,0:T(8,128)(2,1)S(1)} %get-tuple-element.151), channel_id=1, source_target_pairs={{0,8},{2,10},{4,12},{6,14},{8,0},{10,2},{12,4},{14,6},{16,24},{18,... | collective-permute-start | bytes 589832 | tf_op jit(solution)/shard_map/ppermute | solution.py:60
  175.8 18.7 %collective-permute-start.47 = (bf16[48,2048]{1,0:T(8,128)(2,1)S(1)}, bf16[48,2048]{1,0:T(8,128)(2,1)S(1)}, u32[]{:S(2)}, u32[]{:S(2)}) collective-permute-start(bf16[48,2048]{1,0:T(8,128)(2,1)S(1)} %get-tuple-element.154), channel_id=1, source_target_pairs={{0,2},{2,0},{4,6},{6,4},{8,10},{10,8},{12,14},{14,12},{16,18},{18,... | collective-permute-start | bytes 589832 | tf_op jit(solution)/shard_map/ppermute | solution.py:60
  176.3 19.6 %collective-permute-start.48 = (bf16[48,2048]{1,0:T(8,128)(2,1)S(1)}, bf16[48,2048]{1,0:T(8,128)(2,1)S(1)}, u32[]{:S(2)}, u32[]{:S(2)}) collective-permute-start(bf16[48,2048]{1,0:T(8,128)(2,1)S(1)} %get-tuple-element.155), channel_id=1, source_target_pairs={{0,4},{2,6},{4,0},{6,2},{8,12},{10,14},{12,8},{14,10},{16,20},{18,... | collective-permute-start | bytes 589832 | tf_op jit(solution)/shard_map/ppermute | solution.py:60
  177.8 18.7 %collective-permute-start.49 = (bf16[48,2048]{1,0:T(8,128)(2,1)S(1)}, bf16[48,2048]{1,0:T(8,128)(2,1)S(1)}, u32[]{:S(2)}, u32[]{:S(2)}) collective-permute-start(bf16[48,2048]{1,0:T(8,128)(2,1)S(1)} %get-tuple-element.156), channel_id=1, source_target_pairs={{0,6},{2,4},{4,2},{6,0},{8,14},{10,12},{12,10},{14,8},{16,22},{18,... | collective-permute-start | bytes 589832 | tf_op jit(solution)/shard_map/ppermute | solution.py:60
  194.4 11.5 %collective-permute-start.55 = (bf16[48,2048]{1,0:T(8,128)(2,1)S(1)}, bf16[48,2048]{1,0:T(8,128)(2,1)S(1)}, u32[]{:S(2)}, u32[]{:S(2)}) collective-permute-start(bf16[48,2048]{1,0:T(8,128)(2,1)S(1)} %collective-permute-done.44.refs_4_), channel_id=1, source_target_pairs={{0,1},{1,0},{16,17},{17,16},{2,3},{3,2},{18,19},{19,18},{4,5},{5,4... | collective-permute-start | bytes 589832 | tf_op jit(solution)/shard_map/ppermute | solution.py:52
  195.9 14.2 %collective-permute-start.52 = (bf16[48,2048]{1,0:T(8,128)(2,1)S(1)}, bf16[48,2048]{1,0:T(8,128)(2,1)S(1)}, u32[]{:S(2)}, u32[]{:S(2)}) collective-permute-start(bf16[48,2048]{1,0:T(8,128)(2,1)S(1)} %collective-permute-done.47.refs_1_), channel_id=1, source_target_pairs={{0,1},{1,0},{16,17},{17,16},{2,3},{3,2},{18,19},{19,18},{4,5},{5,4... | collective-permute-start | bytes 589832 | tf_op jit(solution)/shard_map/ppermute | solution.py:52
  196.5 17.9 %collective-permute-start.53 = (bf16[48,2048]{1,0:T(8,128)(2,1)S(1)}, bf16[48,2048]{1,0:T(8,128)(2,1)S(1)}, u32[]{:S(2)}, u32[]{:S(2)}) collective-permute-start(bf16[48,2048]{1,0:T(8,128)(2,1)S(1)} %collective-permute-done.48.refs_2_), channel_id=1, source_target_pairs={{0,1},{1,0},{16,17},{17,16},{2,3},{3,2},{18,19},{19,18},{4,5},{5,4... | collective-permute-start | bytes 589832 | tf_op jit(solution)/shard_map/ppermute | solution.py:52
  198.0 19.4 %collective-permute-start.54 = (bf16[48,2048]{1,0:T(8,128)(2,1)S(1)}, bf16[48,2048]{1,0:T(8,128)(2,1)S(1)}, u32[]{:S(2)}, u32[]{:S(2)}) collective-permute-start(bf16[48,2048]{1,0:T(8,128)(2,1)S(1)} %collective-permute-done.49.refs_3_), channel_id=1, source_target_pairs={{0,1},{1,0},{16,17},{17,16},{2,3},{3,2},{18,19},{19,18},{4,5},{5,4... | collective-permute-start | bytes 589832 | tf_op jit(solution)/shard_map/ppermute | solution.py:52
  201.7 31.6 %collective-permute-start.45 = (bf16[48,2048]{1,0:T(8,128)(2,1)S(1)}, bf16[48,2048]{1,0:T(8,128)(2,1)S(1)}, u32[]{:S(2)}, u32[]{:S(2)}) collective-permute-start(bf16[48,2048]{1,0:T(8,128)(2,1)S(1)} %get-tuple-element.152), channel_id=1, source_target_pairs={{0,12},{2,14},{4,8},{6,10},{8,4},{10,6},{12,0},{14,2},{16,28},{18,... | collective-permute-start | bytes 589832 | tf_op jit(solution)/shard_map/ppermute | solution.py:60
  205.9 28.0 %collective-permute-start.66 = (bf16[48,2048]{1,0:T(8,128)(2,1)S(1)}, bf16[48,2048]{1,0:T(8,128)(2,1)S(1)}, u32[]{:S(2)}, u32[]{:S(2)}) collective-permute-start(bf16[48,2048]{1,0:T(8,128)(2,1)S(1)} %get-tuple-element.178), channel_id=1, source_target_pairs={{0,14},{2,12},{4,10},{6,8},{8,6},{10,4},{12,2},{14,0},{16,30},{18,... | collective-permute-start | bytes 589832 | tf_op jit(solution)/shard_map/ppermute | solution.py:60
  233.9 14.2 %collective-permute-start.67 = (bf16[48,2048]{1,0:T(8,128)(2,1)S(1)}, bf16[48,2048]{1,0:T(8,128)(2,1)S(1)}, u32[]{:S(2)}, u32[]{:S(2)}) collective-permute-start(bf16[48,2048]{1,0:T(8,128)(2,1)S(1)} %collective-permute-done.66.refs_1_), channel_id=1, source_target_pairs={{0,1},{1,0},{16,17},{17,16},{2,3},{3,2},{18,19},{19,18},{4,5},{5,4... | collective-permute-start | bytes 589832 | tf_op jit(solution)/shard_map/ppermute | solution.py:52
  235.3 22.6 %collective-permute-start.57 = (bf16[48,2048]{1,0:T(8,128)(2,1)S(1)}, bf16[48,2048]{1,0:T(8,128)(2,1)S(1)}, u32[]{:S(2)}, u32[]{:S(2)}) collective-permute-start(bf16[48,2048]{1,0:T(8,128)(2,1)S(1)} %get-tuple-element.164), channel_id=1, source_target_pairs={{0,1},{1,0},{16,17},{17,16},{2,3},{3,2},{18,19},{19,18},{4,5},{5,4... | collective-permute-start | bytes 589832 | tf_op jit(solution)/shard_map/ppermute | solution.py:52
  239.8 20.3 %collective-permute-start.71 = (bf16[48,2048]{1,0:T(8,128)(2,1)S(1)}, bf16[48,2048]{1,0:T(8,128)(2,1)S(1)}, u32[]{:S(2)}, u32[]{:S(2)}) collective-permute-start(bf16[48,2048]{1,0:T(8,128)(2,1)S(1)} %add.113), channel_id=1, source_target_pairs={{0,10},{2,8},{4,14},{6,12},{8,2},{10,0},{12,6},{14,4},{16,26},{18,... | collective-permute-start | bytes 589832 | tf_op jit(solution)/shard_map/ppermute | solution.py:60
  258.8 14.0 %collective-permute-start.64 = (bf16[48,2048]{1,0:T(8,128)(2,1)S(1)}, bf16[48,2048]{1,0:T(8,128)(2,1)S(1)}, u32[]{:S(2)}, u32[]{:S(2)}) collective-permute-start(bf16[48,2048]{1,0:T(8,128)(2,1)S(1)} %get-tuple-element.177), channel_id=1, source_target_pairs={{0,1},{1,0},{16,17},{17,16},{2,3},{3,2},{18,19},{19,18},{4,5},{5,4... | collective-permute-start | bytes 589832 | tf_op jit(solution)/shard_map/ppermute | solution.py:52
  260.1 48.0 %collective-permute-start.35 = (bf16[128,2048]{1,0:T(8,128)(2,1)}, bf16[128,2048]{1,0:T(8,128)(2,1)S(1)}, u32[]{:S(2)}, u32[]{:S(2)}) collective-permute-start(bf16[128,2048]{1,0:T(8,128)(2,1)} %get-tuple-element.146), channel_id=1, source_target_pairs={{0,1},{1,0},{16,17},{17,16},{2,3},{3,2},{18,19},{19,18},{4,5},{5,4... | collective-permute-start | bytes 1572872 | tf_op jit(solution)/shard_map/ppermute | solution.py:52
  264.4 23.9 %collective-permute-start.62 = (bf16[48,2048]{1,0:T(8,128)(2,1)S(1)}, bf16[48,2048]{1,0:T(8,128)(2,1)S(1)}, u32[]{:S(2)}, u32[]{:S(2)}) collective-permute-start(bf16[48,2048]{1,0:T(8,128)(2,1)S(1)} %get-tuple-element.173), channel_id=1, source_target_pairs={{0,1},{1,0},{16,17},{17,16},{2,3},{3,2},{18,19},{19,18},{4,5},{5,4... | collective-permute-start | bytes 589832 | tf_op jit(solution)/shard_map/ppermute | solution.py:52
  265.9 25.8 %collective-permute-start.60 = (bf16[48,2048]{1,0:T(8,128)(2,1)S(1)}, bf16[48,2048]{1,0:T(8,128)(2,1)S(1)}, u32[]{:S(2)}, u32[]{:S(2)}) collective-permute-start(bf16[48,2048]{1,0:T(8,128)(2,1)S(1)} %get-tuple-element.169), channel_id=1, source_target_pairs={{0,1},{1,0},{16,17},{17,16},{2,3},{3,2},{18,19},{19,18},{4,5},{5,4... | collective-permute-start | bytes 589832 | tf_op jit(solution)/shard_map/ppermute | solution.py:52
  268.6 26.2 %collective-permute-start.58 = (bf16[48,2048]{1,0:T(8,128)(2,1)S(1)}, bf16[48,2048]{1,0:T(8,128)(2,1)}, u32[]{:S(2)}, u32[]{:S(2)}) collective-permute-start(bf16[48,2048]{1,0:T(8,128)(2,1)S(1)} %get-tuple-element.165), channel_id=1, source_target_pairs={{0,1},{1,0},{16,17},{17,16},{2,3},{3,2},{18,19},{19,18},{4,5},{5,4... | collective-permute-start | bytes 589832 | tf_op jit(solution)/shard_map/ppermute | solution.py:52
  272.8 23.9 %collective-permute-start.73 = (bf16[48,2048]{1,0:T(8,128)(2,1)S(1)}, bf16[48,2048]{1,0:T(8,128)(2,1)S(1)}, u32[]{:S(2)}, u32[]{:S(2)}) collective-permute-start(bf16[48,2048]{1,0:T(8,128)(2,1)S(1)} %add.112), channel_id=1, source_target_pairs={{0,14},{2,12},{4,10},{6,8},{8,6},{10,4},{12,2},{14,0},{16,30},{18,... | collective-permute-start | bytes 589832 | tf_op jit(solution)/shard_map/ppermute | solution.py:60
  (59 other events, 1132.6 us)

commit v2 on v1

--- a/solution.py
+++ b/solution.py
@@ -13,6 +13,7 @@
 F32 = jnp.float32
 BF16 = jnp.bfloat16
 MIB = 1024 * 1024
+IN_FLIGHT = 4
 
 
 def params(mib):
@@ -188,11 +189,11 @@
     return residual, stats, blocks
 
 
-def expert_kernel(blocks, width, scalar_ref, *refs):
+def expert_kernel(blocks, groups, width, scalar_ref, *refs):
     own_refs, far_refs, refs = refs[:blocks], refs[blocks : 2 * blocks], refs[2 * blocks :]
     up_ref, down_ref, gain_ref, *refs = refs
-    away_refs, kept_refs = refs[:blocks], refs[blocks : 2 * blocks]
-    rows_ref, sum_ref, inner_ref, up_held, down_held, up_sems, down_sems = refs[2 * blocks :]
+    away_refs, kept_refs = refs[:groups], refs[groups : 2 * groups]
+    rows_ref, sum_ref, inner_ref, up_held, down_held, up_sems, down_sems = refs[2 * groups :]
     slots, half = rows_ref.shape[1:]
     hidden = down_ref.shape[0]
     plane = scalar_ref[0]
@@ -217,8 +218,14 @@
         )
         for index in range(hidden // down_depth)
     ]
-    for copy in copies + down_copies:
+    order = copies + down_copies
+    for copy in order[:IN_FLIGHT]:
         copy.start()
+
+    def landed(index):
+        order[index].wait()
+        if index + IN_FLIGHT < len(order):
+            order[index + IN_FLIGHT].start()
 
     scales = []
     start = 0
@@ -235,8 +242,8 @@
     scale = jnp.concatenate(scales, axis=0)
 
     columns = min(512, hidden)
-    for index, copy in enumerate(copies):
-        copy.wait()
+    for index in range(len(copies)):
+        landed(index)
         lanes = slice(index % parts * depth, (index % parts + 1) * depth)
 
         @pl.loop(0, 2 * hidden // columns)
@@ -248,8 +255,8 @@
     gate = sum_ref[:, :hidden] * scale
     value = sum_ref[:, hidden:] * scale
     inner_ref[...] = (gate / (1.0 + jnp.exp(-gate)) * value).astype(BF16)
-    for copy in down_copies:
-        copy.wait()
+    for index in range(len(copies), len(order)):
+        landed(index)
     columns = min(512, half)
     for target_refs, side in ((away_refs, sides[1]), (kept_refs, sides[0])):
 
@@ -268,18 +275,19 @@
                 start += ref.shape[0]
 
 
-def expert_rows(scalars, own, far, up, down, gain):
+def expert_rows(scalars, own, far, sizes, up, down, gain):
     blocks = len(own)
     slots = sum(array.shape[0] for array in own)
     half = own[0].shape[1]
     hidden, width = down.shape
+    groups = [jax.ShapeDtypeStruct((size * own[0].shape[0], half), BF16) for size in sizes]
     depth, down_depth = min(1024, half), min(256, hidden)
     anywhere = pl.BlockSpec(memory_space=pl.ANY)
     outs = pl.pallas_call(
-        functools.partial(expert_kernel, blocks, width),
-        out_shape=[jax.ShapeDtypeStruct(array.shape, BF16) for array in (*own, *own)],
+        functools.partial(expert_kernel, blocks, len(groups), width),
+        out_shape=groups + groups,
         in_specs=[smem()] + [vmem()] * (2 * blocks) + [anywhere, anywhere, vmem()],
-        out_specs=[vmem()] * (2 * blocks),
+        out_specs=[vmem()] * (2 * len(groups)),
         scratch_shapes=[
             pltpu.VMEM((2, slots, half), BF16),
             pltpu.VMEM((slots, 2 * hidden), F32),
@@ -293,7 +301,7 @@
         cost_estimate=cost(),
         name="expert_rows",
     )(scalars, *own, *far, up, down, gain)
-    return list(outs[:blocks]), list(outs[blocks:])
+    return outs[: len(groups)], outs[len(groups) :]
 
 
 def combine_kernel(expert_count, width, *refs):
@@ -405,36 +413,34 @@
     near = range(count // 2)
     far, farther = range(count // 2, 3 * count // 4), range(3 * count // 4, count)
 
-    def exchange(blocks):
+    def dispatch(blocks, *sooner):
         got = list(blocks)
         for k in [*far, *near]:
             got[k] = across(blocks[k], k, both)
-        for k, sooner in zip(farther, far):
-            block, got[sooner] = lax.optimization_barrier((blocks[k], got[sooner]))
+        first = [to_other_plane(got[k], both) for k in (0, 1)]
+        held, first, sooner = lax.optimization_barrier(([got[k] for k in far], first, sooner))
+        for k, block in zip(far, held):
+            got[k] = block
+        for k, earlier in zip(farther, far):
+            block, got[earlier] = lax.optimization_barrier((blocks[k], got[earlier]))
             got[k] = across(block, k, both)
+        return got, first + [to_other_plane(block, both) for block in got[2:]], sooner
+
+    def answer(own, other):
+        parts = (near, far, farther)
+        sizes = [len(part) for part in parts]
+        away, kept = expert_rows(scalars, own, other, sizes, up_weight, down_weight, ffn_gain)
+        received = [None, to_other_plane(away[1], both), to_other_plane(away[2], both)]
+        rows, received[1] = lax.optimization_barrier((away[0], received[1]))
+        received[0] = to_other_plane(rows, both)
+        got = [None] * count
+        for index in (1, 2, 0):
+            for place, k in enumerate(parts[index]):
+                at = slice(place * capacity, (place + 1) * capacity)
+                got[k] = across(kept[index][at] + received[index][at], k, both)
         return got
 
-    def experts(own):
-        other = [to_other_plane(block, both) for block in own]
-        away, kept = [], []
-        for group in ([*near, *far], farther):
-            mine, theirs = [own[k] for k in group], [other[k] for k in group]
-            if kept:
-                theirs[0], kept[0] = lax.optimization_barrier((theirs[0], kept[0]))
-            made = expert_rows(scalars, mine, theirs, up_weight, down_weight, ffn_gain)
-            away += made[0]
-            kept += made[1]
-        received = [None] * count
-        for k in [*far, *farther]:
-            received[k] = to_other_plane(away[k], both)
-        for k in near:
-            later = far[k % len(far)]
-            block, received[later] = lax.optimization_barrier((away[k], received[later]))
-            received[k] = to_other_plane(block, both)
-        return [k + r for k, r in zip(kept, received)]
-
-    def whole_rows(made):
-        other = to_other_plane(made, both)
+    def whole_rows(made, other):
         low, high = jnp.where(plane == 0, made, other), jnp.where(plane == 0, other, made)
         return jnp.concatenate([low, high], axis=1)
 
@@ -446,29 +452,38 @@
         gains, router_rows, send_place[0],
     )
     stats_other = to_other_plane(stats, both)
-    returned = exchange(experts(exchange(rows)))
-    made, squares = combine(
-        count, width, returned, residual, stats, stats_other, combine_place[0]
-    )
-
+    own, other, _ = dispatch(rows)
+    own[0], fresh_rows, doc_fresh = lax.optimization_barrier((own[0], fresh_rows, doc_fresh))
     fresh = half_of(fresh_rows[0])
     fresh_prior = to_next_block(fresh, (0,))
     fresh_meta = meta_of(fresh_rows[0], doc_fresh[0])
     fresh_prior_meta = to_next_block(fresh_meta, (0,))
+    returned = answer(own, other)
+    last = count - 1
+    returned[last], fresh_prior, fresh_prior_meta = lax.optimization_barrier(
+        (returned[last], fresh_prior, fresh_prior_meta)
+    )
+    made, squares = combine(
+        count, width, returned, residual, stats, stats_other, combine_place[0]
+    )
+
     sent_prior, sent = to_next_phase(made, 1, False), to_next_phase(made, 0, False)
     scales = [to_next_phase(squares, step, swap) for step in (0, 1) for swap in (False, True)]
-    results = [whole_rows(made)]
+    other = to_other_plane(made, both)
+    sent, other = lax.optimization_barrier((sent, other))
+    results = [whole_rows(made, other)]
     residual, stats, rows = attend(
         True, width, count, scalars,
         [fresh, fresh_prior, fresh_meta, fresh_prior_meta, sent, sent_prior, *sent_ids, *scales],
         gains, router_rows, send_place[1],
     )
     stats_other = to_other_plane(stats, both)
-    returned = exchange(experts(exchange(rows)))
+    own, other, _ = dispatch(rows)
+    returned = answer(own, other)
     made, squares = combine(
         count, width, returned, residual, stats, stats_other, combine_place[1]
     )
-    results.append(whole_rows(made))
+    results.append(whole_rows(made, to_other_plane(made, both)))
     return jnp.stack(results)[:, None]
 
 

time: 319 us -> 322 us (level)
  waiting for transfers between devices: 116 us -> 135 us
  Pallas kernels: 49.9 us -> 39.4 us
  local copies, waits for them, and re-layouts: 21.7 us -> 29.2 us
  other arithmetic: 15.6 us -> 8.49 us
  starting transfers between devices: 113 us -> 109 us
    ppermute x36 -> x26, starting transfers between devices: 41.3 us -> 22.2 us  [to_other_plane(): return lax.ppermute(array, ('section', 'dp'), pairs)]
    ppermute x28, waiting for transfers between devices: 28.6 us -> 44.4 us  [across(): return lax.ppermute(array, ('section', 'expert'), pairs)]
    ppermute x28, starting transfers between devices: 46.1 us -> 59.7 us  [across(): return lax.ppermute(array, ('section', 'expert'), pairs)]
    pallas_call x4 -> x2, Pallas kernels: 40.3 us -> 29.4 us  [expert_rows(): pl.pallas_call(functools.partial(expert_kernel, blocks, len(groups), widt...]
    ppermute x36 -> x26, waiting for transfers between devices: 81.9 us -> 89.2 us  [to_other_plane(): return lax.ppermute(array, ('section', 'dp'), pairs)]
    unnamed x63 -> x61, local copies, waits for them, and re-layouts: 18.7 us -> 25.7 us
    add x16 -> x6, other arithmetic: 8.73 us -> 3.95 us  [answer(): got[k] = across(kept[index][at] + received[index][at], k, both)]
    ppermute x4, waiting for transfers between devices: 3.72 us -> 0.01 us  [to_next_block(): return lax.ppermute(array, ('section', 'expert'), pairs)]
  transfers between devices with their start and end apart: 76 -> 66, of which waited for: 36 -> 32; matrix products, arithmetic and copies ran while one was open for 10% -> 7% of each run, Pallas kernels for 14% -> 0%
where the time goes in v2:
time: 322 us
  waiting for transfers between devices  135 us (42%)
  starting transfers between devices  109 us (34%)
  Pallas kernels  39.4 us (12%)
  local copies, waits for them, and re-layouts  29.2 us (9%)
  other arithmetic  8.49 us (3%)
    ppermute x26, waiting for transfers between devices, to_other_plane(): return lax.ppermute(array, ('section', 'dp'), pairs)  89.2 us
    ppermute x28, starting transfers between devices, across(): return lax.ppermute(array, ('section', 'expert'), pairs)  59.7 us
    ppermute x28, waiting for transfers between devices, across(): return lax.ppermute(array, ('section', 'expert'), pairs)  44.4 us
    pallas_call x2, Pallas kernels, expert_rows(): pl.pallas_call(functools.partial(expert_kernel, blocks, len(groups), widt...  29.4 us
    unnamed x61, local copies, waits for them, and re-layouts  25.7 us
    ppermute x26, starting transfers between devices, to_other_plane(): return lax.ppermute(array, ('section', 'dp'), pairs)  22.2 us
    ppermute x8, starting transfers between devices, to_next_phase(): return lax.ppermute(array, ('section', 'expert', 'dp'), pairs)  13.9 us
    ppermute x4, starting transfers between devices, to_next_block(): return lax.ppermute(array, ('section', 'expert'), pairs)  12.7 us
  transfers between devices with their start and end apart: 66, of which 32 were waited for; matrix products, arithmetic and copies ran while one was open for 7% of the time, Pallas kernels for 0%

profile of v2, /device:TPU:0, one launch (start us, length us, event | category | flops | bytes accessed | tf_op | source)
XLA Modules:
  0.0 321.6 jit_solution(5453316380171625001)
XLA Ops:
  0.7 2.3 collective-permute-start.1
  3.1 3.2 %collective-permute-start.2 = (f32[1,128]{1,0:T(1,128)S(1)}, f32[1,128]{1,0:T(1,128)S(1)}, u32[]{:S(2)}, u32[]{:S(2)}) collective-permute-start(f32[1,128]{1,0:T(1,128)S(1)} %add_convert_fusion.1), channel_id=1, source_target_pairs={{0,18},{1,19},{2,20},{3,21},{4,22},{5,23},{6,24},{7,25},{8,26},{9,... | collective-permute-start | bytes 1544 | tf_op jit(solution)/shard_map/ppermute | solution.py:48
  7.4 3.5 %collective-permute-start = (bf16[128,2048]{1,0:T(8,128)(2,1)S(1)}, bf16[128,2048]{1,0:T(8,128)(2,1)S(1)}, u32[]{:S(2)}, u32[]{:S(2)}) collective-permute-start(bf16[128,2048]{1,0:T(8,128)(2,1)S(1)} %dynamic-slice_bitcast_fusion.1.own_ref), channel_id=1, source_target_pairs={{0,2},{2,4},{4,6},{6,8},{8,10},{10,12},{12,14},{16,18},{18,20},{20... | collective-permute-start | bytes 1572872 | tf_op jit(solution)/shard_map/ppermute | solution.py:38
  12.4 3.4 %collective-permute-start.3 = (f32[2,128]{1,0:T(2,128)S(1)}, f32[2,128]{1,0:T(2,128)S(1)}, u32[]{:S(2)}, u32[]{:S(2)}) collective-permute-start(f32[2,128]{1,0:T(2,128)S(1)} %pad_maximum_fusion.refs_0_), channel_id=1, source_target_pairs={{0,2},{2,4},{4,6},{6,8},{8,10},{10,12},{12,14},{16,18},{18,20},{20... | collective-permute-start | bytes 3080 | tf_op jit(solution)/shard_map/ppermute | solution.py:38
  17.3 13.7 %copy.23 = bf16[512,8,2,768]{3,1,2,0:T(8,128)(2,1)} copy(bf16[512,8,2,768]{3,2,1,0:T(2,128)(2,1)} %bitcast.49) | data formatting | bytes 25165824
  31.1 2.8 attend.2
  38.6 2.9 collective-permute-start.8
  43.7 7.5 %collective-permute-done.5.refs_2_ = bf16[48,2048]{1,0:T(8,128)(2,1)S(1)} collective-permute-done((bf16[48,2048]{1,0:T(8,128)(2,1)S(1)}, bf16[48,2048]{1,0:T(8,128)(2,1)S(1)}, u32[]{:S(2)}, u32[]{:S(2)}) %collective-permute-start.5) | collective-permute-done | bytes 196640 | tf_op jit(solution)/shard_map/ppermute | solution.py:61
  51.7 3.7 %collective-permute-done.8.refs_5_ = bf16[48,2048]{1,0:T(8,128)(2,1)S(1)} collective-permute-done((bf16[48,2048]{1,0:T(8,128)(2,1)S(1)}, bf16[48,2048]{1,0:T(8,128)(2,1)S(1)}, u32[]{:S(2)}, u32[]{:S(2)}) %collective-permute-start.8) | collective-permute-done | bytes 196640 | tf_op jit(solution)/shard_map/ppermute | solution.py:61
  57.2 3.4 %collective-permute-start.11 = (bf16[48,2048]{1,0:T(8,128)(2,1)S(1)}, bf16[48,2048]{1,0:T(8,128)(2,1)S(1)}, u32[]{:S(2)}, u32[]{:S(2)}) collective-permute-start(bf16[48,2048]{1,0:T(8,128)(2,1)S(1)} %get-tuple-element.86), channel_id=1, source_target_pairs={{0,12},{2,14},{4,8},{6,10},{8,4},{10,6},{12,0},{14,2},{16,28},{18,... | collective-permute-start | bytes 589832 | tf_op jit(solution)/shard_map/ppermute | solution.py:61
  68.8 4.0 %collective-permute-done.16.refs_13_ = bf16[48,2048]{1,0:T(8,128)(2,1)S(1)} collective-permute-done((bf16[48,2048]{1,0:T(8,128)(2,1)S(1)}, bf16[48,2048]{1,0:T(8,128)(2,1)S(1)}, u32[]{:S(2)}, u32[]{:S(2)}) %collective-permute-start.16) | collective-permute-done | bytes 196640 | tf_op jit(solution)/shard_map/ppermute | solution.py:53
  79.1 14.7 %expert_rows.2 = (bf16[192,2048]{1,0:T(8,128)(2,1)S(1)}, bf16[96,2048]{1,0:T(8,128)(2,1)S(1)}, bf16[96,2048]{1,0:T(8,128)(2,1)S(1)}, bf16[192,2048]{1,0:T(8,128)...) custom-call(s32[2]{0:T(128)S(1)} %pad_add_fusion.scalar_ref, ...), custom_call_target="tpu_custom_call" | custom-call | flops 1 | bytes 1 | tf_op jit(solution)/shard_map/expert_rows/pallas_call | solution.py:286
  94.4 2.4 collective-permute-start.30
  96.9 3.5 %collective-permute-start.29 = (bf16[128,2048]{1,0:T(8,128)(2,1)S(1)}, bf16[128,2048]{1,0:T(8,128)(2,1)S(1)}, u32[]{:S(2)}, u32[]{:S(2)}) collective-permute-start(bf16[128,2048]{1,0:T(8,128)(2,1)S(1)} %dynamic-slice_bitcast_fusion.own_ref), channel_id=1, source_target_pairs={{0,2},{2,4},{4,6},{6,8},{8,10},{10,12},{12,14},{1,3},{3,5},{5,7},{... | collective-permute-start | bytes 1572872 | tf_op jit(solution)/shard_map/ppermute | solution.py:38
  102.5 3.4 %collective-permute-done.19 = bf16[96,2048]{1,0:T(8,128)(2,1)S(1)} collective-permute-done((bf16[96,2048]{1,0:T(8,128)(2,1)S(1)}, bf16[96,2048]{1,0:T(8,128)(2,1)S(1)}, u32[]{:S(2)}, u32[]{:S(2)}) %collective-permute-start.19) | collective-permute-done | bytes 393248 | tf_op jit(solution)/shard_map/ppermute | solution.py:53
  107.2 8.6 %collective-permute-done.26 = bf16[96,2048]{1,0:T(8,128)(2,1)S(1)} collective-permute-done((bf16[96,2048]{1,0:T(8,128)(2,1)S(1)}, bf16[96,2048]{1,0:T(8,128)(2,1)S(1)}, u32[]{:S(2)}, u32[]{:S(2)}) %collective-permute-start.26) | collective-permute-done | bytes 393248 | tf_op jit(solution)/shard_map/ppermute | solution.py:53
  116.5 8.7 %collective-permute-done.20 = bf16[192,2048]{1,0:T(8,128)(2,1)S(1)} collective-permute-done((bf16[192,2048]{1,0:T(8,128)(2,1)S(1)}, bf16[192,2048]{1,0:T(8,128)(2,1)S(1)}, u32[]{:S(2)}, u32[]{:S(2)}) %collective-permute-start.20) | collective-permute-done | bytes 786464 | tf_op jit(solution)/shard_map/ppermute | solution.py:53
  125.1 3.7 %collective-permute-start.28 = (bf16[48,2048]{1,0:T(8,128)(2,1)S(1)}, bf16[48,2048]{1,0:T(8,128)(2,1)S(1)}, u32[]{:S(2)}, u32[]{:S(2)}) collective-permute-start(bf16[48,2048]{1,0:T(8,128)(2,1)S(1)} %get-tuple-element.158), channel_id=1, source_target_pairs={{0,14},{2,12},{4,10},{6,8},{8,6},{10,4},{12,2},{14,0},{16,30},{18,... | collective-permute-start | bytes 589832 | tf_op jit(solution)/shard_map/ppermute | solution.py:61
  129.7 3.9 %collective-permute-start.25 = (bf16[48,2048]{1,0:T(8,128)(2,1)}, bf16[48,2048]{1,0:T(8,128)(2,1)S(1)}, u32[]{:S(2)}, u32[]{:S(2)}) collective-permute-start(bf16[48,2048]{1,0:T(8,128)(2,1)} %get-tuple-element.159), channel_id=1, source_target_pairs={{0,10},{2,8},{4,14},{6,12},{8,2},{10,0},{12,6},{14,4},{16,26},{18,... | collective-permute-start | bytes 589832 | tf_op jit(solution)/shard_map/ppermute | solution.py:61
  135.1 2.9 collective-permute-start.21
  138.1 6.8 %collective-permute-start.23 = (bf16[48,2048]{1,0:T(8,128)(2,1)}, bf16[48,2048]{1,0:T(8,128)(2,1)}, u32[]{:S(2)}, u32[]{:S(2)}) collective-permute-start(bf16[48,2048]{1,0:T(8,128)(2,1)} %get-tuple-element.145), channel_id=1, source_target_pairs={{0,6},{2,4},{4,2},{6,0},{8,14},{10,12},{12,10},{14,8},{16,22},{18,... | collective-permute-start | bytes 589832 | tf_op jit(solution)/shard_map/ppermute | solution.py:61
  146.6 4.0 %collective-permute-done.25.refs_5_ = bf16[48,2048]{1,0:T(8,128)(2,1)S(1)} collective-permute-done((bf16[48,2048]{1,0:T(8,128)(2,1)}, bf16[48,2048]{1,0:T(8,128)(2,1)S(1)}, u32[]{:S(2)}, u32[]{:S(2)}) %collective-permute-start.25) | collective-permute-done | bytes 196640 | tf_op jit(solution)/shard_map/ppermute | solution.py:61
  158.1 2.4 combine.2
  167.9 5.8 %collective-permute-done.33 = bf16[128,2048]{1,0:T(8,128)(2,1)S(1)} collective-permute-done((bf16[128,2048]{1,0:T(8,128)(2,1)S(1)}, bf16[128,2048]{1,0:T(8,128)(2,1)S(1)}, u32[]{:S(2)}, u32[]{:S(2)}) %collective-permute-start.33) | collective-permute-done | bytes 524320 | tf_op jit(solution)/shard_map/ppermute | solution.py:53
  177.5 3.0 attend.3
  184.9 2.9 collective-permute-start.40
  189.9 9.8 %collective-permute-done.42.refs_4_ = bf16[48,2048]{1,0:T(8,128)(2,1)S(1)} collective-permute-done((bf16[48,2048]{1,0:T(8,128)(2,1)S(1)}, bf16[48,2048]{1,0:T(8,128)(2,1)S(1)}, u32[]{:S(2)}, u32[]{:S(2)}) %collective-permute-start.42) | collective-permute-done | bytes 196640 | tf_op jit(solution)/shard_map/ppermute | solution.py:61
  199.6 2.3 collective-permute-done.43.refs_5_
  202.0 4.1 %collective-permute-start.47 = (bf16[48,2048]{1,0:T(8,128)(2,1)S(1)}, bf16[48,2048]{1,0:T(8,128)(2,1)S(1)}, u32[]{:S(2)}, u32[]{:S(2)}) collective-permute-start(bf16[48,2048]{1,0:T(8,128)(2,1)S(1)} %get-tuple-element.125), channel_id=1, source_target_pairs={{0,14},{2,12},{4,10},{6,8},{8,6},{10,4},{12,2},{14,0},{16,30},{18,... | collective-permute-start | bytes 589832 | tf_op jit(solution)/shard_map/ppermute | solution.py:61
  206.1 2.4 collective-permute-start.46
  213.8 3.6 %collective-permute-done.46.refs_6_ = bf16[48,2048]{1,0:T(8,128)(2,1)S(1)} collective-permute-done((bf16[48,2048]{1,0:T(8,128)(2,1)S(1)}, bf16[48,2048]{1,0:T(8,128)(2,1)S(1)}, u32[]{:S(2)}, u32[]{:S(2)}) %collective-permute-start.46) | collective-permute-done | bytes 196640 | tf_op jit(solution)/shard_map/ppermute | solution.py:61
  218.1 2.5 collective-permute-done.51.refs_13_
  220.6 4.2 %collective-permute-done.50.refs_12_ = bf16[48,2048]{1,0:T(8,128)(2,1)S(1)} collective-permute-done((bf16[48,2048]{1,0:T(8,128)(2,1)S(1)}, bf16[48,2048]{1,0:T(8,128)(2,1)S(1)}, u32[]{:S(2)}, u32[]{:S(2)}) %collective-permute-start.50) | collective-permute-done | bytes 196640 | tf_op jit(solution)/shard_map/ppermute | solution.py:53
  224.8 4.2 %collective-permute-done.53.refs_15_ = bf16[48,2048]{1,0:T(8,128)(2,1)S(1)} collective-permute-done((bf16[48,2048]{1,0:T(8,128)(2,1)S(1)}, bf16[48,2048]{1,0:T(8,128)(2,1)S(1)}, u32[]{:S(2)}, u32[]{:S(2)}) %collective-permute-start.53) | collective-permute-done | bytes 196640 | tf_op jit(solution)/shard_map/ppermute | solution.py:53
  229.0 2.5 collective-permute-done.52.refs_14_
  231.4 2.8 copy-done.2
  234.2 14.7 %expert_rows.3 = (bf16[192,2048]{1,0:T(8,128)(2,1)S(1)}, bf16[96,2048]{1,0:T(8,128)(2,1)S(1)}, bf16[96,2048]{1,0:T(8,128)(2,1)S(1)}, bf16[192,2048]{1,0:T(8,128)...) custom-call(s32[2]{0:T(128)S(1)} %pad_add_fusion.scalar_ref, ...), custom_call_target="tpu_custom_call" | custom-call | flops 1 | bytes 1 | tf_op jit(solution)/shard_map/expert_rows/pallas_call | solution.py:286
  252.4 8.7 %collective-permute-done.54 = bf16[96,2048]{1,0:T(8,128)(2,1)S(1)} collective-permute-done((bf16[96,2048]{1,0:T(8,128)(2,1)S(1)}, bf16[96,2048]{1,0:T(8,128)(2,1)S(1)}, u32[]{:S(2)}, u32[]{:S(2)}) %collective-permute-start.54) | collective-permute-done | bytes 393248 | tf_op jit(solution)/shard_map/ppermute | solution.py:53
  262.4 7.1 %collective-permute-done.61 = bf16[96,2048]{1,0:T(8,128)(2,1)S(1)} collective-permute-done((bf16[96,2048]{1,0:T(8,128)(2,1)S(1)}, bf16[96,2048]{1,0:T(8,128)(2,1)S(1)}, u32[]{:S(2)}, u32[]{:S(2)}) %collective-permute-start.61) | collective-permute-done | bytes 393248 | tf_op jit(solution)/shard_map/ppermute | solution.py:53
  269.5 2.2 collective-permute-start.62
  271.8 2.6 collective-permute-start.63
  275.2 10.4 %collective-permute-done.55 = bf16[192,2048]{1,0:T(8,128)(2,1)S(1)} collective-permute-done((bf16[192,2048]{1,0:T(8,128)(2,1)S(1)}, bf16[192,2048]{1,0:T(8,128)(2,1)S(1)}, u32[]{:S(2)}, u32[]{:S(2)}) %collective-permute-start.55) | collective-permute-done | bytes 786464 | tf_op jit(solution)/shard_map/ppermute | solution.py:53
  288.3 2.6 collective-permute-start.57
  290.9 6.3 %collective-permute-start.58 = (bf16[48,2048]{1,0:T(8,128)(2,1)}, bf16[48,2048]{1,0:T(8,128)(2,1)S(1)}, u32[]{:S(2)}, u32[]{:S(2)}) collective-permute-start(bf16[48,2048]{1,0:T(8,128)(2,1)} %get-tuple-element.141), channel_id=1, source_target_pairs={{0,6},{2,4},{4,2},{6,0},{8,14},{10,12},{12,10},{14,8},{16,22},{18,... | collective-permute-start | bytes 589832 | tf_op jit(solution)/shard_map/ppermute | solution.py:61
  297.3 2.7 collective-permute-done.59.refs_4_
  299.9 2.8 collective-permute-done.60.refs_5_
  304.4 2.5 collective-permute-done.58.refs_3_
  308.9 11.1 %collective-permute-done.65 = bf16[128,2048]{1,0:T(8,128)(2,1)S(1)} collective-permute-done((bf16[128,2048]{1,0:T(8,128)(2,1)S(1)}, bf16[128,2048]{1,0:T(8,128)(2,1)S(1)}, u32[]{:S(2)}, u32[]{:S(2)}) %collective-permute-start.65) | collective-permute-done | bytes 524320 | tf_op jit(solution)/shard_map/ppermute | solution.py:53
  (187 shorter events, 82.1 us)
Async XLA Ops:
  0.7 30.3 %collective-permute-start.1 = (f32[1,128]{1,0:T(1,128)S(1)}, f32[1,128]{1,0:T(1,128)S(1)}, u32[]{:S(2)}, u32[]{:S(2)}) collective-permute-start(f32[1,128]{1,0:T(1,128)S(1)} %add_convert_fusion.1), channel_id=1, source_target_pairs={{0,16},{1,17},{2,18},{3,19},{4,20},{5,21},{6,22},{7,23},{8,24},{9,... | collective-permute-start | bytes 1544 | tf_op jit(solution)/shard_map/ppermute | solution.py:48
  3.1 28.0 %collective-permute-start.2 = (f32[1,128]{1,0:T(1,128)S(1)}, f32[1,128]{1,0:T(1,128)S(1)}, u32[]{:S(2)}, u32[]{:S(2)}) collective-permute-start(f32[1,128]{1,0:T(1,128)S(1)} %add_convert_fusion.1), channel_id=1, source_target_pairs={{0,18},{1,19},{2,20},{3,21},{4,22},{5,23},{6,24},{7,25},{8,26},{9,... | collective-permute-start | bytes 1544 | tf_op jit(solution)/shard_map/ppermute | solution.py:48
  7.4 23.7 %collective-permute-start = (bf16[128,2048]{1,0:T(8,128)(2,1)S(1)}, bf16[128,2048]{1,0:T(8,128)(2,1)S(1)}, u32[]{:S(2)}, u32[]{:S(2)}) collective-permute-start(bf16[128,2048]{1,0:T(8,128)(2,1)S(1)} %dynamic-slice_bitcast_fusion.1.own_ref), channel_id=1, source_target_pairs={{0,2},{2,4},{4,6},{6,8},{8,10},{10,12},{12,14},{16,18},{18,20},{20... | collective-permute-start | bytes 1572872 | tf_op jit(solution)/shard_map/ppermute | solution.py:38
  12.4 18.7 %collective-permute-start.3 = (f32[2,128]{1,0:T(2,128)S(1)}, f32[2,128]{1,0:T(2,128)S(1)}, u32[]{:S(2)}, u32[]{:S(2)}) collective-permute-start(f32[2,128]{1,0:T(2,128)S(1)} %pad_maximum_fusion.refs_0_), channel_id=1, source_target_pairs={{0,2},{2,4},{4,6},{6,8},{8,10},{10,12},{12,14},{16,18},{18,20},{20... | collective-permute-start | bytes 3080 | tf_op jit(solution)/shard_map/ppermute | solution.py:38
  37.1 14.7 %collective-permute-start.7 = (bf16[48,2048]{1,0:T(8,128)(2,1)S(1)}, bf16[48,2048]{1,0:T(8,128)(2,1)S(1)}, u32[]{:S(2)}, u32[]{:S(2)}) collective-permute-start(bf16[48,2048]{1,0:T(8,128)(2,1)S(1)} %get-tuple-element.79), channel_id=1, source_target_pairs={{0,8},{2,10},{4,12},{6,14},{8,0},{10,2},{12,4},{14,6},{16,24},{18,... | collective-permute-start | bytes 589832 | tf_op jit(solution)/shard_map/ppermute | solution.py:61
  38.2 13.0 %collective-permute-start.5 = (bf16[48,2048]{1,0:T(8,128)(2,1)S(1)}, bf16[48,2048]{1,0:T(8,128)(2,1)S(1)}, u32[]{:S(2)}, u32[]{:S(2)}) collective-permute-start(bf16[48,2048]{1,0:T(8,128)(2,1)S(1)} %get-tuple-element.76), channel_id=1, source_target_pairs={{0,4},{2,6},{4,0},{6,2},{8,12},{10,14},{12,8},{14,10},{16,20},{18,... | collective-permute-start | bytes 589832 | tf_op jit(solution)/shard_map/ppermute | solution.py:61
  38.6 16.9 %collective-permute-start.8 = (bf16[48,2048]{1,0:T(8,128)(2,1)S(1)}, bf16[48,2048]{1,0:T(8,128)(2,1)S(1)}, u32[]{:S(2)}, u32[]{:S(2)}) collective-permute-start(bf16[48,2048]{1,0:T(8,128)(2,1)S(1)} %get-tuple-element.80), channel_id=1, source_target_pairs={{0,10},{2,8},{4,14},{6,12},{8,2},{10,0},{12,6},{14,4},{16,26},{18,... | collective-permute-start | bytes 589832 | tf_op jit(solution)/shard_map/ppermute | solution.py:61
  41.5 14.0 %collective-permute-start.10 = (bf16[48,2048]{1,0:T(8,128)(2,1)S(1)}, bf16[48,2048]{1,0:T(8,128)(2,1)S(1)}, u32[]{:S(2)}, u32[]{:S(2)}) collective-permute-start(bf16[48,2048]{1,0:T(8,128)(2,1)S(1)} %collective-permute-done.4.refs_1_), channel_id=1, source_target_pairs={{0,1},{1,0},{16,17},{17,16},{2,3},{3,2},{18,19},{19,18},{4,5},{5,4... | collective-permute-start | bytes 589832 | tf_op jit(solution)/shard_map/ppermute | solution.py:53
  42.0 18.8 %collective-permute-start.6 = (bf16[48,2048]{1,0:T(8,128)(2,1)S(1)}, bf16[48,2048]{1,0:T(8,128)(2,1)S(1)}, u32[]{:S(2)}, u32[]{:S(2)}) collective-permute-start(bf16[48,2048]{1,0:T(8,128)(2,1)S(1)} %get-tuple-element.77), channel_id=1, source_target_pairs={{0,6},{2,4},{4,2},{6,0},{8,14},{10,12},{12,10},{14,8},{16,22},{18,... | collective-permute-start | bytes 589832 | tf_op jit(solution)/shard_map/ppermute | solution.py:61
  51.2 11.8 %collective-permute-start.13 = (bf16[48,2048]{1,0:T(8,128)(2,1)S(1)}, bf16[48,2048]{1,0:T(8,128)(2,1)S(1)}, u32[]{:S(2)}, u32[]{:S(2)}) collective-permute-start(bf16[48,2048]{1,0:T(8,128)(2,1)S(1)} %collective-permute-done.5.refs_2_), channel_id=1, source_target_pairs={{0,1},{1,0},{16,17},{17,16},{2,3},{3,2},{18,19},{19,18},{4,5},{5,4... | collective-permute-start | bytes 589832 | tf_op jit(solution)/shard_map/ppermute | solution.py:53
  63.0 11.9 %collective-permute-start.15 = (bf16[48,2048]{1,0:T(8,128)(2,1)S(1)}, bf16[48,2048]{1,0:T(8,128)(2,1)S(1)}, u32[]{:S(2)}, u32[]{:S(2)}) collective-permute-start(bf16[48,2048]{1,0:T(8,128)(2,1)S(1)} %collective-permute-done.7.refs_4_), channel_id=1, source_target_pairs={{0,1},{1,0},{16,17},{17,16},{2,3},{3,2},{18,19},{19,18},{4,5},{5,4... | collective-permute-start | bytes 589832 | tf_op jit(solution)/shard_map/ppermute | solution.py:53
  64.0 13.0 %collective-permute-start.18 = (bf16[48,2048]{1,0:T(8,128)(2,1)S(1)}, bf16[48,2048]{1,0:T(8,128)(2,1)S(1)}, u32[]{:S(2)}, u32[]{:S(2)}) collective-permute-start(bf16[48,2048]{1,0:T(8,128)(2,1)S(1)} %collective-permute-done.12.refs_7_), channel_id=1, source_target_pairs={{0,1},{1,0},{16,17},{17,16},{2,3},{3,2},{18,19},{19,18},{4,5},{5,4... | collective-permute-start | bytes 589832 | tf_op jit(solution)/shard_map/ppermute | solution.py:53
  66.4 12.7 %collective-permute-start.17 = (bf16[48,2048]{1,0:T(8,128)(2,1)S(1)}, bf16[48,2048]{1,0:T(8,128)(2,1)S(1)}, u32[]{:S(2)}, u32[]{:S(2)}) collective-permute-start(bf16[48,2048]{1,0:T(8,128)(2,1)S(1)} %collective-permute-done.11.refs_6_), channel_id=1, source_target_pairs={{0,1},{1,0},{16,17},{17,16},{2,3},{3,2},{18,19},{19,18},{4,5},{5,4... | collective-permute-start | bytes 589832 | tf_op jit(solution)/shard_map/ppermute | solution.py:53
  93.8 12.1 %collective-permute-start.19 = (bf16[96,2048]{1,0:T(8,128)(2,1)S(1)}, bf16[96,2048]{1,0:T(8,128)(2,1)S(1)}, u32[]{:S(2)}, u32[]{:S(2)}) collective-permute-start(bf16[96,2048]{1,0:T(8,128)(2,1)S(1)} %get-tuple-element.93), channel_id=1, source_target_pairs={{0,1},{1,0},{16,17},{17,16},{2,3},{3,2},{18,19},{19,18},{4,5},{5,4... | collective-permute-start | bytes 1179656 | tf_op jit(solution)/shard_map/ppermute | solution.py:53
  94.4 35.3 %collective-permute-start.30 = (f32[2,128]{1,0:T(2,128)S(1)}, f32[2,128]{1,0:T(2,128)S(1)}, u32[]{:S(2)}, u32[]{:S(2)}) collective-permute-start(f32[2,128]{1,0:T(2,128)S(1)} %pad_maximum_fusion.1.refs_0_), channel_id=1, source_target_pairs={{0,2},{2,4},{4,6},{6,8},{8,10},{10,12},{12,14},{1,3},{3,5},{5,7},{... | collective-permute-start | bytes 3080 | tf_op jit(solution)/shard_map/ppermute | solution.py:38
  96.9 37.4 %collective-permute-start.29 = (bf16[128,2048]{1,0:T(8,128)(2,1)S(1)}, bf16[128,2048]{1,0:T(8,128)(2,1)S(1)}, u32[]{:S(2)}, u32[]{:S(2)}) collective-permute-start(bf16[128,2048]{1,0:T(8,128)(2,1)S(1)} %dynamic-slice_bitcast_fusion.own_ref), channel_id=1, source_target_pairs={{0,2},{2,4},{4,6},{6,8},{8,10},{10,12},{12,14},{1,3},{3,5},{5,7},{... | collective-permute-start | bytes 1572872 | tf_op jit(solution)/shard_map/ppermute | solution.py:38
  100.4 33.3 %collective-permute-start.31 = (f32[128,128]{1,0:T(8,128)S(1)}, f32[128,128]{1,0:T(8,128)S(1)}, u32[]{:S(2)}, u32[]{:S(2)}) collective-permute-start(f32[128,128]{1,0:T(8,128)S(1)} %get-tuple-element.103.refs_9_), channel_id=1, source_target_pairs={{0,1},{1,0},{16,17},{17,16},{2,3},{3,2},{18,19},{19,18},{4,5},{5,4... | collective-permute-start | bytes 196616 | tf_op jit(solution)/shard_map/ppermute | solution.py:53
  101.9 13.8 %collective-permute-start.26 = (bf16[96,2048]{1,0:T(8,128)(2,1)S(1)}, bf16[96,2048]{1,0:T(8,128)(2,1)S(1)}, u32[]{:S(2)}, u32[]{:S(2)}) collective-permute-start(bf16[96,2048]{1,0:T(8,128)(2,1)S(1)} %get-tuple-element.98), channel_id=1, source_target_pairs={{0,1},{1,0},{16,17},{17,16},{2,3},{3,2},{18,19},{19,18},{4,5},{5,4... | collective-permute-start | bytes 1179656 | tf_op jit(solution)/shard_map/ppermute | solution.py:53
  105.9 19.2 %collective-permute-start.20 = (bf16[192,2048]{1,0:T(8,128)(2,1)S(1)}, bf16[192,2048]{1,0:T(8,128)(2,1)S(1)}, u32[]{:S(2)}, u32[]{:S(2)}) collective-permute-start(bf16[192,2048]{1,0:T(8,128)(2,1)S(1)} %get-tuple-element.94), channel_id=1, source_target_pairs={{0,1},{1,0},{16,17},{17,16},{2,3},{3,2},{18,19},{19,18},{4,5},{5,4... | collective-permute-start | bytes 2359304 | tf_op jit(solution)/shard_map/ppermute | solution.py:53
  115.7 22.3 %collective-permute-start.24 = (bf16[48,2048]{1,0:T(8,128)(2,1)S(1)}, bf16[48,2048]{1,0:T(8,128)(2,1)S(1)}, u32[]{:S(2)}, u32[]{:S(2)}) collective-permute-start(bf16[48,2048]{1,0:T(8,128)(2,1)S(1)} %get-tuple-element.160), channel_id=1, source_target_pairs={{0,8},{2,10},{4,12},{6,14},{8,0},{10,2},{12,4},{14,6},{16,24},{18,... | collective-permute-start | bytes 589832 | tf_op jit(solution)/shard_map/ppermute | solution.py:61
  125.1 12.9 %collective-permute-start.28 = (bf16[48,2048]{1,0:T(8,128)(2,1)S(1)}, bf16[48,2048]{1,0:T(8,128)(2,1)S(1)}, u32[]{:S(2)}, u32[]{:S(2)}) collective-permute-start(bf16[48,2048]{1,0:T(8,128)(2,1)S(1)} %get-tuple-element.158), channel_id=1, source_target_pairs={{0,14},{2,12},{4,10},{6,8},{8,6},{10,4},{12,2},{14,0},{16,30},{18,... | collective-permute-start | bytes 589832 | tf_op jit(solution)/shard_map/ppermute | solution.py:61
  129.7 20.9 %collective-permute-start.25 = (bf16[48,2048]{1,0:T(8,128)(2,1)}, bf16[48,2048]{1,0:T(8,128)(2,1)S(1)}, u32[]{:S(2)}, u32[]{:S(2)}) collective-permute-start(bf16[48,2048]{1,0:T(8,128)(2,1)} %get-tuple-element.159), channel_id=1, source_target_pairs={{0,10},{2,8},{4,14},{6,12},{8,2},{10,0},{12,6},{14,4},{16,26},{18,... | collective-permute-start | bytes 589832 | tf_op jit(solution)/shard_map/ppermute | solution.py:61
  134.3 17.0 %collective-permute-start.27 = (bf16[48,2048]{1,0:T(8,128)(2,1)}, bf16[48,2048]{1,0:T(8,128)(2,1)S(1)}, u32[]{:S(2)}, u32[]{:S(2)}) collective-permute-start(bf16[48,2048]{1,0:T(8,128)(2,1)} %get-tuple-element.157), channel_id=1, source_target_pairs={{0,12},{2,14},{4,8},{6,10},{8,4},{10,6},{12,0},{14,2},{16,28},{18,... | collective-permute-start | bytes 589832 | tf_op jit(solution)/shard_map/ppermute | solution.py:61
  135.1 16.9 %collective-permute-start.21 = (bf16[48,2048]{1,0:T(8,128)(2,1)}, bf16[48,2048]{1,0:T(8,128)(2,1)}, u32[]{:S(2)}, u32[]{:S(2)}) collective-permute-start(bf16[48,2048]{1,0:T(8,128)(2,1)} %get-tuple-element.147), channel_id=1, source_target_pairs={{0,2},{2,0},{4,6},{6,4},{8,10},{10,8},{12,14},{14,12},{16,18},{18,... | collective-permute-start | bytes 589832 | tf_op jit(solution)/shard_map/ppermute | solution.py:61
  138.0 13.9 %collective-permute-start.22 = (bf16[48,2048]{1,0:T(8,128)(2,1)}, bf16[48,2048]{1,0:T(8,128)(2,1)}, u32[]{:S(2)}, u32[]{:S(2)}) collective-permute-start(bf16[48,2048]{1,0:T(8,128)(2,1)} %get-tuple-element.146), channel_id=1, source_target_pairs={{0,4},{2,6},{4,0},{6,2},{8,12},{10,14},{12,8},{14,10},{16,20},{18,... | collective-permute-start | bytes 589832 | tf_op jit(solution)/shard_map/ppermute | solution.py:61
  138.1 14.7 %collective-permute-start.23 = (bf16[48,2048]{1,0:T(8,128)(2,1)}, bf16[48,2048]{1,0:T(8,128)(2,1)}, u32[]{:S(2)}, u32[]{:S(2)}) collective-permute-start(bf16[48,2048]{1,0:T(8,128)(2,1)} %get-tuple-element.145), channel_id=1, source_target_pairs={{0,6},{2,4},{4,2},{6,0},{8,14},{10,12},{12,10},{14,8},{16,22},{18,... | collective-permute-start | bytes 589832 | tf_op jit(solution)/shard_map/ppermute | solution.py:61
  162.1 11.6 %collective-permute-start.33 = (bf16[128,2048]{1,0:T(8,128)(2,1)S(1)}, bf16[128,2048]{1,0:T(8,128)(2,1)S(1)}, u32[]{:S(2)}, u32[]{:S(2)}) collective-permute-start(bf16[128,2048]{1,0:T(8,128)(2,1)S(1)} %get-tuple-element.104), channel_id=1, source_target_pairs={{0,1},{1,0},{16,17},{17,16},{2,3},{3,2},{18,19},{19,18},{4,5},{5,4... | collective-permute-start | bytes 1572872 | tf_op jit(solution)/shard_map/ppermute | solution.py:53
  162.7 14.0 %collective-permute-start.34 = (bf16[128,2048]{1,0:T(8,128)(2,1)S(1)}, bf16[128,2048]{1,0:T(8,128)(2,1)S(1)}, u32[]{:S(2)}, u32[]{:S(2)}) collective-permute-start(bf16[128,2048]{1,0:T(8,128)(2,1)S(1)} %get-tuple-element.104), channel_id=1, source_target_pairs={{0,18},{1,19},{2,20},{3,21},{4,22},{5,23},{6,24},{7,25},{8,26},{9,... | collective-permute-start | bytes 1572872 | tf_op jit(solution)/shard_map/ppermute | solution.py:48
  182.5 17.1 %collective-permute-start.42 = (bf16[48,2048]{1,0:T(8,128)(2,1)S(1)}, bf16[48,2048]{1,0:T(8,128)(2,1)S(1)}, u32[]{:S(2)}, u32[]{:S(2)}) collective-permute-start(bf16[48,2048]{1,0:T(8,128)(2,1)S(1)} %get-tuple-element.117), channel_id=1, source_target_pairs={{0,8},{2,10},{4,12},{6,14},{8,0},{10,2},{12,4},{14,6},{16,24},{18,... | collective-permute-start | bytes 589832 | tf_op jit(solution)/shard_map/ppermute | solution.py:61
  183.9 18.0 %collective-permute-start.43 = (bf16[48,2048]{1,0:T(8,128)(2,1)S(1)}, bf16[48,2048]{1,0:T(8,128)(2,1)S(1)}, u32[]{:S(2)}, u32[]{:S(2)}) collective-permute-start(bf16[48,2048]{1,0:T(8,128)(2,1)S(1)} %get-tuple-element.118), channel_id=1, source_target_pairs={{0,10},{2,8},{4,14},{6,12},{8,2},{10,0},{12,6},{14,4},{16,26},{18,... | collective-permute-start | bytes 589832 | tf_op jit(solution)/shard_map/ppermute | solution.py:61
  184.9 14.7 %collective-permute-start.40 = (bf16[48,2048]{1,0:T(8,128)(2,1)S(1)}, bf16[48,2048]{1,0:T(8,128)(2,1)S(1)}, u32[]{:S(2)}, u32[]{:S(2)}) collective-permute-start(bf16[48,2048]{1,0:T(8,128)(2,1)S(1)} %get-tuple-element.114), channel_id=1, source_target_pairs={{0,4},{2,6},{4,0},{6,2},{8,12},{10,14},{12,8},{14,10},{16,20},{18,... | collective-permute-start | bytes 589832 | tf_op jit(solution)/shard_map/ppermute | solution.py:61
  187.8 14.2 %collective-permute-start.44 = (bf16[48,2048]{1,0:T(8,128)(2,1)S(1)}, bf16[48,2048]{1,0:T(8,128)(2,1)S(1)}, u32[]{:S(2)}, u32[]{:S(2)}) collective-permute-start(bf16[48,2048]{1,0:T(8,128)(2,1)S(1)} %get-tuple-element.112.refs_0_), channel_id=1, source_target_pairs={{0,1},{1,0},{16,17},{17,16},{2,3},{3,2},{18,19},{19,18},{4,5},{5,4... | collective-permute-start | bytes 589832 | tf_op jit(solution)/shard_map/ppermute | solution.py:53
  189.3 12.7 %collective-permute-start.45 = (bf16[48,2048]{1,0:T(8,128)(2,1)S(1)}, bf16[48,2048]{1,0:T(8,128)(2,1)S(1)}, u32[]{:S(2)}, u32[]{:S(2)}) collective-permute-start(bf16[48,2048]{1,0:T(8,128)(2,1)S(1)} %collective-permute-done.39.refs_1_), channel_id=1, source_target_pairs={{0,1},{1,0},{16,17},{17,16},{2,3},{3,2},{18,19},{19,18},{4,5},{5,4... | collective-permute-start | bytes 589832 | tf_op jit(solution)/shard_map/ppermute | solution.py:53
  209.0 11.5 %collective-permute-start.51 = (bf16[48,2048]{1,0:T(8,128)(2,1)S(1)}, bf16[48,2048]{1,0:T(8,128)(2,1)S(1)}, u32[]{:S(2)}, u32[]{:S(2)}) collective-permute-start(bf16[48,2048]{1,0:T(8,128)(2,1)S(1)} %collective-permute-done.43.refs_5_), channel_id=1, source_target_pairs={{0,1},{1,0},{16,17},{17,16},{2,3},{3,2},{18,19},{19,18},{4,5},{5,4... | collective-permute-start | bytes 589832 | tf_op jit(solution)/shard_map/ppermute | solution.py:53
  210.5 14.2 %collective-permute-start.50 = (bf16[48,2048]{1,0:T(8,128)(2,1)S(1)}, bf16[48,2048]{1,0:T(8,128)(2,1)S(1)}, u32[]{:S(2)}, u32[]{:S(2)}) collective-permute-start(bf16[48,2048]{1,0:T(8,128)(2,1)S(1)} %collective-permute-done.42.refs_4_), channel_id=1, source_target_pairs={{0,1},{1,0},{16,17},{17,16},{2,3},{3,2},{18,19},{19,18},{4,5},{5,4... | collective-permute-start | bytes 589832 | tf_op jit(solution)/shard_map/ppermute | solution.py:53
  212.3 16.7 %collective-permute-start.53 = (bf16[48,2048]{1,0:T(8,128)(2,1)S(1)}, bf16[48,2048]{1,0:T(8,128)(2,1)S(1)}, u32[]{:S(2)}, u32[]{:S(2)}) collective-permute-start(bf16[48,2048]{1,0:T(8,128)(2,1)S(1)} %collective-permute-done.47.refs_7_), channel_id=1, source_target_pairs={{0,1},{1,0},{16,17},{17,16},{2,3},{3,2},{18,19},{19,18},{4,5},{5,4... | collective-permute-start | bytes 589832 | tf_op jit(solution)/shard_map/ppermute | solution.py:53
  217.4 14.0 %collective-permute-start.52 = (bf16[48,2048]{1,0:T(8,128)(2,1)S(1)}, bf16[48,2048]{1,0:T(8,128)(2,1)S(1)}, u32[]{:S(2)}, u32[]{:S(2)}) collective-permute-start(bf16[48,2048]{1,0:T(8,128)(2,1)S(1)} %collective-permute-done.46.refs_6_), channel_id=1, source_target_pairs={{0,1},{1,0},{16,17},{17,16},{2,3},{3,2},{18,19},{19,18},{4,5},{5,4... | collective-permute-start | bytes 589832 | tf_op jit(solution)/shard_map/ppermute | solution.py:53
  248.9 12.1 %collective-permute-start.54 = (bf16[96,2048]{1,0:T(8,128)(2,1)S(1)}, bf16[96,2048]{1,0:T(8,128)(2,1)S(1)}, u32[]{:S(2)}, u32[]{:S(2)}) collective-permute-start(bf16[96,2048]{1,0:T(8,128)(2,1)S(1)} %get-tuple-element.130), channel_id=1, source_target_pairs={{0,1},{1,0},{16,17},{17,16},{2,3},{3,2},{18,19},{19,18},{4,5},{5,4... | collective-permute-start | bytes 1179656 | tf_op jit(solution)/shard_map/ppermute | solution.py:53
  250.3 19.1 %collective-permute-start.61 = (bf16[96,2048]{1,0:T(8,128)(2,1)S(1)}, bf16[96,2048]{1,0:T(8,128)(2,1)S(1)}, u32[]{:S(2)}, u32[]{:S(2)}) collective-permute-start(bf16[96,2048]{1,0:T(8,128)(2,1)S(1)} %get-tuple-element.135), channel_id=1, source_target_pairs={{0,1},{1,0},{16,17},{17,16},{2,3},{3,2},{18,19},{19,18},{4,5},{5,4... | collective-permute-start | bytes 1179656 | tf_op jit(solution)/shard_map/ppermute | solution.py:53
  251.0 37.3 %collective-permute-start.64 = (f32[128,128]{1,0:T(8,128)S(1)}, f32[128,128]{1,0:T(8,128)S(1)}, u32[]{:S(2)}, u32[]{:S(2)}) collective-permute-start(f32[128,128]{1,0:T(8,128)S(1)} %get-tuple-element.137.refs_9_), channel_id=1, source_target_pairs={{0,1},{1,0},{16,17},{17,16},{2,3},{3,2},{18,19},{19,18},{4,5},{5,4... | collective-permute-start | bytes 196616 | tf_op jit(solution)/shard_map/ppermute | solution.py:53
  261.0 24.5 %collective-permute-start.55 = (bf16[192,2048]{1,0:T(8,128)(2,1)S(1)}, bf16[192,2048]{1,0:T(8,128)(2,1)S(1)}, u32[]{:S(2)}, u32[]{:S(2)}) collective-permute-start(bf16[192,2048]{1,0:T(8,128)(2,1)S(1)} %get-tuple-element.131), channel_id=1, source_target_pairs={{0,1},{1,0},{16,17},{17,16},{2,3},{3,2},{18,19},{19,18},{4,5},{5,4... | collective-permute-start | bytes 2359304 | tf_op jit(solution)/shard_map/ppermute | solution.py:53
  269.5 18.8 %collective-permute-start.62 = (bf16[48,2048]{1,0:T(8,128)(2,1)S(1)}, bf16[48,2048]{1,0:T(8,128)(2,1)S(1)}, u32[]{:S(2)}, u32[]{:S(2)}) collective-permute-start(bf16[48,2048]{1,0:T(8,128)(2,1)S(1)} %get-tuple-element.154), channel_id=1, source_target_pairs={{0,12},{2,14},{4,8},{6,10},{8,4},{10,6},{12,0},{14,2},{16,28},{18,... | collective-permute-start | bytes 589832 | tf_op jit(solution)/shard_map/ppermute | solution.py:61
  271.8 19.1 %collective-permute-start.63 = (bf16[48,2048]{1,0:T(8,128)(2,1)S(1)}, bf16[48,2048]{1,0:T(8,128)(2,1)S(1)}, u32[]{:S(2)}, u32[]{:S(2)}) collective-permute-start(bf16[48,2048]{1,0:T(8,128)(2,1)S(1)} %get-tuple-element.153), channel_id=1, source_target_pairs={{0,14},{2,12},{4,10},{6,8},{8,6},{10,4},{12,2},{14,0},{16,30},{18,... | collective-permute-start | bytes 589832 | tf_op jit(solution)/shard_map/ppermute | solution.py:61
  275.2 24.8 %collective-permute-start.59 = (bf16[48,2048]{1,0:T(8,128)(2,1)}, bf16[48,2048]{1,0:T(8,128)(2,1)S(1)}, u32[]{:S(2)}, u32[]{:S(2)}) collective-permute-start(bf16[48,2048]{1,0:T(8,128)(2,1)} %get-tuple-element.156), channel_id=1, source_target_pairs={{0,8},{2,10},{4,12},{6,14},{8,0},{10,2},{12,4},{14,6},{16,24},{18,... | collective-permute-start | bytes 589832 | tf_op jit(solution)/shard_map/ppermute | solution.py:61
  285.6 17.2 %collective-permute-start.60 = (bf16[48,2048]{1,0:T(8,128)(2,1)}, bf16[48,2048]{1,0:T(8,128)(2,1)S(1)}, u32[]{:S(2)}, u32[]{:S(2)}) collective-permute-start(bf16[48,2048]{1,0:T(8,128)(2,1)} %get-tuple-element.155), channel_id=1, source_target_pairs={{0,10},{2,8},{4,14},{6,12},{8,2},{10,0},{12,6},{14,4},{16,26},{18,... | collective-permute-start | bytes 589832 | tf_op jit(solution)/shard_map/ppermute | solution.py:61
  288.3 14.4 %collective-permute-start.56 = (bf16[48,2048]{1,0:T(8,128)(2,1)}, bf16[48,2048]{1,0:T(8,128)(2,1)S(1)}, u32[]{:S(2)}, u32[]{:S(2)}) collective-permute-start(bf16[48,2048]{1,0:T(8,128)(2,1)} %get-tuple-element.143), channel_id=1, source_target_pairs={{0,2},{2,0},{4,6},{6,4},{8,10},{10,8},{12,14},{14,12},{16,18},{18,... | collective-permute-start | bytes 589832 | tf_op jit(solution)/shard_map/ppermute | solution.py:61
  288.3 16.1 %collective-permute-start.57 = (bf16[48,2048]{1,0:T(8,128)(2,1)}, bf16[48,2048]{1,0:T(8,128)(2,1)S(1)}, u32[]{:S(2)}, u32[]{:S(2)}) collective-permute-start(bf16[48,2048]{1,0:T(8,128)(2,1)} %get-tuple-element.142), channel_id=1, source_target_pairs={{0,4},{2,6},{4,0},{6,2},{8,12},{10,14},{12,8},{14,10},{16,20},{18,... | collective-permute-start | bytes 589832 | tf_op jit(solution)/shard_map/ppermute | solution.py:61
  290.9 16.0 %collective-permute-start.58 = (bf16[48,2048]{1,0:T(8,128)(2,1)}, bf16[48,2048]{1,0:T(8,128)(2,1)S(1)}, u32[]{:S(2)}, u32[]{:S(2)}) collective-permute-start(bf16[48,2048]{1,0:T(8,128)(2,1)} %get-tuple-element.141), channel_id=1, source_target_pairs={{0,6},{2,4},{4,2},{6,0},{8,14},{10,12},{12,10},{14,8},{16,22},{18,... | collective-permute-start | bytes 589832 | tf_op jit(solution)/shard_map/ppermute | solution.py:61
  (48 other events, 636.9 us)

commit v3 on v1

--- a/solution.py
+++ b/solution.py
@@ -414,8 +414,12 @@
             got[k] = across(block, k, both)
         return got
 
-    def experts(own):
+    def experts(own, hurry):
         other = [to_other_plane(block, both) for block in own]
+        if hurry:
+            other[0], rest = lax.optimization_barrier((other[0], [own[k] for k in farther]))
+            for k, block in zip(farther, rest):
+                own[k] = block
         away, kept = [], []
         for group in ([*near, *far], farther):
             mine, theirs = [own[k] for k in group], [other[k] for k in group]
@@ -433,8 +437,7 @@
             received[k] = to_other_plane(block, both)
         return [k + r for k, r in zip(kept, received)]
 
-    def whole_rows(made):
-        other = to_other_plane(made, both)
+    def whole_rows(made, other):
         low, high = jnp.where(plane == 0, made, other), jnp.where(plane == 0, other, made)
         return jnp.concatenate([low, high], axis=1)
 
@@ -446,29 +449,39 @@
         gains, router_rows, send_place[0],
     )
     stats_other = to_other_plane(stats, both)
-    returned = exchange(experts(exchange(rows)))
-    made, squares = combine(
-        count, width, returned, residual, stats, stats_other, combine_place[0]
-    )
-
+    rows = exchange(rows)
+    entry = far[-1]
+    rows[entry], fresh_rows, doc_fresh = lax.optimization_barrier(
+        (rows[entry], fresh_rows, doc_fresh)
+    )
     fresh = half_of(fresh_rows[0])
     fresh_prior = to_next_block(fresh, (0,))
     fresh_meta = meta_of(fresh_rows[0], doc_fresh[0])
     fresh_prior_meta = to_next_block(fresh_meta, (0,))
+    rows[1], fresh_prior, fresh_prior_meta = lax.optimization_barrier(
+        (rows[1], fresh_prior, fresh_prior_meta)
+    )
+    returned = exchange(experts(rows, False))
+    made, squares = combine(
+        count, width, returned, residual, stats, stats_other, combine_place[0]
+    )
+
     sent_prior, sent = to_next_phase(made, 1, False), to_next_phase(made, 0, False)
     scales = [to_next_phase(squares, step, swap) for step in (0, 1) for swap in (False, True)]
-    results = [whole_rows(made)]
+    other = to_other_plane(made, both)
+    sent, other = lax.optimization_barrier((sent, other))
+    results = [whole_rows(made, other)]
     residual, stats, rows = attend(
         True, width, count, scalars,
         [fresh, fresh_prior, fresh_meta, fresh_prior_meta, sent, sent_prior, *sent_ids, *scales],
         gains, router_rows, send_place[1],
     )
     stats_other = to_other_plane(stats, both)
-    returned = exchange(experts(exchange(rows)))
+    returned = exchange(experts(exchange(rows), True))
     made, squares = combine(
         count, width, returned, residual, stats, stats_other, combine_place[1]
     )
-    results.append(whole_rows(made))
+    results.append(whole_rows(made, to_other_plane(made, both)))
     return jnp.stack(results)[:, None]
 
 

time: 319 us -> 308 us (0.966)
  waiting for transfers between devices: 116 us -> 102 us
  local copies, waits for them, and re-layouts: 21.7 us -> 26.3 us
    ppermute x36, waiting for transfers between devices: 81.9 us -> 46.2 us  [to_other_plane(): return lax.ppermute(array, ('section', 'dp'), pairs)]
    ppermute x28, waiting for transfers between devices: 28.6 us -> 52.5 us  [across(): return lax.ppermute(array, ('section', 'expert'), pairs)]
    unnamed x63 -> x89, local copies, waits for them, and re-layouts: 18.7 us -> 23.4 us
  transfers between devices with their start and end apart: 76 -> 76, of which waited for: 36 -> 35; matrix products, arithmetic and copies ran while one was open for 10% -> 10% of each run, Pallas kernels for 14% -> 9%
where the time goes in v3:
time: 308 us; the launch traced here: 307 us
  starting transfers between devices  113 us (37%)
  waiting for transfers between devices  102 us (33%)
  Pallas kernels  50.3 us (16%)
  local copies, waits for them, and re-layouts  26.3 us (9%)
  other arithmetic  14.1 us (5%)
    ppermute x28, waiting for transfers between devices, across(): return lax.ppermute(array, ('section', 'expert'), pairs)  52.5 us
    ppermute x28, starting transfers between devices, across(): return lax.ppermute(array, ('section', 'expert'), pairs)  47.1 us
    ppermute x36, waiting for transfers between devices, to_other_plane(): return lax.ppermute(array, ('section', 'dp'), pairs)  46.2 us
    pallas_call x4, Pallas kernels, expert_rows(): pl.pallas_call(functools.partial(expert_kernel, blocks, width), out_shape...  40.3 us
    ppermute x36, starting transfers between devices, to_other_plane(): return lax.ppermute(array, ('section', 'dp'), pairs)  39.7 us
    unnamed x89, local copies, waits for them, and re-layouts  23.4 us
    ppermute x8, starting transfers between devices, to_next_phase(): return lax.ppermute(array, ('section', 'expert', 'dp'), pairs)  13.6 us
    ppermute x4, starting transfers between devices, to_next_block(): return lax.ppermute(array, ('section', 'expert'), pairs)  12.6 us
  transfers between devices with their start and end apart: 76, of which 35 were waited for; matrix products, arithmetic and copies ran while one was open for 10% of the time, Pallas kernels for 9%

profile of v3, /device:TPU:0, one launch (start us, length us, event | category | flops | bytes accessed | tf_op | source)
XLA Modules:
  0.0 306.9 jit_solution(12832716092948967245)
XLA Ops:
  0.7 2.3 collective-permute-start.1
  3.1 3.2 %collective-permute-start.2 = (f32[1,128]{1,0:T(1,128)S(1)}, f32[1,128]{1,0:T(1,128)S(1)}, u32[]{:S(2)}, u32[]{:S(2)}) collective-permute-start(f32[1,128]{1,0:T(1,128)S(1)} %add_convert_fusion.1), channel_id=1, source_target_pairs={{0,18},{1,19},{2,20},{3,21},{4,22},{5,23},{6,24},{7,25},{8,26},{9,... | collective-permute-start | bytes 1544 | tf_op jit(solution)/shard_map/ppermute | solution.py:47
  7.4 3.5 %collective-permute-start = (bf16[128,2048]{1,0:T(8,128)(2,1)S(1)}, bf16[128,2048]{1,0:T(8,128)(2,1)S(1)}, u32[]{:S(2)}, u32[]{:S(2)}) collective-permute-start(bf16[128,2048]{1,0:T(8,128)(2,1)S(1)} %dynamic-slice_bitcast_fusion.1.own_ref), channel_id=1, source_target_pairs={{0,2},{2,4},{4,6},{6,8},{8,10},{10,12},{12,14},{16,18},{18,20},{20... | collective-permute-start | bytes 1572872 | tf_op jit(solution)/shard_map/ppermute | solution.py:37
  12.4 3.4 %collective-permute-start.3 = (f32[2,128]{1,0:T(2,128)S(1)}, f32[2,128]{1,0:T(2,128)S(1)}, u32[]{:S(2)}, u32[]{:S(2)}) collective-permute-start(f32[2,128]{1,0:T(2,128)S(1)} %pad_maximum_fusion.refs_0_), channel_id=1, source_target_pairs={{0,2},{2,4},{4,6},{6,8},{8,10},{10,12},{12,14},{16,18},{18,20},{20... | collective-permute-start | bytes 3080 | tf_op jit(solution)/shard_map/ppermute | solution.py:37
  16.7 14.1 %copy.23 = bf16[512,8,2,768]{3,1,2,0:T(8,128)(2,1)} copy(bf16[512,8,2,768]{3,2,1,0:T(2,128)(2,1)} %bitcast.57) | data formatting | bytes 25165824
  30.9 2.9 attend.2
  33.8 2.1 collective-permute-start.8
  35.9 2.0 collective-permute-start.7
  38.2 11.5 %collective-permute-done.8.refs_5_ = bf16[48,2048]{1,0:T(8,128)(2,1)S(1)} collective-permute-done((bf16[48,2048]{1,0:T(8,128)(2,1)S(1)}, bf16[48,2048]{1,0:T(8,128)(2,1)S(1)}, u32[]{:S(2)}, u32[]{:S(2)}) %collective-permute-start.8) | collective-permute-done | bytes 196640 | tf_op jit(solution)/shard_map/ppermute | solution.py:60
  50.1 3.7 %collective-permute-start.9 = (bf16[128,2048]{1,0:T(8,128)(2,1)S(1)}, bf16[128,2048]{1,0:T(8,128)(2,1)S(1)}, u32[]{:S(2)}, u32[]{:S(2)}) collective-permute-start(bf16[128,2048]{1,0:T(8,128)(2,1)S(1)} %dynamic-slice_bitcast_fusion.own_ref), channel_id=1, source_target_pairs={{0,2},{2,4},{4,6},{6,8},{8,10},{10,12},{12,14},{1,3},{3,5},{5,7},{... | collective-permute-start | bytes 1572872 | tf_op jit(solution)/shard_map/ppermute | solution.py:37
  54.7 2.1 collective-permute-start.10
  59.9 2.0 collective-permute-done.10.refs_1_
  61.9 2.0 collective-permute-start.18
  66.2 4.1 %collective-permute-start.5 = (bf16[48,2048]{1,0:T(8,128)(2,1)S(1)}, bf16[48,2048]{1,0:T(8,128)(2,1)S(1)}, u32[]{:S(2)}, u32[]{:S(2)}) collective-permute-start(bf16[48,2048]{1,0:T(8,128)(2,1)S(1)} %get-tuple-element.114), channel_id=1, source_target_pairs={{0,12},{2,14},{4,8},{6,10},{8,4},{10,6},{12,0},{14,2},{16,28},{18,... | collective-permute-start | bytes 589832 | tf_op jit(solution)/shard_map/ppermute | solution.py:60
  76.1 2.7 collective-permute-done.28.refs_1_
  78.7 2.0 collective-permute-start.29
  80.8 2.3 collective-permute-done.16.refs_9_
  83.1 2.1 collective-permute-done.14.refs_7_
  85.2 12.0 %expert_rows.4 = (bf16[48,2048]{1,0:T(8,128)(2,1)S(1)}, bf16[48,2048]{1,0:T(8,128)(2,1)S(1)}, bf16[48,2048]{1,0:T(8,128)(2,1)S(1)}, bf16[48,2048]{1,0:T(8,128)(2...) custom-call(s32[2]{0:T(128)S(1)} %pad_add_fusion.scalar_ref, ...), custom_call_target="tpu_custom_call" | custom-call | flops 1 | bytes 1 | tf_op jit(solution)/shard_map/expert_rows/pallas_call | solution.py:278
  99.4 8.2 %expert_rows.5 = (bf16[48,2048]{1,0:T(8,128)(2,1)S(1)}, bf16[48,2048]{1,0:T(8,128)(2,1)S(1)}, bf16[48,2048]{1,0:T(8,128)(2,1)S(1)}, bf16[48,2048]{1,0:T(8,128)(2,1)S(1)}) custom-call(s32[2]{0:T(128)S(1)} %pad_add_fusion.scalar_ref, bf16[48,2048]{1,0:T(8,128)(2,1)S(1)} %collective-permute-done.5.refs_0_, ...), custom_call_target="tpu_custom_call" | custom-call | flops 1 | bytes 1 | tf_op jit(solution)/shard_map/expert_rows/pallas_call | solution.py:278
  109.8 3.0 collective-permute-start.33
  117.1 2.7 collective-permute-done.30
  121.3 6.5 %collective-permute-done.33.refs_5_ = bf16[48,2048]{1,0:T(8,128)(2,1)S(1)} collective-permute-done((bf16[48,2048]{1,0:T(8,128)(2,1)S(1)}, bf16[48,2048]{1,0:T(8,128)(2,1)S(1)}, u32[]{:S(2)}, u32[]{:S(2)}) %collective-permute-start.33) | collective-permute-done | bytes 196640 | tf_op jit(solution)/shard_map/ppermute | solution.py:60
  132.9 2.4 collective-permute-start.35
  136.0 3.2 %collective-permute-start.34 = (bf16[48,2048]{1,0:T(8,128)(2,1)}, bf16[48,2048]{1,0:T(8,128)(2,1)}, u32[]{:S(2)}, u32[]{:S(2)}) collective-permute-start(bf16[48,2048]{1,0:T(8,128)(2,1)} %add.102), channel_id=1, source_target_pairs={{0,12},{2,14},{4,8},{6,10},{8,4},{10,6},{12,0},{14,2},{16,28},{18,... | collective-permute-start | bytes 589832 | tf_op jit(solution)/shard_map/ppermute | solution.py:60
  142.0 2.4 collective-permute-start.23
  150.2 2.5 combine.2
  160.2 3.0 collective-permute-done.38
  168.2 2.9 attend.3
  173.1 2.4 collective-permute-start.44
  177.4 12.4 %collective-permute-done.50.refs_5_ = bf16[48,2048]{1,0:T(8,128)(2,1)S(1)} collective-permute-done((bf16[48,2048]{1,0:T(8,128)(2,1)S(1)}, bf16[48,2048]{1,0:T(8,128)(2,1)S(1)}, u32[]{:S(2)}, u32[]{:S(2)}) %collective-permute-start.50) | collective-permute-done | bytes 196640 | tf_op jit(solution)/shard_map/ppermute | solution.py:60
  189.9 3.9 %collective-permute-done.44.refs_4_ = bf16[48,2048]{1,0:T(8,128)(2,1)S(1)} collective-permute-done((bf16[48,2048]{1,0:T(8,128)(2,1)S(1)}, bf16[48,2048]{1,0:T(8,128)(2,1)S(1)}, u32[]{:S(2)}, u32[]{:S(2)}) %collective-permute-start.44) | collective-permute-done | bytes 196640 | tf_op jit(solution)/shard_map/ppermute | solution.py:60
  199.2 5.2 %collective-permute-done.52.refs_1_ = bf16[48,2048]{1,0:T(8,128)(2,1)S(1)} collective-permute-done((bf16[48,2048]{1,0:T(8,128)(2,1)S(1)}, bf16[48,2048]{1,0:T(8,128)(2,1)S(1)}, u32[]{:S(2)}, u32[]{:S(2)}) %collective-permute-start.52) | collective-permute-done | bytes 196640 | tf_op jit(solution)/shard_map/ppermute | solution.py:60
  208.1 4.2 %collective-permute-done.53.refs_7_ = bf16[48,2048]{1,0:T(8,128)(2,1)S(1)} collective-permute-done((bf16[48,2048]{1,0:T(8,128)(2,1)S(1)}, bf16[48,2048]{1,0:T(8,128)(2,1)S(1)}, u32[]{:S(2)}, u32[]{:S(2)}) %collective-permute-start.53) | collective-permute-done | bytes 196640 | tf_op jit(solution)/shard_map/ppermute | solution.py:52
  212.3 4.2 %collective-permute-done.54.refs_8_ = bf16[48,2048]{1,0:T(8,128)(2,1)S(1)} collective-permute-done((bf16[48,2048]{1,0:T(8,128)(2,1)S(1)}, bf16[48,2048]{1,0:T(8,128)(2,1)S(1)}, u32[]{:S(2)}, u32[]{:S(2)}) %collective-permute-start.54) | collective-permute-done | bytes 196640 | tf_op jit(solution)/shard_map/ppermute | solution.py:52
  216.6 2.7 collective-permute-done.55.refs_9_
  219.2 2.8 copy-done.2
  222.0 11.7 %expert_rows.6 = (bf16[48,2048]{1,0:T(8,128)(2,1)S(1)}, bf16[48,2048]{1,0:T(8,128)(2,1)S(1)}, bf16[48,2048]{1,0:T(8,128)(2,1)S(1)}, bf16[48,2048]{1,0:T(8,128)(2...) custom-call(s32[2]{0:T(128)S(1)} %pad_add_fusion.scalar_ref, ...), custom_call_target="tpu_custom_call" | custom-call | flops 1 | bytes 1 | tf_op jit(solution)/shard_map/expert_rows/pallas_call | solution.py:278
  237.9 3.8 %collective-permute-done.60 = bf16[48,2048]{1,0:T(8,128)(2,1)S(1)} collective-permute-done((bf16[48,2048]{1,0:T(8,128)(2,1)S(1)}, bf16[48,2048]{1,0:T(8,128)(2,1)S(1)}, u32[]{:S(2)}, u32[]{:S(2)}) %collective-permute-start.60) | collective-permute-done | bytes 196640 | tf_op jit(solution)/shard_map/ppermute | solution.py:52
  241.7 2.2 collective-permute-start.71
  243.8 2.0 collective-permute-done.46.refs_2_
  245.8 3.8 %collective-permute-done.67.refs_3_ = bf16[48,2048]{1,0:T(8,128)(2,1)S(1)} collective-permute-done((bf16[48,2048]{1,0:T(8,128)(2,1)S(1)}, bf16[48,2048]{1,0:T(8,128)(2,1)S(1)}, u32[]{:S(2)}, u32[]{:S(2)}) %collective-permute-start.67) | collective-permute-done | bytes 196640 | tf_op jit(solution)/shard_map/ppermute | solution.py:52
  249.7 8.3 %expert_rows.7 = (bf16[48,2048]{1,0:T(8,128)(2,1)S(1)}, bf16[48,2048]{1,0:T(8,128)(2,1)S(1)}, bf16[48,2048]{1,0:T(8,128)(2,1)S(1)}, bf16[48,2048]{1,0:T(8,128)(2,1)S(1)}) custom-call(s32[2]{0:T(128)S(1)} %pad_add_fusion.scalar_ref, bf16[48,2048]{1,0:T(8,128)(2,1)S(1)} %collective-permute-done.45.refs_0_, ...), custom_call_target="tpu_custom_call" | custom-call | flops 1 | bytes 1 | tf_op jit(solution)/shard_map/expert_rows/pallas_call | solution.py:278
  274.3 3.6 %collective-permute-start.73 = (bf16[48,2048]{1,0:T(8,128)(2,1)}, bf16[48,2048]{1,0:T(8,128)(2,1)S(1)}, u32[]{:S(2)}, u32[]{:S(2)}) collective-permute-start(bf16[48,2048]{1,0:T(8,128)(2,1)} %add.112), channel_id=1, source_target_pairs={{0,14},{2,12},{4,10},{6,8},{8,6},{10,4},{12,2},{14,0},{16,30},{18,... | collective-permute-start | bytes 589832 | tf_op jit(solution)/shard_map/ppermute | solution.py:60
  278.6 3.8 %collective-permute-start.72 = (bf16[48,2048]{1,0:T(8,128)(2,1)}, bf16[48,2048]{1,0:T(8,128)(2,1)S(1)}, u32[]{:S(2)}, u32[]{:S(2)}) collective-permute-start(bf16[48,2048]{1,0:T(8,128)(2,1)} %add.110), channel_id=1, source_target_pairs={{0,12},{2,14},{4,8},{6,10},{8,4},{10,6},{12,0},{14,2},{16,28},{18,... | collective-permute-start | bytes 589832 | tf_op jit(solution)/shard_map/ppermute | solution.py:60
  284.1 2.9 collective-permute-start.64
  292.0 2.2 collective-permute-done.64.refs_2_
  297.3 8.0 %collective-permute-done.75 = bf16[128,2048]{1,0:T(8,128)(2,1)S(1)} collective-permute-done((bf16[128,2048]{1,0:T(8,128)(2,1)S(1)}, bf16[128,2048]{1,0:T(8,128)(2,1)S(1)}, u32[]{:S(2)}, u32[]{:S(2)}) %collective-permute-start.75) | collective-permute-done | bytes 524320 | tf_op jit(solution)/shard_map/ppermute | solution.py:52
  (249 shorter events, 99.3 us)
Async XLA Ops:
  0.7 30.1 %collective-permute-start.1 = (f32[1,128]{1,0:T(1,128)S(1)}, f32[1,128]{1,0:T(1,128)S(1)}, u32[]{:S(2)}, u32[]{:S(2)}) collective-permute-start(f32[1,128]{1,0:T(1,128)S(1)} %add_convert_fusion.1), channel_id=1, source_target_pairs={{0,16},{1,17},{2,18},{3,19},{4,20},{5,21},{6,22},{7,23},{8,24},{9,... | collective-permute-start | bytes 1544 | tf_op jit(solution)/shard_map/ppermute | solution.py:47
  3.1 27.8 %collective-permute-start.2 = (f32[1,128]{1,0:T(1,128)S(1)}, f32[1,128]{1,0:T(1,128)S(1)}, u32[]{:S(2)}, u32[]{:S(2)}) collective-permute-start(f32[1,128]{1,0:T(1,128)S(1)} %add_convert_fusion.1), channel_id=1, source_target_pairs={{0,18},{1,19},{2,20},{3,21},{4,22},{5,23},{6,24},{7,25},{8,26},{9,... | collective-permute-start | bytes 1544 | tf_op jit(solution)/shard_map/ppermute | solution.py:47
  7.4 23.4 %collective-permute-start = (bf16[128,2048]{1,0:T(8,128)(2,1)S(1)}, bf16[128,2048]{1,0:T(8,128)(2,1)S(1)}, u32[]{:S(2)}, u32[]{:S(2)}) collective-permute-start(bf16[128,2048]{1,0:T(8,128)(2,1)S(1)} %dynamic-slice_bitcast_fusion.1.own_ref), channel_id=1, source_target_pairs={{0,2},{2,4},{4,6},{6,8},{8,10},{10,12},{12,14},{16,18},{18,20},{20... | collective-permute-start | bytes 1572872 | tf_op jit(solution)/shard_map/ppermute | solution.py:37
  12.4 18.4 %collective-permute-start.3 = (f32[2,128]{1,0:T(2,128)S(1)}, f32[2,128]{1,0:T(2,128)S(1)}, u32[]{:S(2)}, u32[]{:S(2)}) collective-permute-start(f32[2,128]{1,0:T(2,128)S(1)} %pad_maximum_fusion.refs_0_), channel_id=1, source_target_pairs={{0,2},{2,4},{4,6},{6,8},{8,10},{10,12},{12,14},{16,18},{18,20},{20... | collective-permute-start | bytes 3080 | tf_op jit(solution)/shard_map/ppermute | solution.py:37
  33.8 16.0 %collective-permute-start.8 = (bf16[48,2048]{1,0:T(8,128)(2,1)S(1)}, bf16[48,2048]{1,0:T(8,128)(2,1)S(1)}, u32[]{:S(2)}, u32[]{:S(2)}) collective-permute-start(bf16[48,2048]{1,0:T(8,128)(2,1)S(1)} %get-tuple-element.118), channel_id=1, source_target_pairs={{0,10},{2,8},{4,14},{6,12},{8,2},{10,0},{12,6},{14,4},{16,26},{18,... | collective-permute-start | bytes 589832 | tf_op jit(solution)/shard_map/ppermute | solution.py:60
  35.9 22.6 %collective-permute-start.7 = (bf16[48,2048]{1,0:T(8,128)(2,1)S(1)}, bf16[48,2048]{1,0:T(8,128)(2,1)S(1)}, u32[]{:S(2)}, u32[]{:S(2)}) collective-permute-start(bf16[48,2048]{1,0:T(8,128)(2,1)S(1)} %get-tuple-element.116), channel_id=1, source_target_pairs={{0,2},{2,0},{4,6},{6,4},{8,10},{10,8},{12,14},{14,12},{16,18},{18,... | collective-permute-start | bytes 589832 | tf_op jit(solution)/shard_map/ppermute | solution.py:60
  37.9 19.0 %collective-permute-start.4 = (bf16[48,2048]{1,0:T(8,128)(2,1)S(1)}, bf16[48,2048]{1,0:T(8,128)(2,1)S(1)}, u32[]{:S(2)}, u32[]{:S(2)}) collective-permute-start(bf16[48,2048]{1,0:T(8,128)(2,1)S(1)} %get-tuple-element.113), channel_id=1, source_target_pairs={{0,8},{2,10},{4,12},{6,14},{8,0},{10,2},{12,4},{14,6},{16,24},{18,... | collective-permute-start | bytes 589832 | tf_op jit(solution)/shard_map/ppermute | solution.py:60
  50.1 13.8 %collective-permute-start.9 = (bf16[128,2048]{1,0:T(8,128)(2,1)S(1)}, bf16[128,2048]{1,0:T(8,128)(2,1)S(1)}, u32[]{:S(2)}, u32[]{:S(2)}) collective-permute-start(bf16[128,2048]{1,0:T(8,128)(2,1)S(1)} %dynamic-slice_bitcast_fusion.own_ref), channel_id=1, source_target_pairs={{0,2},{2,4},{4,6},{6,8},{8,10},{10,12},{12,14},{1,3},{3,5},{5,7},{... | collective-permute-start | bytes 1572872 | tf_op jit(solution)/shard_map/ppermute | solution.py:37
  56.9 13.3 %collective-permute-start.12 = (bf16[48,2048]{1,0:T(8,128)(2,1)S(1)}, bf16[48,2048]{1,0:T(8,128)(2,1)S(1)}, u32[]{:S(2)}, u32[]{:S(2)}) collective-permute-start(bf16[48,2048]{1,0:T(8,128)(2,1)S(1)} %get-tuple-element.124), channel_id=1, source_target_pairs={{0,6},{2,4},{4,2},{6,0},{8,14},{10,12},{12,10},{14,8},{16,22},{18,... | collective-permute-start | bytes 589832 | tf_op jit(solution)/shard_map/ppermute | solution.py:60
  58.5 13.3 %collective-permute-start.13 = (bf16[48,2048]{1,0:T(8,128)(2,1)S(1)}, bf16[48,2048]{1,0:T(8,128)(2,1)S(1)}, u32[]{:S(2)}, u32[]{:S(2)}) collective-permute-start(bf16[48,2048]{1,0:T(8,128)(2,1)S(1)} %get-tuple-element.115.refs_0_), channel_id=1, source_target_pairs={{0,1},{1,0},{16,17},{17,16},{2,3},{3,2},{18,19},{19,18},{4,5},{5,4... | collective-permute-start | bytes 589832 | tf_op jit(solution)/shard_map/ppermute | solution.py:52
  61.9 11.7 %collective-permute-start.18 = (bf16[48,2048]{1,0:T(8,128)(2,1)S(1)}, bf16[48,2048]{1,0:T(8,128)(2,1)S(1)}, u32[]{:S(2)}, u32[]{:S(2)}) collective-permute-start(bf16[48,2048]{1,0:T(8,128)(2,1)S(1)} %collective-permute-done.8.refs_5_), channel_id=1, source_target_pairs={{0,1},{1,0},{16,17},{17,16},{2,3},{3,2},{18,19},{19,18},{4,5},{5,4... | collective-permute-start | bytes 589832 | tf_op jit(solution)/shard_map/ppermute | solution.py:52
  74.0 11.2 %collective-permute-start.14 = (bf16[48,2048]{1,0:T(8,128)(2,1)S(1)}, bf16[48,2048]{1,0:T(8,128)(2,1)S(1)}, u32[]{:S(2)}, u32[]{:S(2)}) collective-permute-start(bf16[48,2048]{1,0:T(8,128)(2,1)S(1)} %collective-permute-done.7.refs_1_), channel_id=1, source_target_pairs={{0,1},{1,0},{16,17},{17,16},{2,3},{3,2},{18,19},{19,18},{4,5},{5,4... | collective-permute-start | bytes 589832 | tf_op jit(solution)/shard_map/ppermute | solution.py:52
  76.0 23.3 %collective-permute-start.6 = (bf16[48,2048]{1,0:T(8,128)(2,1)S(1)}, bf16[48,2048]{1,0:T(8,128)(2,1)S(1)}, u32[]{:S(2)}, u32[]{:S(2)}) collective-permute-start(bf16[48,2048]{1,0:T(8,128)(2,1)S(1)} %collective-permute-done.5.refs_0_), channel_id=1, source_target_pairs={{0,1},{1,0},{16,17},{17,16},{2,3},{3,2},{18,19},{19,18},{4,5},{5,4... | collective-permute-start | bytes 589832 | tf_op jit(solution)/shard_map/ppermute | solution.py:52
  78.7 20.6 %collective-permute-start.29 = (bf16[48,2048]{1,0:T(8,128)(2,1)S(1)}, bf16[48,2048]{1,0:T(8,128)(2,1)S(1)}, u32[]{:S(2)}, u32[]{:S(2)}) collective-permute-start(bf16[48,2048]{1,0:T(8,128)(2,1)S(1)} %collective-permute-done.28.refs_1_), channel_id=1, source_target_pairs={{0,1},{1,0},{16,17},{17,16},{2,3},{3,2},{18,19},{19,18},{4,5},{5,4... | collective-permute-start | bytes 589832 | tf_op jit(solution)/shard_map/ppermute | solution.py:52
  97.3 12.5 %collective-permute-start.21 = (bf16[48,2048]{1,0:T(8,128)(2,1)S(1)}, bf16[48,2048]{1,0:T(8,128)(2,1)S(1)}, u32[]{:S(2)}, u32[]{:S(2)}) collective-permute-start(bf16[48,2048]{1,0:T(8,128)(2,1)S(1)} %get-tuple-element.135), channel_id=1, source_target_pairs={{0,1},{1,0},{16,17},{17,16},{2,3},{3,2},{18,19},{19,18},{4,5},{5,4... | collective-permute-start | bytes 589832 | tf_op jit(solution)/shard_map/ppermute | solution.py:52
  98.8 14.0 %collective-permute-start.19 = (bf16[48,2048]{1,0:T(8,128)(2,1)S(1)}, bf16[48,2048]{1,0:T(8,128)(2,1)S(1)}, u32[]{:S(2)}, u32[]{:S(2)}) collective-permute-start(bf16[48,2048]{1,0:T(8,128)(2,1)S(1)} %get-tuple-element.131), channel_id=1, source_target_pairs={{0,1},{1,0},{16,17},{17,16},{2,3},{3,2},{18,19},{19,18},{4,5},{5,4... | collective-permute-start | bytes 589832 | tf_op jit(solution)/shard_map/ppermute | solution.py:52
  109.2 10.6 %collective-permute-start.30 = (bf16[48,2048]{1,0:T(8,128)(2,1)S(1)}, bf16[48,2048]{1,0:T(8,128)(2,1)S(1)}, u32[]{:S(2)}, u32[]{:S(2)}) collective-permute-start(bf16[48,2048]{1,0:T(8,128)(2,1)S(1)} %get-tuple-element.148), channel_id=1, source_target_pairs={{0,1},{1,0},{16,17},{17,16},{2,3},{3,2},{18,19},{19,18},{4,5},{5,4... | collective-permute-start | bytes 589832 | tf_op jit(solution)/shard_map/ppermute | solution.py:52
  109.8 18.0 %collective-permute-start.33 = (bf16[48,2048]{1,0:T(8,128)(2,1)S(1)}, bf16[48,2048]{1,0:T(8,128)(2,1)S(1)}, u32[]{:S(2)}, u32[]{:S(2)}) collective-permute-start(bf16[48,2048]{1,0:T(8,128)(2,1)S(1)} %add.105), channel_id=1, source_target_pairs={{0,10},{2,8},{4,14},{6,12},{8,2},{10,0},{12,6},{14,4},{16,26},{18,... | collective-permute-start | bytes 589832 | tf_op jit(solution)/shard_map/ppermute | solution.py:60
  112.8 17.2 %collective-permute-start.31 = (bf16[48,2048]{1,0:T(8,128)(2,1)S(1)}, bf16[48,2048]{1,0:T(8,128)(2,1)S(1)}, u32[]{:S(2)}, u32[]{:S(2)}) collective-permute-start(bf16[48,2048]{1,0:T(8,128)(2,1)S(1)} %add.103), channel_id=1, source_target_pairs={{0,8},{2,10},{4,12},{6,14},{8,0},{10,2},{12,4},{14,6},{16,24},{18,... | collective-permute-start | bytes 589832 | tf_op jit(solution)/shard_map/ppermute | solution.py:60
  114.1 26.7 %collective-permute-start.36 = (f32[128,128]{1,0:T(8,128)S(1)}, f32[128,128]{1,0:T(8,128)S(1)}, u32[]{:S(2)}, u32[]{:S(2)}) collective-permute-start(f32[128,128]{1,0:T(8,128)S(1)} %get-tuple-element.160.refs_9_), channel_id=1, source_target_pairs={{0,1},{1,0},{16,17},{17,16},{2,3},{3,2},{18,19},{19,18},{4,5},{5,4... | collective-permute-start | bytes 196616 | tf_op jit(solution)/shard_map/ppermute | solution.py:52
  115.6 17.4 %collective-permute-start.26 = (bf16[48,2048]{1,0:T(8,128)(2,1)S(1)}, bf16[48,2048]{1,0:T(8,128)(2,1)S(1)}, u32[]{:S(2)}, u32[]{:S(2)}) collective-permute-start(bf16[48,2048]{1,0:T(8,128)(2,1)S(1)} %get-tuple-element.144), channel_id=1, source_target_pairs={{0,1},{1,0},{16,17},{17,16},{2,3},{3,2},{18,19},{19,18},{4,5},{5,4... | collective-permute-start | bytes 589832 | tf_op jit(solution)/shard_map/ppermute | solution.py:52
  119.8 16.3 %collective-permute-start.24 = (bf16[48,2048]{1,0:T(8,128)(2,1)S(1)}, bf16[48,2048]{1,0:T(8,128)(2,1)S(1)}, u32[]{:S(2)}, u32[]{:S(2)}) collective-permute-start(bf16[48,2048]{1,0:T(8,128)(2,1)S(1)} %get-tuple-element.140), channel_id=1, source_target_pairs={{0,1},{1,0},{16,17},{17,16},{2,3},{3,2},{18,19},{19,18},{4,5},{5,4... | collective-permute-start | bytes 589832 | tf_op jit(solution)/shard_map/ppermute | solution.py:52
  127.8 12.3 %collective-permute-start.22 = (bf16[48,2048]{1,0:T(8,128)(2,1)S(1)}, bf16[48,2048]{1,0:T(8,128)(2,1)S(1)}, u32[]{:S(2)}, u32[]{:S(2)}) collective-permute-start(bf16[48,2048]{1,0:T(8,128)(2,1)S(1)} %get-tuple-element.136), channel_id=1, source_target_pairs={{0,1},{1,0},{16,17},{17,16},{2,3},{3,2},{18,19},{19,18},{4,5},{5,4... | collective-permute-start | bytes 589832 | tf_op jit(solution)/shard_map/ppermute | solution.py:52
  130.0 12.0 %collective-permute-start.20 = (bf16[48,2048]{1,0:T(8,128)(2,1)S(1)}, bf16[48,2048]{1,0:T(8,128)(2,1)S(1)}, u32[]{:S(2)}, u32[]{:S(2)}) collective-permute-start(bf16[48,2048]{1,0:T(8,128)(2,1)S(1)} %get-tuple-element.132), channel_id=1, source_target_pairs={{0,1},{1,0},{16,17},{17,16},{2,3},{3,2},{18,19},{19,18},{4,5},{5,4... | collective-permute-start | bytes 589832 | tf_op jit(solution)/shard_map/ppermute | solution.py:52
  132.9 14.2 %collective-permute-start.35 = (bf16[48,2048]{1,0:T(8,128)(2,1)}, bf16[48,2048]{1,0:T(8,128)(2,1)S(1)}, u32[]{:S(2)}, u32[]{:S(2)}) collective-permute-start(bf16[48,2048]{1,0:T(8,128)(2,1)} %add.104), channel_id=1, source_target_pairs={{0,14},{2,12},{4,10},{6,8},{8,6},{10,4},{12,2},{14,0},{16,30},{18,... | collective-permute-start | bytes 589832 | tf_op jit(solution)/shard_map/ppermute | solution.py:60
  136.0 11.1 %collective-permute-start.34 = (bf16[48,2048]{1,0:T(8,128)(2,1)}, bf16[48,2048]{1,0:T(8,128)(2,1)}, u32[]{:S(2)}, u32[]{:S(2)}) collective-permute-start(bf16[48,2048]{1,0:T(8,128)(2,1)} %add.102), channel_id=1, source_target_pairs={{0,12},{2,14},{4,8},{6,10},{8,4},{10,6},{12,0},{14,2},{16,28},{18,... | collective-permute-start | bytes 589832 | tf_op jit(solution)/shard_map/ppermute | solution.py:60
  155.0 10.8 %collective-permute-start.39 = (bf16[128,2048]{1,0:T(8,128)(2,1)S(1)}, bf16[128,2048]{1,0:T(8,128)(2,1)S(1)}, u32[]{:S(2)}, u32[]{:S(2)}) collective-permute-start(bf16[128,2048]{1,0:T(8,128)(2,1)S(1)} %get-tuple-element.161), channel_id=1, source_target_pairs={{0,18},{1,19},{2,20},{3,21},{4,22},{5,23},{6,24},{7,25},{8,26},{9,... | collective-permute-start | bytes 1572872 | tf_op jit(solution)/shard_map/ppermute | solution.py:47
  172.0 17.8 %collective-permute-start.50 = (bf16[48,2048]{1,0:T(8,128)(2,1)S(1)}, bf16[48,2048]{1,0:T(8,128)(2,1)S(1)}, u32[]{:S(2)}, u32[]{:S(2)}) collective-permute-start(bf16[48,2048]{1,0:T(8,128)(2,1)S(1)} %get-tuple-element.178), channel_id=1, source_target_pairs={{0,10},{2,8},{4,14},{6,12},{8,2},{10,0},{12,6},{14,4},{16,26},{18,... | collective-permute-start | bytes 589832 | tf_op jit(solution)/shard_map/ppermute | solution.py:60
  173.1 20.7 %collective-permute-start.44 = (bf16[48,2048]{1,0:T(8,128)(2,1)S(1)}, bf16[48,2048]{1,0:T(8,128)(2,1)S(1)}, u32[]{:S(2)}, u32[]{:S(2)}) collective-permute-start(bf16[48,2048]{1,0:T(8,128)(2,1)S(1)} %get-tuple-element.170), channel_id=1, source_target_pairs={{0,8},{2,10},{4,12},{6,14},{8,0},{10,2},{12,4},{14,6},{16,24},{18,... | collective-permute-start | bytes 589832 | tf_op jit(solution)/shard_map/ppermute | solution.py:60
  175.5 20.3 %collective-permute-start.51 = (bf16[48,2048]{1,0:T(8,128)(2,1)S(1)}, bf16[48,2048]{1,0:T(8,128)(2,1)S(1)}, u32[]{:S(2)}, u32[]{:S(2)}) collective-permute-start(bf16[48,2048]{1,0:T(8,128)(2,1)S(1)} %get-tuple-element.172.refs_0_), channel_id=1, source_target_pairs={{0,1},{1,0},{16,17},{17,16},{2,3},{3,2},{18,19},{19,18},{4,5},{5,4... | collective-permute-start | bytes 589832 | tf_op jit(solution)/shard_map/ppermute | solution.py:52
  176.3 19.8 %collective-permute-start.47 = (bf16[48,2048]{1,0:T(8,128)(2,1)S(1)}, bf16[48,2048]{1,0:T(8,128)(2,1)S(1)}, u32[]{:S(2)}, u32[]{:S(2)}) collective-permute-start(bf16[48,2048]{1,0:T(8,128)(2,1)S(1)} %get-tuple-element.173), channel_id=1, source_target_pairs={{0,2},{2,0},{4,6},{6,4},{8,10},{10,8},{12,14},{14,12},{16,18},{18,... | collective-permute-start | bytes 589832 | tf_op jit(solution)/shard_map/ppermute | solution.py:60
  177.4 19.8 %collective-permute-start.48 = (bf16[48,2048]{1,0:T(8,128)(2,1)S(1)}, bf16[48,2048]{1,0:T(8,128)(2,1)S(1)}, u32[]{:S(2)}, u32[]{:S(2)}) collective-permute-start(bf16[48,2048]{1,0:T(8,128)(2,1)S(1)} %get-tuple-element.174), channel_id=1, source_target_pairs={{0,4},{2,6},{4,0},{6,2},{8,12},{10,14},{12,8},{14,10},{16,20},{18,... | collective-permute-start | bytes 589832 | tf_op jit(solution)/shard_map/ppermute | solution.py:60
  193.8 10.6 %collective-permute-start.52 = (bf16[48,2048]{1,0:T(8,128)(2,1)S(1)}, bf16[48,2048]{1,0:T(8,128)(2,1)S(1)}, u32[]{:S(2)}, u32[]{:S(2)}) collective-permute-start(bf16[48,2048]{1,0:T(8,128)(2,1)S(1)} %get-tuple-element.180), channel_id=1, source_target_pairs={{0,14},{2,12},{4,10},{6,8},{8,6},{10,4},{12,2},{14,0},{16,30},{18,... | collective-permute-start | bytes 589832 | tf_op jit(solution)/shard_map/ppermute | solution.py:60
  197.2 11.0 %collective-permute-start.56 = (bf16[48,2048]{1,0:T(8,128)(2,1)S(1)}, bf16[48,2048]{1,0:T(8,128)(2,1)S(1)}, u32[]{:S(2)}, u32[]{:S(2)}) collective-permute-start(bf16[48,2048]{1,0:T(8,128)(2,1)S(1)} %collective-permute-done.44.refs_4_), channel_id=1, source_target_pairs={{0,1},{1,0},{16,17},{17,16},{2,3},{3,2},{18,19},{19,18},{4,5},{5,4... | collective-permute-start | bytes 589832 | tf_op jit(solution)/shard_map/ppermute | solution.py:52
  198.1 14.2 %collective-permute-start.53 = (bf16[48,2048]{1,0:T(8,128)(2,1)S(1)}, bf16[48,2048]{1,0:T(8,128)(2,1)S(1)}, u32[]{:S(2)}, u32[]{:S(2)}) collective-permute-start(bf16[48,2048]{1,0:T(8,128)(2,1)S(1)} %collective-permute-done.47.refs_1_), channel_id=1, source_target_pairs={{0,1},{1,0},{16,17},{17,16},{2,3},{3,2},{18,19},{19,18},{4,5},{5,4... | collective-permute-start | bytes 589832 | tf_op jit(solution)/shard_map/ppermute | solution.py:52
  204.3 12.2 %collective-permute-start.54 = (bf16[48,2048]{1,0:T(8,128)(2,1)S(1)}, bf16[48,2048]{1,0:T(8,128)(2,1)S(1)}, u32[]{:S(2)}, u32[]{:S(2)}) collective-permute-start(bf16[48,2048]{1,0:T(8,128)(2,1)S(1)} %collective-permute-done.48.refs_2_), channel_id=1, source_target_pairs={{0,1},{1,0},{16,17},{17,16},{2,3},{3,2},{18,19},{19,18},{4,5},{5,4... | collective-permute-start | bytes 589832 | tf_op jit(solution)/shard_map/ppermute | solution.py:52
  205.4 13.8 %collective-permute-start.55 = (bf16[48,2048]{1,0:T(8,128)(2,1)S(1)}, bf16[48,2048]{1,0:T(8,128)(2,1)S(1)}, u32[]{:S(2)}, u32[]{:S(2)}) collective-permute-start(bf16[48,2048]{1,0:T(8,128)(2,1)S(1)} %collective-permute-done.49.refs_3_), channel_id=1, source_target_pairs={{0,1},{1,0},{16,17},{17,16},{2,3},{3,2},{18,19},{19,18},{4,5},{5,4... | collective-permute-start | bytes 589832 | tf_op jit(solution)/shard_map/ppermute | solution.py:52
  234.8 11.1 %collective-permute-start.46 = (bf16[48,2048]{1,0:T(8,128)(2,1)S(1)}, bf16[48,2048]{1,0:T(8,128)(2,1)S(1)}, u32[]{:S(2)}, u32[]{:S(2)}) collective-permute-start(bf16[48,2048]{1,0:T(8,128)(2,1)S(1)} %collective-permute-done.45.refs_0_), channel_id=1, source_target_pairs={{0,1},{1,0},{16,17},{17,16},{2,3},{3,2},{18,19},{19,18},{4,5},{5,4... | collective-permute-start | bytes 589832 | tf_op jit(solution)/shard_map/ppermute | solution.py:52
  235.8 13.9 %collective-permute-start.67 = (bf16[48,2048]{1,0:T(8,128)(2,1)S(1)}, bf16[48,2048]{1,0:T(8,128)(2,1)S(1)}, u32[]{:S(2)}, u32[]{:S(2)}) collective-permute-start(bf16[48,2048]{1,0:T(8,128)(2,1)S(1)} %collective-permute-done.52.refs_1_), channel_id=1, source_target_pairs={{0,1},{1,0},{16,17},{17,16},{2,3},{3,2},{18,19},{19,18},{4,5},{5,4... | collective-permute-start | bytes 589832 | tf_op jit(solution)/shard_map/ppermute | solution.py:52
  236.8 22.1 %collective-permute-start.58 = (bf16[48,2048]{1,0:T(8,128)(2,1)S(1)}, bf16[48,2048]{1,0:T(8,128)(2,1)S(1)}, u32[]{:S(2)}, u32[]{:S(2)}) collective-permute-start(bf16[48,2048]{1,0:T(8,128)(2,1)S(1)} %get-tuple-element.185), channel_id=1, source_target_pairs={{0,1},{1,0},{16,17},{17,16},{2,3},{3,2},{18,19},{19,18},{4,5},{5,4... | collective-permute-start | bytes 589832 | tf_op jit(solution)/shard_map/ppermute | solution.py:52
  241.7 21.2 %collective-permute-start.71 = (bf16[48,2048]{1,0:T(8,128)(2,1)S(1)}, bf16[48,2048]{1,0:T(8,128)(2,1)S(1)}, u32[]{:S(2)}, u32[]{:S(2)}) collective-permute-start(bf16[48,2048]{1,0:T(8,128)(2,1)S(1)} %add.113), channel_id=1, source_target_pairs={{0,10},{2,8},{4,14},{6,12},{8,2},{10,0},{12,6},{14,4},{16,26},{18,... | collective-permute-start | bytes 589832 | tf_op jit(solution)/shard_map/ppermute | solution.py:60
  261.9 12.4 %collective-permute-start.65 = (bf16[48,2048]{1,0:T(8,128)(2,1)S(1)}, bf16[48,2048]{1,0:T(8,128)(2,1)S(1)}, u32[]{:S(2)}, u32[]{:S(2)}) collective-permute-start(bf16[48,2048]{1,0:T(8,128)(2,1)S(1)} %get-tuple-element.198), channel_id=1, source_target_pairs={{0,1},{1,0},{16,17},{17,16},{2,3},{3,2},{18,19},{19,18},{4,5},{5,4... | collective-permute-start | bytes 589832 | tf_op jit(solution)/shard_map/ppermute | solution.py:52
  262.9 15.7 %collective-permute-start.63 = (bf16[48,2048]{1,0:T(8,128)(2,1)S(1)}, bf16[48,2048]{1,0:T(8,128)(2,1)S(1)}, u32[]{:S(2)}, u32[]{:S(2)}) collective-permute-start(bf16[48,2048]{1,0:T(8,128)(2,1)S(1)} %get-tuple-element.194), channel_id=1, source_target_pairs={{0,1},{1,0},{16,17},{17,16},{2,3},{3,2},{18,19},{19,18},{4,5},{5,4... | collective-permute-start | bytes 589832 | tf_op jit(solution)/shard_map/ppermute | solution.py:52
  265.9 17.3 %collective-permute-start.61 = (bf16[48,2048]{1,0:T(8,128)(2,1)S(1)}, bf16[48,2048]{1,0:T(8,128)(2,1)S(1)}, u32[]{:S(2)}, u32[]{:S(2)}) collective-permute-start(bf16[48,2048]{1,0:T(8,128)(2,1)S(1)} %get-tuple-element.190), channel_id=1, source_target_pairs={{0,1},{1,0},{16,17},{17,16},{2,3},{3,2},{18,19},{19,18},{4,5},{5,4... | collective-permute-start | bytes 589832 | tf_op jit(solution)/shard_map/ppermute | solution.py:52
  267.7 19.3 %collective-permute-start.59 = (bf16[48,2048]{1,0:T(8,128)(2,1)S(1)}, bf16[48,2048]{1,0:T(8,128)(2,1)S(1)}, u32[]{:S(2)}, u32[]{:S(2)}) collective-permute-start(bf16[48,2048]{1,0:T(8,128)(2,1)S(1)} %get-tuple-element.186), channel_id=1, source_target_pairs={{0,1},{1,0},{16,17},{17,16},{2,3},{3,2},{18,19},{19,18},{4,5},{5,4... | collective-permute-start | bytes 589832 | tf_op jit(solution)/shard_map/ppermute | solution.py:52
  270.1 14.0 %collective-permute-start.74 = (f32[128,128]{1,0:T(8,128)S(1)}, f32[128,128]{1,0:T(8,128)S(1)}, u32[]{:S(2)}, u32[]{:S(2)}) collective-permute-start(f32[128,128]{1,0:T(8,128)S(1)} %get-tuple-element.215.refs_9_), channel_id=1, source_target_pairs={{0,1},{1,0},{16,17},{17,16},{2,3},{3,2},{18,19},{19,18},{4,5},{5,4... | collective-permute-start | bytes 196616 | tf_op jit(solution)/shard_map/ppermute | solution.py:52
  274.3 15.2 %collective-permute-start.73 = (bf16[48,2048]{1,0:T(8,128)(2,1)}, bf16[48,2048]{1,0:T(8,128)(2,1)S(1)}, u32[]{:S(2)}, u32[]{:S(2)}) collective-permute-start(bf16[48,2048]{1,0:T(8,128)(2,1)} %add.112), channel_id=1, source_target_pairs={{0,14},{2,12},{4,10},{6,8},{8,6},{10,4},{12,2},{14,0},{16,30},{18,... | collective-permute-start | bytes 589832 | tf_op jit(solution)/shard_map/ppermute | solution.py:60
  278.6 12.2 %collective-permute-start.72 = (bf16[48,2048]{1,0:T(8,128)(2,1)}, bf16[48,2048]{1,0:T(8,128)(2,1)S(1)}, u32[]{:S(2)}, u32[]{:S(2)}) collective-permute-start(bf16[48,2048]{1,0:T(8,128)(2,1)} %add.110), channel_id=1, source_target_pairs={{0,12},{2,14},{4,8},{6,10},{8,4},{10,6},{12,0},{14,2},{16,28},{18,... | collective-permute-start | bytes 589832 | tf_op jit(solution)/shard_map/ppermute | solution.py:60
  (72 other events, 1100.4 us)
